TPU v7x, 32 devices: a whole 2x2x4 slice. The times are simulated.
32 devices in a mesh: dp: 8 (over z, y), seq: 4 (over x, core).
Axes of the slice: x: 2, y: 2, z: 4, core: 2. Of those that a mesh axis runs over, the one named last changes fastest.
Arguments:
- tokens: bfloat16 [8, 64, 64, 320], P('dp', 'seq'), may hold values from -6 to 6
- buckets: int32 [8], P('dp'), may hold values from 0 to 1, as said below
- cotangent: bfloat16 [8, 4, 8, 128, 320], P(None, 'seq', 'dp'), may hold values from -8 to 8
- query_weight: float32 [320, 320], P('dp', 'seq'), may hold values from -0.3125 to 0.3125
- reduce_weight: float32 [1280, 320], P('dp', 'seq'), may hold values from -0.15625 to 0.15625
- memory_weight: float32 [320, 640], P('dp', 'seq'), may hold values from -0.3125 to 0.3125
- output_weight: float32 [320, 320], P('dp', 'seq'), may hold values from -2.5 to 2.5
- expand_weight: float32 [320, 1280], P('dp', 'seq'), may hold values from -0.3125 to 0.3125
- contract_weight: float32 [1280, 320], P('dp', 'seq'), may hold values from -0.15625 to 0.15625
- norm_gains: float32 [3, 320], P(None, 'dp'), may hold values from 0.3 to 2.7
- biases: float32 [8, 320], P(None, 'dp'), may hold values from -1 to 1
- hidden_params: float32 [11, 1280], P(None, 'dp'), may hold values from -1.6 to 1.6
- moment_query: float32 [320, 320], P('dp', 'seq'), may hold values from -0.00048828125 to 0.00048828125
- moment_reduce: float32 [1280, 320], P('dp', 'seq'), may hold values from -0.00048828125 to 0.00048828125
- moment_memory: float32 [320, 640], P('dp', 'seq'), may hold values from -0.00048828125 to 0.00048828125
- moment_output: float32 [320, 320], P('dp', 'seq'), may hold values from -0.00048828125 to 0.00048828125
- moment_expand: float32 [320, 1280], P('dp', 'seq'), may hold values from -0.00048828125 to 0.00048828125
- moment_contract: float32 [1280, 320], P('dp', 'seq'), may hold values from -0.00048828125 to 0.00048828125
- moment_gains: float32 [3, 320], P(None, 'dp'), may hold values from -0.00048828125 to 0.00048828125
- moment_biases: float32 [8, 320], P(None, 'dp'), may hold values from -0.0029296875 to 0.0029296875
- moment_hidden: float32 [11, 1280], P(None, 'dp'), may hold values from -0.00048828125 to 0.00048828125
- square_query: float32 [320, 320], P('dp', 'seq'), may hold values from 3.1763285e-08 to 1.268116e-07
- square_reduce: float32 [1280, 320], P('dp', 'seq'), may hold values from 3.1763285e-08 to 1.268116e-07
- square_memory: float32 [320, 640], P('dp', 'seq'), may hold values from 3.1763285e-08 to 1.268116e-07
- square_output: float32 [320, 320], P('dp', 'seq'), may hold values from 3.1763285e-08 to 1.268116e-07
- square_expand: float32 [320, 1280], P('dp', 'seq'), may hold values from 3.1763285e-08 to 1.268116e-07
- square_contract: float32 [1280, 320], P('dp', 'seq'), may hold values from 3.1763285e-08 to 1.268116e-07
- square_gains: float32 [3, 320], P(None, 'dp'), may hold values from 3.1763285e-08 to 1.268116e-07
- square_biases: float32 [8, 320], P(None, 'dp'), may hold values from 9.661836e-07 to 3.804348e-06
- square_hidden: float32 [11, 1280], P(None, 'dp'), may hold values from 3.1763285e-08 to 1.268116e-07
Outputs:
- block_output: bfloat16 [8, 4, 8, 128, 320], P(None, 'seq', 'dp')
- token_grad: bfloat16 [8, 64, 64, 320], P('dp', 'seq')
- global_norm: float32 [], replicated
- updated_query: float32 [320, 320], P('dp', 'seq')
- updated_reduce: float32 [1280, 320], P('dp', 'seq')
- updated_memory: float32 [320, 640], P('dp', 'seq')
- updated_output: float32 [320, 320], P('dp', 'seq')
- updated_expand: float32 [320, 1280], P('dp', 'seq')
- updated_contract: float32 [1280, 320], P('dp', 'seq')
- updated_gains: float32 [3, 320], P(None, 'dp')
- updated_biases: float32 [8, 320], P(None, 'dp')
- updated_hidden: float32 [11, 1280], P(None, 'dp')
- momentum_query: float32 [320, 320], P('dp', 'seq')
- momentum_reduce: float32 [1280, 320], P('dp', 'seq')
- momentum_memory: float32 [320, 640], P('dp', 'seq')
- momentum_output: float32 [320, 320], P('dp', 'seq')
- momentum_expand: float32 [320, 1280], P('dp', 'seq')
- momentum_contract: float32 [1280, 320], P('dp', 'seq')
- momentum_gains: float32 [3, 320], P(None, 'dp')
- momentum_biases: float32 [8, 320], P(None, 'dp')
- momentum_hidden: float32 [11, 1280], P(None, 'dp')
- squares_query: float32 [320, 320], P('dp', 'seq')
- squares_reduce: float32 [1280, 320], P('dp', 'seq')
- squares_memory: float32 [320, 640], P('dp', 'seq')
- squares_output: float32 [320, 320], P('dp', 'seq')
- squares_expand: float32 [320, 1280], P('dp', 'seq')
- squares_contract: float32 [1280, 320], P('dp', 'seq')
- squares_gains: float32 [3, 320], P(None, 'dp')
- squares_biases: float32 [8, 320], P(None, 'dp')
- squares_hidden: float32 [11, 1280], P(None, 'dp')
Inputs may be any that keep to these rules, and one draw needn't show every extreme that they name: `buckets`: 0 marks a canvas holding one scene of 64 x 64 tokens, 1 a canvas holding four scenes, one in each quadrant; both values occur in every draw.
All inputs are finite; a program needn't handle non-finite values.
Results may differ from a plain program's by a relative error of at most 0.023.
Values may be sent and summed in bfloat16 or wider, within the bound.
A program may use at most 128 MiB of HBM per device.

v0:
```python
import jax
import jax.numpy as jnp
from jax import lax
from jax.sharding import PartitionSpec as P

D = 320
HEADS = 5
HEAD = 64
FF = 1280
STEP = 10
OUT_FAN = 5


NORM_EPS = 1e-06
MAX_NORM = 1.0
BETA_ONE = 0.9
BETA_TWO = 0.95
ADAM_EPS = 1e-08
DECAY_RATE = 0.01
VECTOR_RATE = 0.3
GAIN_RATE = 0.8
MASKED = -1e30


def extended(cells, sides, width):
    for axis, dim in sides:
        count = lax.axis_size(axis)
        ends = count - 1
        head = lax.slice_in_dim(cells, 0, width, axis=dim)
        tail = lax.slice_in_dim(cells, cells.shape[dim] - width, cells.shape[dim], axis=dim)
        cells = jnp.concatenate(
            [
                lax.ppermute(tail, axis, [(i, (i + 1) % count) for i in range(ends)]),
                cells,
                lax.ppermute(head, axis, [((i + 1) % count, i) for i in range(ends)]),
            ],
            axis=dim,
        )
    return cells


def layer_norm(values, scale_row, offset_row):
    average = jnp.mean(values, axis=-1, keepdims=True)
    centered = values - average
    spread = jnp.mean(centered * centered, axis=-1, keepdims=True)
    return centered * lax.rsqrt(spread + NORM_EPS) * scale_row + offset_row


def gelu_exact(values):
    return jax.nn.gelu(values, approximate=False)


def scene_ids(bucket_id, row_ids, col_ids, side):
    half = side // 2
    quarter = (row_ids >= half).astype(jnp.int32) * 2 + (col_ids >= half).astype(jnp.int32)
    return quarter * bucket_id


def padded_ids(bucket_id, first_row, band_rows, side):
    row_ids = first_row + jnp.arange(band_rows + 2, dtype=jnp.int32) - 1
    col_ids = jnp.arange(side + 2, dtype=jnp.int32) - 1
    inside = (
        (row_ids[:, None] >= 0)
        & (row_ids[:, None] < side)
        & (col_ids[None, :] >= 0)
        & (col_ids[None, :] < side)
    )
    return jnp.where(inside, scene_ids(bucket_id, row_ids[:, None], col_ids[None, :], side), -1)


def neighbor_masks(ids_pad, band_rows, side):
    center = ids_pad[1 : 1 + band_rows, 1 : 1 + side]
    masks = []
    for row_step in range(3):
        for col_step in range(3):
            masks.append(
                (
                    ids_pad[row_step : row_step + band_rows, col_step : col_step + side] == center
                ).astype(jnp.float32)
            )
    return masks


def head_scores(query_head, key_head, same_scene, scale):
    raw = jnp.einsum("qe,ke->qk", query_head, key_head, preferred_element_type=jnp.float32) * scale
    return jnp.where(same_scene, raw, MASKED)


def expand_hidden(mid_low, expand_matrix, hidden_rows, masks, band_rows, side):
    hidden_low = (
        jnp.dot(mid_low, expand_matrix, preferred_element_type=jnp.float32) + hidden_rows[9]
    ).astype(jnp.bfloat16)
    hidden_low = hidden_low.reshape(band_rows, side, hidden_low.shape[1])
    with_rim = extended(hidden_low, (("seq", 0),), 1)
    padded = jnp.pad(with_rim, ((0, 0), (1, 1), (0, 0)))
    total = jnp.zeros(hidden_low.shape, jnp.float32) + hidden_rows[10]
    for tap_index in range(9):
        row_step = tap_index // 3
        col_step = tap_index % 3
        total = (
            total
            + hidden_rows[tap_index]
            * padded[row_step : row_step + band_rows, col_step : col_step + side]
            * masks[tap_index][:, :, None]
        )
    return (padded, total)


def vector_total(gain_grad, shift_grad, hidden_grad):
    return (
        lax.psum(gain_grad.astype(jnp.bfloat16), "seq").astype(jnp.float32),
        lax.psum(shift_grad.astype(jnp.bfloat16), "seq").astype(jnp.float32),
        lax.psum(hidden_grad.astype(jnp.bfloat16), "seq").astype(jnp.float32),
    )


def adam_step(weight_now, first_now, second_now, clipped, step_rate, decay_rate):
    first_new = BETA_ONE * first_now + (1.0 - BETA_ONE) * clipped
    second_new = BETA_TWO * second_now + (1.0 - BETA_TWO) * clipped * clipped
    direction = (
        first_new
        / (1.0 - BETA_ONE**STEP)
        / (jnp.sqrt(second_new / (1.0 - BETA_TWO**STEP)) + ADAM_EPS)
    )
    return (weight_now - step_rate * (direction + decay_rate * weight_now), first_new, second_new)


def on_device(
    tokens,
    buckets,
    cotangent,
    query_weight,
    reduce_weight,
    memory_weight,
    output_weight,
    expand_weight,
    contract_weight,
    norm_gains,
    biases,
    hidden_params,
    moment_query,
    moment_reduce,
    moment_memory,
    moment_output,
    moment_expand,
    moment_contract,
    moment_gains,
    moment_biases,
    moment_hidden,
    square_query,
    square_reduce,
    square_memory,
    square_output,
    square_expand,
    square_contract,
    square_gains,
    square_biases,
    square_hidden,
):
    band_rows = tokens.shape[1]
    side = tokens.shape[2]
    width = tokens.shape[3]
    band_tokens = band_rows * side
    local_keys = band_tokens // 4
    band_index = lax.axis_index("seq")
    bucket_id = buckets[0]
    column_parts = (
        lax.all_gather(query_weight.astype(jnp.bfloat16), "seq", axis=1, tiled=True),
        lax.all_gather(reduce_weight.astype(jnp.bfloat16), "seq", axis=1, tiled=True),
        lax.all_gather(memory_weight.astype(jnp.bfloat16), "seq", axis=1, tiled=True),
        lax.all_gather(output_weight.astype(jnp.bfloat16), "seq", axis=1, tiled=True),
        lax.all_gather(expand_weight.astype(jnp.bfloat16), "seq", axis=1, tiled=True),
        lax.all_gather(contract_weight.astype(jnp.bfloat16), "seq", axis=1, tiled=True),
    )
    gathered = (
        lax.all_gather(column_parts[0], "dp", axis=0, tiled=True),
        lax.all_gather(column_parts[1], "dp", axis=0, tiled=True),
        lax.all_gather(column_parts[2], "dp", axis=0, tiled=True),
        lax.all_gather(column_parts[3], "dp", axis=0, tiled=True),
        lax.all_gather(column_parts[4], "dp", axis=0, tiled=True),
        lax.all_gather(column_parts[5], "dp", axis=0, tiled=True),
        lax.all_gather(norm_gains.astype(jnp.bfloat16), "dp", axis=1, tiled=True),
        lax.all_gather(biases.astype(jnp.bfloat16), "dp", axis=1, tiled=True),
        lax.all_gather(hidden_params.astype(jnp.bfloat16), "dp", axis=1, tiled=True),
    )
    query_matrix, reduce_matrix, memory_matrix, output_matrix, expand_matrix, contract_matrix = (
        gathered[0],
        gathered[1],
        gathered[2],
        gathered[3],
        gathered[4],
        gathered[5],
    )
    gain_rows = gathered[6].astype(jnp.float32)
    shift_rows = gathered[7].astype(jnp.float32)
    hidden_rows = gathered[8].astype(jnp.float32)
    inputs = tokens[0].astype(jnp.float32).reshape(band_tokens, width)
    normed_in, first_norm_back = jax.vjp(layer_norm, inputs, gain_rows[0], shift_rows[0])
    normed_low = normed_in.astype(jnp.bfloat16)
    query_low = (
        jnp.dot(normed_low, query_matrix, preferred_element_type=jnp.float32) + shift_rows[1]
    ).astype(jnp.bfloat16)
    patches = (
        normed_low.reshape(band_rows // 2, 2, side // 2, 2, width)
        .transpose(0, 2, 1, 3, 4)
        .reshape(local_keys, 4 * width)
    )
    reduced = jnp.dot(patches, reduce_matrix, preferred_element_type=jnp.float32) + shift_rows[2]
    memory_in, memory_norm_back = jax.vjp(layer_norm, reduced, gain_rows[1], shift_rows[3])
    memory_low = memory_in.astype(jnp.bfloat16)
    value_shift = jnp.concatenate([jnp.zeros((width,), jnp.float32), shift_rows[4]])
    memory_out = (
        jnp.dot(memory_low, memory_matrix, preferred_element_type=jnp.float32) + value_shift
    ).astype(jnp.bfloat16)
    canvas_memory = lax.all_gather(memory_out, "seq", axis=0, tiled=True)
    places = band_index * band_rows + jnp.arange(band_rows, dtype=jnp.int32)
    columns = jnp.arange(side, dtype=jnp.int32)
    query_ids = scene_ids(bucket_id, places[:, None], columns[None, :], side).reshape(-1)
    key_cells = jnp.arange(side // 2, dtype=jnp.int32)
    key_ids = scene_ids(bucket_id, key_cells[:, None], key_cells[None, :], side // 2).reshape(-1)
    same_scene = query_ids[:, None] == key_ids[None, :]
    scale = HEAD ** (-0.5)
    attended_parts = []
    log_totals = []
    for head_index in range(HEADS):
        start_col = head_index * HEAD
        query_head = query_low[:, start_col : start_col + HEAD]
        key_head = canvas_memory[:, start_col : start_col + HEAD]
        value_head = canvas_memory[:, width + start_col : width + start_col + HEAD]
        scores = head_scores(query_head, key_head, same_scene, scale)
        largest = jnp.max(scores, axis=1, keepdims=True)
        powers = jnp.exp(scores - largest)
        totals = jnp.sum(powers, axis=1, keepdims=True)
        probs_low = (powers / totals).astype(jnp.bfloat16)
        attended_parts.append(jnp.dot(probs_low, value_head, preferred_element_type=jnp.float32))
        log_totals.append(largest + jnp.log(totals))
    attended_low = jnp.concatenate(attended_parts, axis=1).astype(jnp.bfloat16)
    middle = (
        inputs
        + jnp.dot(attended_low, output_matrix, preferred_element_type=jnp.float32)
        + shift_rows[5]
    )
    normed_mid, second_norm_back = jax.vjp(layer_norm, middle, gain_rows[2], shift_rows[6])
    mid_low = normed_mid.astype(jnp.bfloat16)
    masks = neighbor_masks(
        padded_ids(bucket_id, band_index * band_rows, band_rows, side), band_rows, side
    )
    padded, pre_act = expand_hidden(mid_low, expand_matrix, hidden_rows, masks, band_rows, side)
    activated, gelu_back = jax.vjp(gelu_exact, pre_act)
    act_low = activated.astype(jnp.bfloat16).reshape(band_tokens, FF)
    outputs = (
        middle
        + jnp.dot(act_low, contract_matrix, preferred_element_type=jnp.float32)
        + shift_rows[7]
    )
    dp_count = lax.axis_size("dp")
    piece = band_tokens // dp_count
    block_output = lax.all_to_all(
        outputs.astype(jnp.bfloat16).reshape(1, 1, dp_count, piece, width),
        "dp",
        split_axis=2,
        concat_axis=0,
        tiled=True,
    )
    slope_low = lax.all_to_all(cotangent, "dp", split_axis=0, concat_axis=2, tiled=True).reshape(
        band_tokens, width
    )
    slope = slope_low.astype(jnp.float32)
    grad_contract = jnp.einsum("qf,qd->fd", act_low, slope_low, preferred_element_type=jnp.float32)
    grad_shift_out = jnp.sum(slope, axis=0)
    act_slope = jnp.einsum(
        "qd,fd->qf", slope_low, contract_matrix, preferred_element_type=jnp.float32
    )
    padded, pre_act = expand_hidden(mid_low, expand_matrix, hidden_rows, masks, band_rows, side)
    activated, gelu_back = jax.vjp(gelu_exact, pre_act)
    pre_slope = gelu_back(act_slope.reshape(band_rows, side, FF))[0].astype(jnp.bfloat16)
    slope_rim = extended(pre_slope, (("seq", 0),), 1)
    slope_pad = jnp.pad(slope_rim, ((0, 0), (1, 1), (0, 0)))
    pre_float = pre_slope.astype(jnp.float32)
    hidden_slope = jnp.zeros(pre_slope.shape, jnp.float32)
    tap_grads = []
    for tap_index in range(9):
        row_step = tap_index // 3
        col_step = tap_index % 3
        back_rows = 2 - row_step
        back_cols = 2 - col_step
        hidden_slope = (
            hidden_slope
            + hidden_rows[tap_index]
            * slope_pad[back_rows : back_rows + band_rows, back_cols : back_cols + side]
            * masks[8 - tap_index][:, :, None]
        )
        tap_grads.append(
            jnp.sum(
                pre_float
                * padded[row_step : row_step + band_rows, col_step : col_step + side]
                * masks[tap_index][:, :, None],
                axis=(0, 1),
            )
        )
    hidden_slope_low = hidden_slope.astype(jnp.bfloat16).reshape(band_tokens, FF)
    grad_expand = jnp.einsum(
        "qd,qf->df", mid_low, hidden_slope_low, preferred_element_type=jnp.float32
    )
    grad_expand_shift = jnp.sum(hidden_slope_low.astype(jnp.float32), axis=0)
    grad_depth_shift = jnp.sum(pre_float, axis=(0, 1))
    mid_norm_slope = jnp.einsum(
        "qf,df->qd", hidden_slope_low, expand_matrix, preferred_element_type=jnp.float32
    )
    back_mid, grad_gain_two, grad_shift_two = second_norm_back(mid_norm_slope)
    middle_slope = slope + back_mid
    branch_low = middle_slope.astype(jnp.bfloat16)
    grad_output = jnp.einsum(
        "qe,qd->ed", attended_low, branch_low, preferred_element_type=jnp.float32
    )
    grad_shift_branch = jnp.sum(branch_low.astype(jnp.float32), axis=0)
    attended_slope = jnp.einsum(
        "qd,ed->qe", branch_low, output_matrix, preferred_element_type=jnp.float32
    ).astype(jnp.bfloat16)
    query_slopes = []
    key_grads = []
    value_grads = []
    for head_index in range(HEADS):
        start_col = head_index * HEAD
        query_head = query_low[:, start_col : start_col + HEAD]
        key_head = canvas_memory[:, start_col : start_col + HEAD]
        value_head = canvas_memory[:, width + start_col : width + start_col + HEAD]
        scores = head_scores(query_head, key_head, same_scene, scale)
        probs_full = jnp.exp(scores - log_totals[head_index])
        probs_low = probs_full.astype(jnp.bfloat16)
        out_slope = attended_slope[:, start_col : start_col + HEAD]
        value_grads.append(
            jnp.einsum("qk,qe->ke", probs_low, out_slope, preferred_element_type=jnp.float32)
        )
        prob_slope = jnp.einsum(
            "qe,ke->qk", out_slope, value_head, preferred_element_type=jnp.float32
        )
        inner = jnp.sum(prob_slope * probs_full, axis=1, keepdims=True)
        score_slope = (probs_full * (prob_slope - inner)).astype(jnp.bfloat16)
        query_slopes.append(
            jnp.einsum("qk,ke->qe", score_slope, key_head, preferred_element_type=jnp.float32)
            * scale
        )
        key_grads.append(
            jnp.einsum("qk,qe->ke", score_slope, query_head, preferred_element_type=jnp.float32)
            * scale
        )
    query_slope = jnp.concatenate(query_slopes, axis=1).astype(jnp.bfloat16)
    memory_part = jnp.concatenate(key_grads + value_grads, axis=1)
    memory_slope = lax.psum_scatter(
        memory_part.astype(jnp.bfloat16), "seq", scatter_dimension=0, tiled=True
    )
    grad_memory = jnp.einsum(
        "kd,ke->de", memory_low, memory_slope, preferred_element_type=jnp.float32
    )
    grad_value_shift = jnp.sum(memory_slope[:, width:].astype(jnp.float32), axis=0)
    memory_in_slope = jnp.einsum(
        "ke,de->kd", memory_slope, memory_matrix, preferred_element_type=jnp.float32
    )
    reduced_slope, grad_gain_mem, grad_shift_mem = memory_norm_back(memory_in_slope)
    reduced_low = reduced_slope.astype(jnp.bfloat16)
    grad_reduce = jnp.einsum("kp,kd->pd", patches, reduced_low, preferred_element_type=jnp.float32)
    grad_reduce_shift = jnp.sum(reduced_low.astype(jnp.float32), axis=0)
    patch_slope = jnp.einsum(
        "kd,pd->kp", reduced_low, reduce_matrix, preferred_element_type=jnp.float32
    )
    patch_back = (
        patch_slope.reshape(band_rows // 2, side // 2, 2, 2, width)
        .transpose(0, 2, 1, 3, 4)
        .reshape(band_tokens, width)
    )
    grad_query = jnp.einsum(
        "qd,qe->de", normed_low, query_slope, preferred_element_type=jnp.float32
    )
    grad_query_shift = jnp.sum(query_slope.astype(jnp.float32), axis=0)
    normed_slope = (
        jnp.einsum("qe,de->qd", query_slope, query_matrix, preferred_element_type=jnp.float32)
        + patch_back
    )
    input_back, grad_gain_one, grad_shift_one = first_norm_back(normed_slope)
    token_grad = (middle_slope + input_back).astype(jnp.bfloat16).reshape(1, band_rows, side, width)
    gain_grad = jnp.stack([grad_gain_one, grad_gain_mem, grad_gain_two])
    shift_grad = jnp.stack(
        [
            grad_shift_one,
            grad_query_shift,
            grad_reduce_shift,
            grad_shift_mem,
            grad_value_shift,
            grad_shift_branch,
            grad_shift_two,
            grad_shift_out,
        ]
    )
    hidden_grad = jnp.stack(tap_grads + [grad_expand_shift, grad_depth_shift])
    column_sums = (
        lax.psum_scatter(
            grad_query.astype(jnp.bfloat16), "seq", scatter_dimension=1, tiled=True
        ).astype(jnp.float32),
        lax.psum_scatter(
            grad_reduce.astype(jnp.bfloat16), "seq", scatter_dimension=1, tiled=True
        ).astype(jnp.float32),
        lax.psum_scatter(
            grad_memory.astype(jnp.bfloat16), "seq", scatter_dimension=1, tiled=True
        ).astype(jnp.float32),
        lax.psum_scatter(
            grad_output.astype(jnp.bfloat16), "seq", scatter_dimension=1, tiled=True
        ).astype(jnp.float32),
        lax.psum_scatter(
            grad_expand.astype(jnp.bfloat16), "seq", scatter_dimension=1, tiled=True
        ).astype(jnp.float32),
        lax.psum_scatter(
            grad_contract.astype(jnp.bfloat16), "seq", scatter_dimension=1, tiled=True
        ).astype(jnp.float32),
    )
    vector_sums = vector_total(gain_grad, shift_grad, hidden_grad)
    owned = (
        lax.psum_scatter(
            column_sums[0].astype(jnp.bfloat16), "dp", scatter_dimension=0, tiled=True
        ).astype(jnp.float32),
        lax.psum_scatter(
            column_sums[1].astype(jnp.bfloat16), "dp", scatter_dimension=0, tiled=True
        ).astype(jnp.float32),
        lax.psum_scatter(
            column_sums[2].astype(jnp.bfloat16), "dp", scatter_dimension=0, tiled=True
        ).astype(jnp.float32),
        lax.psum_scatter(
            column_sums[3].astype(jnp.bfloat16), "dp", scatter_dimension=0, tiled=True
        ).astype(jnp.float32),
        lax.psum_scatter(
            column_sums[4].astype(jnp.bfloat16), "dp", scatter_dimension=0, tiled=True
        ).astype(jnp.float32),
        lax.psum_scatter(
            column_sums[5].astype(jnp.bfloat16), "dp", scatter_dimension=0, tiled=True
        ).astype(jnp.float32),
        lax.psum_scatter(
            vector_sums[0].astype(jnp.bfloat16), "dp", scatter_dimension=1, tiled=True
        ).astype(jnp.float32),
        lax.psum_scatter(
            vector_sums[1].astype(jnp.bfloat16), "dp", scatter_dimension=1, tiled=True
        ).astype(jnp.float32),
        lax.psum_scatter(
            vector_sums[2].astype(jnp.bfloat16), "dp", scatter_dimension=1, tiled=True
        ).astype(jnp.float32),
    )
    first_band = (lax.axis_index("seq") == 0).astype(jnp.float32)
    matrix_squares = sum((jnp.sum(element * element) for element in owned[:6]))
    vector_squares = sum((jnp.sum(element * element) for element in owned[6:]))
    total_squares = lax.psum(matrix_squares + first_band * vector_squares, ("dp", "seq"))
    global_norm = jnp.sqrt(total_squares)
    clip_factor = jnp.minimum(1.0, MAX_NORM / (global_norm + 1e-06))
    weights = (
        query_weight,
        reduce_weight,
        memory_weight,
        output_weight,
        expand_weight,
        contract_weight,
        norm_gains,
        biases,
        hidden_params,
    )
    firsts = (
        moment_query,
        moment_reduce,
        moment_memory,
        moment_output,
        moment_expand,
        moment_contract,
        moment_gains,
        moment_biases,
        moment_hidden,
    )
    seconds = (
        square_query,
        square_reduce,
        square_memory,
        square_output,
        square_expand,
        square_contract,
        square_gains,
        square_biases,
        square_hidden,
    )
    step_rates = (
        D ** (-0.5),
        (4 * D) ** (-0.5),
        D ** (-0.5),
        OUT_FAN ** (-0.5),
        D ** (-0.5),
        FF ** (-0.5),
        GAIN_RATE,
        VECTOR_RATE,
        VECTOR_RATE,
    )
    decays = (DECAY_RATE,) * 6 + (0.0,) * 3
    results = [
        adam_step(
            weights[index],
            firsts[index],
            seconds[index],
            clip_factor * owned[index],
            step_rates[index],
            decays[index],
        )
        for index in range(9)
    ]
    updated = [entry[0] for entry in results]
    momenta = [entry[1] for entry in results]
    squares = [entry[2] for entry in results]
    return (
        block_output,
        token_grad,
        global_norm,
        updated[0],
        updated[1],
        updated[2],
        updated[3],
        updated[4],
        updated[5],
        updated[6],
        updated[7],
        updated[8],
        momenta[0],
        momenta[1],
        momenta[2],
        momenta[3],
        momenta[4],
        momenta[5],
        momenta[6],
        momenta[7],
        momenta[8],
        squares[0],
        squares[1],
        squares[2],
        squares[3],
        squares[4],
        squares[5],
        squares[6],
        squares[7],
        squares[8],
    )


def solution(mesh):
    placed = (
        P("dp", "seq", None, None),
        P("dp"),
        P(None, "seq", "dp", None, None),
        P("dp", "seq"),
        P("dp", "seq"),
        P("dp", "seq"),
        P("dp", "seq"),
        P("dp", "seq"),
        P("dp", "seq"),
        P(None, "dp"),
        P(None, "dp"),
        P(None, "dp"),
        P("dp", "seq"),
        P("dp", "seq"),
        P("dp", "seq"),
        P("dp", "seq"),
        P("dp", "seq"),
        P("dp", "seq"),
        P(None, "dp"),
        P(None, "dp"),
        P(None, "dp"),
        P("dp", "seq"),
        P("dp", "seq"),
        P("dp", "seq"),
        P("dp", "seq"),
        P("dp", "seq"),
        P("dp", "seq"),
        P(None, "dp"),
        P(None, "dp"),
        P(None, "dp"),
    )
    return jax.shard_map(
        on_device,
        mesh=mesh,
        in_specs=placed,
        out_specs=(
            P(None, "seq", "dp", None, None),
            P("dp", "seq", None, None),
            P(),
            P("dp", "seq"),
            P("dp", "seq"),
            P("dp", "seq"),
            P("dp", "seq"),
            P("dp", "seq"),
            P("dp", "seq"),
            P(None, "dp"),
            P(None, "dp"),
            P(None, "dp"),
            P("dp", "seq"),
            P("dp", "seq"),
            P("dp", "seq"),
            P("dp", "seq"),
            P("dp", "seq"),
            P("dp", "seq"),
            P(None, "dp"),
            P(None, "dp"),
            P(None, "dp"),
            P("dp", "seq"),
            P("dp", "seq"),
            P("dp", "seq"),
            P("dp", "seq"),
            P("dp", "seq"),
            P("dp", "seq"),
            P(None, "dp"),
            P(None, "dp"),
            P(None, "dp"),
        ),
        check_vma=False,
    )
```

profile of v0, /device:TPU:0, one launch (start us, length us, event | category | flops | bytes accessed | tf_op | source)
XLA Modules:
  0.0 1074.6 jit_solution(8567536084389594148)
XLA Ops:
  12.7 27.8 %all-gather.1 = bf16[8,40,8]{1,2,0:T(8,128)(2,1)S(1)} all-gather(bf16[1,40,8]{1,2,0:T(8,128)(2,1)S(1)} %convert_bitcast_fusion.5), channel_id=1, replica_groups=mesh['dp'=8,'seq'=4] {'dp'}, dimensions={0}, use_global_device_ids=true | all-gather | bytes 5760 | tf_op jit(solution)/shard_map/all_gather | solution.py:183
  41.2 19.0 %all-gather = bf16[8,40,3]{1,2,0:T(4,128)(2,1)S(1)} all-gather(bf16[1,40,3]{1,2,0:T(4,128)(2,1)S(1)} %convert_bitcast_fusion.6), channel_id=1, replica_groups=mesh['dp'=8,'seq'=4] {'dp'}, dimensions={0}, use_global_device_ids=true | all-gather | bytes 2160 | tf_op jit(solution)/shard_map/all_gather | solution.py:182
  62.7 5.6 all_gather.52
  68.6 32.7 %all_gather.53 = bf16[1280,320]{1,0:T(8,128)(2,1)S(1)} all-gather(bf16[160,320]{1,0:T(8,128)(2,1)S(1)} %copy.318), channel_id=1, replica_groups=mesh['dp'=8,'seq'=4] {'dp'}, dimensions={0}, use_global_device_ids=true | all-gather | bytes 921600 | tf_op jit(solution)/shard_map/all_gather | solution.py:177
  102.5 5.3 all-gather.3
  108.0 31.1 %all_gather.55 = bf16[320,640]{1,0:T(8,128)(2,1)S(1)} all-gather(bf16[40,640]{1,0:T(8,128)(2,1)S(1)} %bitcast.169), channel_id=1, replica_groups=mesh['dp'=8,'seq'=4] {'dp'}, dimensions={0}, use_global_device_ids=true | all-gather | bytes 460800 | tf_op jit(solution)/shard_map/all_gather | solution.py:178
  141.1 3.6 all-to-all-start.1
  144.8 5.2 all-gather.2
  150.2 31.3 %all_gather.51 = bf16[320,320]{1,0:T(8,128)(2,1)S(1)} all-gather(bf16[40,320]{1,0:T(8,128)(2,1)S(1)} %bitcast.170), channel_id=1, replica_groups=mesh['dp'=8,'seq'=4] {'dp'}, dimensions={0}, use_global_device_ids=true | all-gather | bytes 230400 | tf_op jit(solution)/shard_map/all_gather | solution.py:176
  182.1 5.2 all-gather.4
  187.4 30.7 %all_gather.58 = bf16[320,320]{1,0:T(8,128)(2,1)S(1)} all-gather(bf16[40,320]{1,0:T(8,128)(2,1)S(1)} %bitcast.171), channel_id=1, replica_groups=mesh['dp'=8,'seq'=4] {'dp'}, dimensions={0}, use_global_device_ids=true | all-gather | bytes 230400 | tf_op jit(solution)/shard_map/all_gather | solution.py:179
  218.2 30.5 %all-gather.5 = bf16[8,160,11]{1,2,0:T(8,128)(2,1)S(1)} all-gather(bf16[1,160,11]{1,2,0:T(8,128)(2,1)S(1)} %convert_bitcast_fusion.4), channel_id=1, replica_groups=mesh['dp'=8,'seq'=4] {'dp'}, dimensions={0}, use_global_device_ids=true | all-gather | bytes 31680 | tf_op jit(solution)/shard_map/all_gather | solution.py:184
  248.9 5.4 all-gather.6
  259.0 5.5 all_gather.62
  266.9 34.0 %all_gather.61 = bf16[320,1280]{1,0:T(8,128)(2,1)} all-gather(bf16[40,1280]{1,0:T(8,128)(2,1)S(1)} %bitcast.166), channel_id=1, replica_groups=mesh['dp'=8,'seq'=4] {'dp'}, dimensions={0}, use_global_device_ids=true | all-gather | bytes 921600 | tf_op jit(solution)/shard_map/all_gather | solution.py:180
  300.9 35.3 %all_gather.63 = bf16[1280,320]{1,0:T(8,128)(2,1)} all-gather(bf16[160,320]{1,0:T(8,128)(2,1)S(1)} %copy.325), channel_id=1, replica_groups=mesh['dp'=8,'seq'=4] {'dp'}, dimensions={0}, use_global_device_ids=true | all-gather | bytes 921600 | tf_op jit(solution)/shard_map/all_gather | solution.py:181
  362.2 3.0 collective-permute-done.1
  366.9 22.1 %multiply_convert_fusion = (bf16[16,64,1280]{2,1,0:T(8,128)(2,1)S(1)}, f32[16,64,1280]{2,1,0:T(8,128)}, f32[16,64,1280]{2,1,0:T(8,128)}) fusion(f32[16,64]{1,0:T(8,128)S(1)} %copy-done.83, bf16[18,66,1280]{2,1,0:T(8,128)(2,1)S(1)} %select_maximum_fusion.2, f32[1280]{0:T(1024)S(1)} %copy-done.85, f32[16,64]{1,0:T(8,128)S(1)} %get-tuple-element.302, ...), kind=kLoop, calls=%fused_computation.70 | loop fusion | flops 133693440 | bytes 31868928 | tf_op jit(solution)/shard_map/convert_element_type | solution.py:250
  389.1 13.1 %fusion.41 = (bf16[1280]{0:T(1024)(128)(2,1)}, bf16[1280]{0:T(1024)(128)(2,1)}, bf16[1280]{0:T(1024)(128)(2,1)}, bf16[1280]{0:T(1024)(128)(2,1)}, bf16[1280]{0:T...) fusion(f32[16,64]{1,0:T(8,128)S(1)} %copy-done.83, ...), kind=kOutput, calls=%fused_computation.68 | convolution fusion | flops 893902080 | bytes 32974336 | tf_op jit(solution)/shard_map/qd,fd->qf/dot_general | solution.py:271
  402.9 6.4 collective-permute-start.2
  412.9 2.5 select_maximum_fusion
  415.6 12.8 %fusion.269 = (bf16[1280]{0:T(1024)(128)(2,1)}, bf16[16,64,1280]{2,1,0:T(8,128)(2,1)S(1)}) fusion(f32[16,64]{1,0:T(8,128)S(1)} %get-tuple-element.301, bf16[18,66,1280]{2,1,0:T(8,128)(2,1)S(1)} %select_maximum_fusion, f32[1280]{0:T(1024)S(1)} %copy-done.86, f32[16,64]{1,0:T(8,128)S(1)} %get-tuple-element.307, ...), kind=kLoop, calls=%fused_computation.453 | loop fusion | flops 49806080 | bytes 21380608 | tf_op jit(solution)/shard_map/reduce_sum | solution.py:305
  446.6 2.5 multiply_convert_fusion.2
  454.5 3.0 fusion.105
  457.5 3.4 multiply_reduce_fusion
  466.1 3.8 fusion.111
  469.9 2.5 fusion.117
  472.4 2.5 fusion.123
  488.1 2.5 convolution_convert_fusion.5
  490.7 3.3 fusion.39
  507.4 15.1 %reduce-scatter.29.cloned.1.call-done = bf16[256,640]{0,1:T(8,128)(2,1)} async-done(((bf16[1024,640]{0,1:T(8,128)(2,1)}), bf16[256,640]{0,1:T(8,128)(2,1)}) %reduce-scatter.29.cloned.1.call-update) | async-done | bytes 327696 | tf_op jit(solution)/shard_map/reduce_scatter | solution.py:350
  527.3 3.3 copy.391
  530.6 3.2 reshape.437
  533.8 3.0 copy.330
  542.0 3.5 reduce-scatter.31.cloned.1.call-done
  545.5 22.3 %reduce-scatter.37.cloned.1.call-done = bf16[320,80]{0,1:T(8,128)(2,1)} async-done(((bf16[320,320]{0,1:T(8,128)(2,1)}), bf16[320,80]{0,1:T(8,128)(2,1)}) %reduce-scatter.37.cloned.1.call-update) | async-done | bytes 51216 | tf_op jit(solution)/shard_map/reduce_scatter | solution.py:406
  569.2 3.1 fusion.86
  573.4 5.5 all-to-all-start
  587.2 48.3 %reduce-scatter.49.cloned.1.call-done = bf16[160,11]{1,0:T(8,128)(2,1)} async-done(((bf16[1280,11]{1,0:T(8,128)(2,1)}), bf16[160,11]{1,0:T(8,128)(2,1)}) %reduce-scatter.49.cloned.1.call-update) | async-done | bytes 3536
  637.0 62.5 %reduce-scatter.47.cloned.1.call-done = bf16[160,80]{1,0:T(8,128)(2,1)} async-done(((bf16[1280,80]{1,0:T(8,128)(2,1)}), bf16[160,80]{1,0:T(8,128)(2,1)}) %reduce-scatter.47.cloned.1.call-update) | async-done | bytes 25616
  700.9 59.9 %reduce-scatter.51.cloned.1.call-done = bf16[40,320]{1,0:T(8,128)(2,1)} async-done(((bf16[320,320]{1,0:T(8,128)(2,1)}), bf16[40,320]{1,0:T(8,128)(2,1)}) %reduce-scatter.51.cloned.1.call-update) | async-done | bytes 25616
  764.6 70.0 %all-reduce.12.cloned.1.call-done = (bf16[320,80]{0,1:T(8,128)(2,1)}, bf16[320,80]{0,1:T(8,128)(2,1)}, bf16[3,320]{1,0:T(4,128)(2,1)}, bf16[8,320]{1,0:T(8,128)(2,1)}) async-done(((bf16[320,80]{0,1:T(8,128)(2,1)}, bf16[320,80]{0,1:T(8,128)(2,1)}, bf16[3,320]{1,0:T(4,128)(2,1)}, bf16[8,320]{1,0:T(8,128)(2,1)}), (bf16[320,80]{0,1:T(8,128)(2,1)}, bf16[320,80]{0,1:T(8,128)(2,1)}, bf16[3,320]{1,0:T(4,128)(2,1)}, ...) | async-done | bytes 109456
  838.0 10.1 all-reduce.9
  848.1 10.3 reduce-scatter.35.cloned.1.call-done
  862.7 21.6 %reduce-scatter.33.cloned.1.call-done = bf16[1280,80]{0,1:T(8,128)(2,1)} async-done(((bf16[1280,320]{0,1:T(8,128)(2,1)}), bf16[1280,80]{0,1:T(8,128)(2,1)}) %reduce-scatter.33.cloned.1.call-update) | async-done | bytes 204816 | tf_op jit(solution)/shard_map/reduce_scatter | solution.py:400
  888.7 54.1 %reduce-scatter.43.cloned.1.call-done = bf16[40,160]{1,0:T(8,128)(2,1)} async-done(((bf16[320,160]{1,0:T(8,128)(2,1)}), bf16[40,160]{1,0:T(8,128)(2,1)}) %reduce-scatter.43.cloned.1.call-update) | async-done | bytes 12816 | tf_op jit(solution)/shard_map/reduce_scatter | solution.py:424
  944.2 63.1 %reduce-scatter.41.cloned.1.call-done = bf16[160,80]{1,0:T(8,128)(2,1)} async-done(((bf16[1280,80]{1,0:T(8,128)(2,1)}), bf16[160,80]{1,0:T(8,128)(2,1)}) %reduce-scatter.41.cloned.1.call-update) | async-done | bytes 25616
  1013.8 40.1 %psum.31 = f32[]{:T(128)} all-reduce(f32[]{:T(128)S(6)} %add.629), channel_id=1, replica_groups=mesh['dp'=8,'seq'=4] {'dp','seq'}, use_global_device_ids=true, to_apply=%region_77.78 | all-reduce | flops 1 | bytes 8 | tf_op jit(solution)/shard_map/psum | solution.py:449
  (588 shorter events, 158.3 us)
Async XLA Ops:
  7.2 331.4 %all-gather.9.cloned.1.call-start = ((), (), s32[]{:S(2)}) async-start(), calls=%async_computation.14 | async-start | bytes 1638400 | tf_op jit(solution)/shard_map/all_gather | solution.py:215
  41.2 315.4 %copy-start.159 = (f32[320]{0:T(512)}, f32[320]{0:T(512)S(1)}, u32[]{:S(2)}) copy-start(f32[320]{0:T(512)S(1)} %get-tuple-element.242) | copy-start | bytes 3844
  60.3 296.2 %copy-start.147 = (f32[320]{0:T(512)}, f32[320]{0:T(512)S(1)}, u32[]{:S(2)}) copy-start(f32[320]{0:T(512)S(1)} %get-tuple-element.249) | copy-start | bytes 3844
  141.1 195.1 %all-to-all-start.1 = ((bf16[8,1,1,128,320]{3,4,2,1,0:T(8,128)(2,1)}), bf16[8,1,1,128,320]{3,4,2,1,0:T(8,128)(2,1)S(1)}, u32[]{:S(2)}, u32[]{:S(2)}) async-start(bf16[8,1,1,128,320]{3,4,2,1,0:T(8,128)(2,1)} %param.32), calls=%async_computation.1 | async-start | bytes 1310720 | tf_op jit(solution)/shard_map/all_to_all | solution.py:265
  144.7 356.0 %reduce-scatter.39.cloned.1.call-start = ((), (), s32[]{:S(2)}) async-start(), calls=%async_computation.20 | async-start | bytes 1024000 | tf_op jit(solution)/shard_map/reduce_scatter | solution.py:412
  358.9 3.3 collective-permute-start
  360.3 4.9 collective-permute-start.1
  402.9 9.9 collective-permute-start.2
  409.3 3.6 collective-permute-start.3
  412.6 93.0 %reduce-scatter.45.cloned.1.call-start = ((), (), s32[]{:S(2)}) async-start(), calls=%async_computation.23 | async-start | bytes 1228800
  466.0 56.4 %reduce-scatter.29.cloned.1.call-start = ((), (), s32[]{:S(2)}) async-start(), calls=%async_computation.15 | async-start | bytes 1638400 | tf_op jit(solution)/shard_map/reduce_scatter | solution.py:350
  479.5 65.9 %reduce-scatter.31.cloned.1.call-start = ((), (), s32[]{:S(2)}) async-start(), calls=%async_computation.16 | async-start | bytes 307200 | tf_op jit(solution)/shard_map/reduce_scatter | solution.py:397
  488.1 79.7 %reduce-scatter.37.cloned.1.call-start = ((), (), s32[]{:S(2)}) async-start(), calls=%async_computation.19 | async-start | bytes 307200 | tf_op jit(solution)/shard_map/reduce_scatter | solution.py:406
  490.6 144.8 %reduce-scatter.49.cloned.1.call-start = ((), (), s32[]{:S(2)}) async-start(), calls=%async_computation.25 | async-start | bytes 368640
  500.6 198.8 %reduce-scatter.47.cloned.1.call-start = ((), (), s32[]{:S(2)}) async-start(), calls=%async_computation.24 | async-start | bytes 368640
  502.6 258.2 %reduce-scatter.51.cloned.1.call-start = ((), (), s32[]{:S(2)}) async-start(), calls=%async_computation.26 | async-start | bytes 276480
  507.3 327.2 %all-reduce.12.cloned.1.call-start = ((), (), s32[]{:S(2)}) async-start(), calls=%async_computation.27 | async-start | bytes 264192
  567.8 290.6 %reduce-scatter.35.cloned.1.call-start = ((), (), s32[]{:S(2)}) async-start(), calls=%async_computation.18 | async-start | bytes 614400 | tf_op jit(solution)/shard_map/reduce_scatter | solution.py:403
  573.4 63.5 %all-to-all-start = ((bf16[1,1,8,128,320]{3,4,1,0,2:T(8,128)(2,1)}), bf16[1,1,8,128,320]{3,4,1,0,2:T(8,128)(2,1)}, u32[]{:S(2)}, u32[]{:S(2)}) async-start(bf16[1,1,8,128,320]{3,4,1,0,2:T(8,128)(2,1)} %copy.326), calls=%async_computation | async-start | bytes 1310720 | tf_op jit(solution)/shard_map/all_to_all | solution.py:258
  578.9 305.5 %reduce-scatter.33.cloned.1.call-start = ((), (), s32[]{:S(2)}) async-start(), calls=%async_computation.17 | async-start | bytes 1024000 | tf_op jit(solution)/shard_map/reduce_scatter | solution.py:400
  580.3 362.5 %reduce-scatter.43.cloned.1.call-start = ((), (), s32[]{:S(2)}) async-start(), calls=%async_computation.22 | async-start | bytes 184320 | tf_op jit(solution)/shard_map/reduce_scatter | solution.py:424
  762.1 292.5 %copy-start.58 = (f32[160,80]{0,1:T(8,128)S(1)}, f32[160,80]{0,1:T(8,128)}, u32[]{:S(2)}) copy-start(f32[160,80]{0,1:T(8,128)} %copy-done.57) | copy-start | bytes 153604
  762.1 295.7 %copy-start.56 = (f32[160,80]{0,1:T(8,128)S(1)}, f32[160,80]{0,1:T(8,128)}, u32[]{:S(2)}) copy-start(f32[160,80]{0,1:T(8,128)} %copy-done.55) | copy-start | bytes 153604
  762.2 301.2 %copy-start.65 = (f32[40,320]{1,0:T(8,128)S(1)}, f32[40,320]{1,0:T(8,128)}, u32[]{:S(2)}) copy-start(f32[40,320]{1,0:T(8,128)} %param.37) | copy-start | bytes 153604
  764.3 293.6 %copy-start.62 = (f32[160,80]{0,1:T(8,128)S(1)}, f32[160,80]{0,1:T(8,128)}, u32[]{:S(2)}) copy-start(f32[160,80]{0,1:T(8,128)} %copy.335) | copy-start | bytes 153604
  764.3 293.6 %copy-start.63 = (f32[160,80]{0,1:T(8,128)S(1)}, f32[160,80]{0,1:T(8,128)}, u32[]{:S(2)}) copy-start(f32[160,80]{0,1:T(8,128)} %copy.336) | copy-start | bytes 153604
  764.3 295.9 %copy-start.109 = (f32[11,160]{1,0:T(8,128)S(1)}, f32[11,160]{1,0:T(8,128)}, u32[]{:S(2)}) copy-start(f32[11,160]{1,0:T(8,128)} %param.41) | copy-start | bytes 21124
  764.3 295.8 %copy-start.140 = (f32[11,160]{1,0:T(8,128)S(1)}, f32[11,160]{1,0:T(8,128)}, u32[]{:S(2)}) copy-start(f32[11,160]{1,0:T(8,128)} %param.50) | copy-start | bytes 21124
  764.3 295.8 %copy-start.141 = (f32[11,160]{1,0:T(8,128)S(1)}, f32[11,160]{1,0:T(8,128)}, u32[]{:S(2)}) copy-start(f32[11,160]{1,0:T(8,128)} %param.59) | copy-start | bytes 21124
  764.3 296.5 %copy-start.139 = (f32[8,40]{1,0:T(8,128)S(1)}, f32[8,40]{1,0:T(8,128)}, u32[]{:S(2)}) copy-start(f32[8,40]{1,0:T(8,128)} %param.40) | copy-start | bytes 3844
  764.3 296.5 %copy-start.156 = (f32[8,40]{1,0:T(8,128)S(1)}, f32[8,40]{1,0:T(8,128)}, u32[]{:S(2)}) copy-start(f32[8,40]{1,0:T(8,128)} %param.49) | copy-start | bytes 3844
  764.4 296.4 %copy-start.157 = (f32[8,40]{1,0:T(8,128)S(1)}, f32[8,40]{1,0:T(8,128)}, u32[]{:S(2)}) copy-start(f32[8,40]{1,0:T(8,128)} %param.58) | copy-start | bytes 3844
  764.4 297.1 %copy-start.154 = (f32[3,40]{1,0:T(4,128)S(1)}, f32[3,40]{1,0:T(4,128)}, u32[]{:S(2)}) copy-start(f32[3,40]{1,0:T(4,128)} %param.39) | copy-start | bytes 1444
  764.4 297.1 %copy-start.161 = (f32[3,40]{1,0:T(4,128)S(1)}, f32[3,40]{1,0:T(4,128)}, u32[]{:S(2)}) copy-start(f32[3,40]{1,0:T(4,128)} %param.48) | copy-start | bytes 1444
  764.4 297.0 %copy-start.162 = (f32[3,40]{1,0:T(4,128)S(1)}, f32[3,40]{1,0:T(4,128)}, u32[]{:S(2)}) copy-start(f32[3,40]{1,0:T(4,128)} %param.57) | copy-start | bytes 1444
  764.4 297.6 %copy-start.74 = (f32[40,80]{1,0:T(8,128)S(1)}, f32[40,80]{1,0:T(8,128)}, u32[]{:S(2)}) copy-start(f32[40,80]{1,0:T(8,128)} %param.36) | copy-start | bytes 38404
  764.4 297.6 %copy-start.132 = (f32[40,80]{1,0:T(8,128)S(1)}, f32[40,80]{1,0:T(8,128)}, u32[]{:S(2)}) copy-start(f32[40,80]{1,0:T(8,128)} %param.45) | copy-start | bytes 38404
  764.4 297.6 %copy-start.133 = (f32[40,80]{1,0:T(8,128)S(1)}, f32[40,80]{1,0:T(8,128)}, u32[]{:S(2)}) copy-start(f32[40,80]{1,0:T(8,128)} %param.54) | copy-start | bytes 38404
  764.4 298.3 %copy-start.76 = (f32[40,80]{1,0:T(8,128)S(1)}, f32[40,80]{1,0:T(8,128)}, u32[]{:S(2)}) copy-start(f32[40,80]{1,0:T(8,128)} %param.33) | copy-start | bytes 38404
  764.5 298.2 %copy-start.134 = (f32[40,80]{1,0:T(8,128)S(1)}, f32[40,80]{1,0:T(8,128)}, u32[]{:S(2)}) copy-start(f32[40,80]{1,0:T(8,128)} %param.42) | copy-start | bytes 38404
  764.5 298.2 %copy-start.135 = (f32[40,80]{1,0:T(8,128)S(1)}, f32[40,80]{1,0:T(8,128)}, u32[]{:S(2)}) copy-start(f32[40,80]{1,0:T(8,128)} %param.51) | copy-start | bytes 38404
  764.5 298.9 %copy-start.68 = (bf16[40,320]{1,0:T(8,128)(2,1)S(1)}, bf16[40,320]{1,0:T(8,128)(2,1)}, u32[]{:S(2)}) copy-start(bf16[40,320]{1,0:T(8,128)(2,1)} %reduce-scatter.51.cloned.1.call-done) | copy-start | bytes 76804
  764.5 298.9 %copy-start.112 = (f32[40,320]{1,0:T(8,128)S(1)}, f32[40,320]{1,0:T(8,128)}, u32[]{:S(2)}) copy-start(f32[40,320]{1,0:T(8,128)} %param.46) | copy-start | bytes 153604
  764.5 298.9 %copy-start.113 = (f32[40,320]{1,0:T(8,128)S(1)}, f32[40,320]{1,0:T(8,128)}, u32[]{:S(2)}) copy-start(f32[40,320]{1,0:T(8,128)} %param.55) | copy-start | bytes 153604
  764.5 299.6 %copy-start.67 = (f32[40,160]{1,0:T(8,128)S(1)}, f32[40,160]{1,0:T(8,128)}, u32[]{:S(2)}) copy-start(f32[40,160]{1,0:T(8,128)} %param.35) | copy-start | bytes 76804
  764.5 299.5 %copy-start.118 = (f32[40,160]{1,0:T(8,128)S(1)}, f32[40,160]{1,0:T(8,128)}, u32[]{:S(2)}) copy-start(f32[40,160]{1,0:T(8,128)} %param.44) | copy-start | bytes 76804
  764.5 299.5 %copy-start.119 = (f32[40,160]{1,0:T(8,128)S(1)}, f32[40,160]{1,0:T(8,128)}, u32[]{:S(2)}) copy-start(f32[40,160]{1,0:T(8,128)} %param.53) | copy-start | bytes 76804
  860.2 147.1 %reduce-scatter.41.cloned.1.call-start = ((), (), s32[]{:S(2)}) async-start(), calls=%async_computation.21 | async-start | bytes 368640
  (138 other events, 3346.6 us)
Sparse Core Ops, SparseCore 0:
  141.2 15.7 all-gather.8
  412.7 25.0 reduce-scatter.38
  466.2 27.2 reduce-scatter.44
  495.9 26.5 reduce-scatter.28
  525.5 19.9 reduce-scatter.30
  547.8 19.9 reduce-scatter.36
  571.4 64.0 reduce-scatter.48
  639.1 60.2 reduce-scatter.46
  703.1 57.6 reduce-scatter.50
  765.3 69.2 all-reduce.11
  837.7 20.7 reduce-scatter.34
  860.9 23.4 reduce-scatter.32
  888.4 54.3 reduce-scatter.42
  946.8 60.3 reduce-scatter.40
where the time goes:
time: 1080 us; the launch traced here: 1070 us
  waiting for transfers between devices  434 us (40%)
  blocking collectives  355 us (33%)
  other arithmetic  84.2 us (8%)
  matrix products  84 us (8%)
  local copies, waits for them, and re-layouts  71.5 us (7%)
  between operations  25.7 us (2%)
  starting transfers between devices  20.2 us (2%)
    unnamed x20, waiting for transfers between devices  304 us
    reduce_scatter x1, waiting for transfers between devices, on_device(): lax.psum_scatter(column_sums[2].astype(jnp.bfloat16), 'dp', scatter_dimen...  54.1 us
    psum x1, blocking collectives, on_device(): lax.psum(matrix_squares + first_band * vector_squares, ('dp', 'seq'))  40.1 us
    unnamed x364, local copies, waits for them, and re-layouts  40 us
    all_gather x1, blocking collectives, on_device(): lax.all_gather(column_parts[5], 'dp', axis=0, tiled=True)  35.3 us
    all_gather x1, blocking collectives, on_device(): lax.all_gather(column_parts[4], 'dp', axis=0, tiled=True)  34 us
    all_gather x1, blocking collectives, on_device(): lax.all_gather(column_parts[1], 'dp', axis=0, tiled=True)  32.7 us
    all_gather x1, blocking collectives, on_device(): lax.all_gather(column_parts[0], 'dp', axis=0, tiled=True)  31.3 us
  transfers between devices with their start and end apart: 20, of which 13 were waited for; matrix products, arithmetic and copies ran while one was open for 14% of the time, Pallas kernels for 0%

commit v1 on v0

v1 whole, which is shorter than its diff:
```python
import functools

import jax
import jax.numpy as jnp
from jax import lax
from jax.experimental import pallas as pl
from jax.experimental.pallas import tpu as pltpu
from jax.sharding import PartitionSpec as P

D = 320
HEADS = 5
HEAD = 64
FF = 1280
STEP = 10
OUT_FAN = 5

NORM_EPS = 1e-06
MAX_NORM = 1.0
BETA_ONE = 0.9
BETA_TWO = 0.95
ADAM_EPS = 1e-08
DECAY_RATE = 0.01
VECTOR_RATE = 0.3
GAIN_RATE = 0.8
MASKED = -1e30

BF = jnp.bfloat16
F32 = jnp.float32
MESH = pl.DeviceIdType.MESH
QC = 256
VMEM_LIMIT = 63 * 1024 * 1024


def nn(a, b):
    return lax.dot_general(a, b, (((1,), (0,)), ((), ())), preferred_element_type=F32)


def nt(a, b):
    return lax.dot_general(a, b, (((1,), (1,)), ((), ())), preferred_element_type=F32)


def up(n, m):
    return (n + m - 1) // m * m


def norm_parts(v):
    centered = v - jnp.mean(v, axis=-1, keepdims=True)
    rstd = lax.rsqrt(jnp.mean(centered * centered, axis=-1, keepdims=True) + NORM_EPS)
    return centered * rstd, rstd


def norm_back(v, gain, e):
    vhat, rstd = norm_parts(v)
    u = e * gain
    dv = rstd * (
        u
        - jnp.mean(u, axis=-1, keepdims=True)
        - vhat * jnp.mean(u * vhat, axis=-1, keepdims=True)
    )
    return dv, jnp.sum(e * vhat, axis=0, keepdims=True), jnp.sum(e, axis=0, keepdims=True)


def colsum(v):
    return jnp.sum(v, axis=0, keepdims=True)


def rows(start, size):
    return pl.ds(pl.multiple_of(start, 16), size)


def block_kernel(
    n,
    side,
    band,
    bucket_ref,
    tok_ref,
    cot_ref,
    wq_ref,
    wr_ref,
    wm_ref,
    wo_ref,
    w1_ref,
    w2_ref,
    gains_ref,
    biases_ref,
    hidden_ref,
    out_ref,
    tgrad_ref,
    own_ref,
    x_s,
    fq,
    fr,
    fm,
    fo,
    f1,
    f2,
    fg,
    fb,
    fh,
    gvec,
    g0,
    g1,
    vp,
    hp,
    wqt,
    wqp,
    wot,
    wop,
    wmt,
    wrt,
    w1t,
    w2t,
    a3,
    abf,
    pat,
    red_s,
    memin,
    kv,
    kvt,
    kmask,
    qmask,
    qnat,
    qt,
    prob,
    att_t,
    att_n,
    rtot,
    delta,
    mid,
    bn,
    bn_t,
    hidp,
    hidh,
    act,
    gp,
    out_t,
    dy_in,
    dy_t,
    dy,
    dzh,
    datn,
    gkv,
    rk1,
    rk2,
    dq_t,
    hg,
    vg,
    rf1,
    rf2,
    rf3,
    rt1,
    rt2,
    rt3,
    rm1,
    rm2,
    rm3,
    sv,
    rv1,
    rv2,
    rv3,
    nrm,
    nrs,
    maskl,
    maskr,
    loc,
    vg_s,
    vg_r,
    ga_s,
    ga_r,
    gb_s,
    gb_r,
    gx_s,
    gx_r,
    co_s,
    co_r,
    ou_s,
    ou_r,
    kv_s,
    kv_r,
    ha_s,
    ha_r,
    dk_s,
    dk_r,
    rs_s,
    rs_r,
    rd_s,
    rd_r,
    nd_s,
    nd_r,
    ns_s,
    ns_r,
):
    me = lax.axis_index("dp")
    j = lax.axis_index("seq")
    j1 = j + 1 - 2 * lax.rem(j, 2)
    j2 = lax.rem(j + 2, 4)
    j3 = 3 - j
    tokens = band * side
    chunks = tokens // QC
    rb = wq_ref.shape[0]
    piece = tokens // n
    keys = kv.shape[2]
    turned = cot_ref.shape[1] == D

    def remote(src, dst, ss, rs, dp, seq):
        return pltpu.make_async_remote_copy(
            src_ref=src,
            dst_ref=dst,
            send_sem=ss,
            recv_sem=rs,
            device_id=(dp, seq),
            device_id_type=MESH,
        )

    def peers(body):
        def step(k, carry):
            body(k, lax.rem(me + k, n), lax.rem(me + n - k, n))
            return carry

        lax.fori_loop(1, n, step, 0)

    loads = [
        pltpu.make_async_copy(src, dst, loc.at[at])
        for at, (src, dst) in enumerate(
            (
                (gains_ref, fg),
                (biases_ref, fb),
                (hidden_ref, fh),
                (wr_ref, fr),
                (wm_ref, fm),
                (wq_ref, fq),
                (wo_ref, fo),
                (w1_ref, f1),
                (w2_ref, f2),
                (tok_ref, x_s),
            )
        )
    ]
    for copy in loads:
        copy.start()
    own_cot = pltpu.make_async_copy(cot_ref.at[me], dy_in.at[me], loc.at[10])
    own_cot.start()

    barrier = pltpu.get_barrier_semaphore()

    def greet(k, peer, source):
        pl.semaphore_signal(barrier, inc=1, device_id=(peer, j), device_id_type=MESH)

    peers(greet)
    for other in (j1, j2, j3):
        pl.semaphore_signal(barrier, inc=1, device_id=(me, other), device_id_type=MESH)

    for copy in loads[:3]:
        copy.wait()
    vl = gvec.shape[2]
    hidden16 = jnp.concatenate([fh[...], jnp.zeros((5, 4 * rb), F32)], axis=0)
    small16 = jnp.concatenate([fg[...], fb[...], jnp.zeros((5, rb), F32)], axis=0)
    gvec[me] = jnp.concatenate(
        [hidden16, small16, jnp.zeros((16, vl - 5 * rb), F32)], axis=1
    ).astype(BF)
    for copy in loads[3:7]:
        copy.wait()
    width0 = up(8 * rb, 128)
    wm_t = fm[...].T
    g0[j, me, :, 0:width0] = jnp.concatenate(
        [
            fr[...].T,
            wm_t[0:80],
            wm_t[80:160],
            fq[...].T,
            fo[...].T,
            jnp.zeros((80, width0 - 8 * rb), F32),
        ],
        axis=1,
    ).astype(BF)

    first_block = g0.at[:, :, :, 0:width0]
    tl = up(6 * rb, 128)
    ml = up(2 * rb, 128)
    st = g0.at[:, :, :, 0:tl]
    sm = g0.at[:, :, :, tl : tl + ml]
    pl.semaphore_wait(barrier, n - 1 + 3)

    def send_vec(k, peer, source):
        remote(gvec.at[me], gvec.at[me], vg_s.at[k], vg_r.at[k], peer, j).start()

    def wait_vec(k, peer, source):
        d = remote(gvec.at[source], gvec.at[source], vg_s.at[k], vg_r.at[k], peer, j)
        d.wait_send()
        d.wait_recv()

    def send_g0(k, peer, source):
        remote(first_block.at[j, me], first_block.at[j, me], ga_s.at[k], ga_r.at[k], peer, j).start()

    def wait_g0(k, peer, source):
        d = remote(first_block.at[j, source], first_block.at[j, source], ga_s.at[k], ga_r.at[k], peer, j)
        d.wait_send()
        d.wait_recv()

    def send_g1(k, peer, source):
        remote(g1.at[j, me], g1.at[j, me], gb_s.at[k], gb_r.at[k], peer, j).start()

    def wait_g1(k, peer, source):
        d = remote(g1.at[j, source], g1.at[j, source], gb_s.at[k], gb_r.at[k], peer, j)
        d.wait_send()
        d.wait_recv()

    def seq_gather(g, at):
        def copy(slot, t, other):
            return remote(g.at[slot], g.at[slot], gx_s.at[at, t], gx_r.at[at, t], me, other)

        def first():
            copy(j, 0, j2).start()
            copy(j, 1, j1).start()

        def second():
            copy(j2, 0, j2).wait_recv()
            copy(j2, 2, j1).start()

        def third():
            copy(j, 0, j2).wait_send()
            copy(j, 1, j1).wait_send()
            copy(j1, 1, j1).wait_recv()
            copy(j2, 2, j1).wait_send()
            copy(j3, 2, j1).wait_recv()

        return first, second, third

    peers(send_vec)
    peers(send_g0)

    for copy in loads[7:9]:
        copy.wait()
    w1_t = f1[...].T
    g1[j, me] = jnp.concatenate(
        [f2[...].T]
        + [w1_t[80 * v : 80 * v + 80] for v in range(4)]
        + [jnp.zeros((80, g1.shape[3] - 8 * rb), F32)],
        axis=1,
    ).astype(BF)

    peers(wait_vec)
    hp[...] = jnp.concatenate([gvec[i, :, 0 : 4 * rb] for i in range(n)], axis=1).astype(F32)
    vp[...] = jnp.concatenate(
        [gvec[i, :, 4 * rb : 5 * rb] for i in range(n)], axis=1
    ).astype(F32)

    def gain(k):
        return vp[k : k + 1, :]

    def shift(k):
        return vp[3 + k : 4 + k, :]

    loads[9].wait()

    def norm_one(c, carry):
        at = rows(c * QC, QC)
        vhat, _ = norm_parts(x_s[at, :].astype(F32))
        low = (vhat * gain(0) + shift(0)).astype(BF)
        abf[at, :] = low
        wide = jnp.concatenate([low.astype(F32), jnp.zeros((QC, 64), F32)], axis=1)
        for t in range(3):
            a3[t, at, :] = wide[:, 128 * t : 128 * t + 128]
        return carry

    lax.fori_loop(0, chunks, norm_one, 0)
    half = side // 2
    for dd in range(4):
        for i in range(band // 2):
            start = (2 * i + dd // 2) * side + dd % 2
            cut = jnp.concatenate(
                [a3[t, pl.ds(start, half, stride=2), :] for t in range(3)], axis=1
            )
            pat[dd, i * half : (i + 1) * half, :] = cut[:, 0:D].astype(BF)

    bucket = bucket_ref[0]
    k_row = lax.broadcasted_iota(jnp.int32, (4 * keys, 128), 0)
    k_lane = lax.broadcasted_iota(jnp.int32, (4 * keys, 128), 1)
    k_id = (lax.div(k_row, half) >= half // 2).astype(jnp.int32) * 2 + (
        lax.rem(k_row, half) >= half // 2
    ).astype(jnp.int32)
    off = (k_id != k_lane).astype(jnp.int32) * bucket * (k_lane < 4).astype(jnp.int32)
    kmask[...] = (off.astype(F32) * MASKED).astype(BF)
    q_row = lax.broadcasted_iota(jnp.int32, (128, QC), 0)
    q_at = lax.broadcasted_iota(jnp.int32, (128, QC), 1)
    for c in range(chunks):
        place = q_at + c * QC
        q_id = (lax.div(place, side) + j * band >= half).astype(jnp.int32) * 2 + (
            lax.rem(place, side) >= half
        ).astype(jnp.int32)
        qmask[c] = (q_id == q_row).astype(F32).astype(BF)
    col = lax.broadcasted_iota(jnp.int32, (side, 128), 0)
    maskl[...] = ((col > 0).astype(jnp.int32) * (1 - bucket * (col == half).astype(jnp.int32))).astype(F32)
    maskr[...] = (
        (col < side - 1).astype(jnp.int32) * (1 - bucket * (col == half - 1).astype(jnp.int32))
    ).astype(F32)
    top_ok = (
        (j > 0).astype(jnp.int32) * (1 - bucket * (j * band == half).astype(jnp.int32))
    ).astype(F32)
    low_ok = (
        (j < 3).astype(jnp.int32) * (1 - bucket * ((j + 1) * band == half).astype(jnp.int32))
    ).astype(F32)

    first0, second0, third0 = seq_gather(first_block, 0)
    first1, second1, third1 = seq_gather(g1, 1)
    peers(wait_g0)
    first0()
    peers(send_g1)

    def send_cot(k, peer, source):
        remote(cot_ref.at[peer], dy_in.at[me], co_s.at[k], co_r.at[k], peer, j).start()

    def wait_cot(k, peer, source):
        d = remote(cot_ref.at[peer], dy_in.at[source], co_s.at[k], co_r.at[k], peer, j)
        d.wait_send()
        d.wait_recv()

    peers(send_cot)
    second0()
    third0()

    for s in range(4):
        span = slice(80 * s, 80 * s + 80)

        def lanes(lo, hi, over):
            return jnp.concatenate([g0[s, i, :, lo:hi] for i in over], axis=1)

        for dd in range(4):
            wrt[dd, span, :] = lanes(0, 4 * rb, range(dd * n // 4, (dd + 1) * n // 4))
        for v in range(2):
            wop[160 * s + 80 * v : 160 * s + 80 * v + 80, :] = lanes(
                (4 + v) * rb, (5 + v) * rb, range(n)
            )
        wqt[span, :] = lanes(6 * rb, 7 * rb, range(n))
        wot[span, :] = lanes(7 * rb, 8 * rb, range(n))
    for h in range(HEADS):
        head = slice(HEAD * h, HEAD * h + HEAD)
        wmt[128 * h : 128 * h + 64, :] = wop[head, :]
        wmt[128 * h + 64 : 128 * h + 128, :] = wop[D + HEAD * h : D + HEAD * h + HEAD, :]
        wqp[128 * h : 128 * h + 64, :] = wqt[head, :]
        wqp[128 * h + 64 : 128 * h + 128, :] = jnp.zeros((64, D), BF)

    red = shift(2) + nt(pat[0], wrt[0])
    for dd in range(1, 4):
        red = red + nt(pat[dd], wrt[dd])
    red_s[...] = red
    vhat, _ = norm_parts(red)
    low = (vhat * gain(1) + shift(3)).astype(BF)
    memin[...] = low
    zero64 = jnp.zeros((1, HEAD), F32)
    value_shift = jnp.concatenate(
        [
            part
            for h in range(HEADS)
            for part in (zero64, shift(4)[:, HEAD * h : HEAD * h + HEAD])
        ],
        axis=1,
    )
    memory = (nt(low, wmt[...]) + value_shift).astype(BF)
    for h in range(HEADS):
        kv[h, j] = memory[:, 128 * h : 128 * h + 128]

    def kv_copy(h, slot, t, other):
        return remote(
            kv.at[h, slot], kv.at[h, slot], kv_s.at[h, t], kv_r.at[h, t], me, other
        )

    def kv_send(h, carry):
        kv_copy(h, j, 0, j2).start()
        kv_copy(h, j, 1, j1).start()
        return carry

    lax.fori_loop(0, HEADS, kv_send, 0)

    query_shift = jnp.concatenate(
        [
            part
            for h in range(HEADS)
            for part in (shift(1)[:, HEAD * h : HEAD * h + HEAD], zero64)
        ],
        axis=1,
    )

    def queries(c, carry):
        at = rows(c * QC, QC)
        q = (nt(abf[at, :], wqp[...]) + query_shift).astype(BF) * jnp.asarray(HEAD**-0.5, BF)
        for h in range(HEADS):
            tile = q[:, 128 * h : 128 * h + 128]
            qnat[h, at, :] = tile
            qt[h, c] = tile.T
        return carry

    lax.fori_loop(0, chunks, queries, 0)
    wop_full = wot[...].T
    for h in range(HEADS):
        wop[128 * h : 128 * h + 64, :] = jnp.zeros((64, D), BF)
        wop[128 * h + 64 : 128 * h + 128, :] = wop_full[HEAD * h : HEAD * h + HEAD, :]

    def kv_forward(h, carry):
        kv_copy(h, j2, 0, j2).wait_recv()
        kv_copy(h, j2, 2, j1).start()
        return carry

    lax.fori_loop(0, HEADS, kv_forward, 0)
    peers(wait_g1)
    first1()

    ones = jnp.ones((16, 4 * keys), BF)

    def attend(h, carry):
        kv_copy(h, j, 0, j2).wait_send()
        kv_copy(h, j, 1, j1).wait_send()
        kv_copy(h, j2, 2, j1).wait_send()
        kv_copy(h, j1, 1, j1).wait_recv()
        kv_copy(h, j3, 2, j1).wait_recv()
        tile = kv[h].reshape(4 * keys, 128)
        kvt[h] = tile.T

        def chunk(c, inner):
            left = jnp.concatenate([kv[h].reshape(4 * keys, 128), kmask[...]], axis=1)
            right = jnp.concatenate([qt[h, c], qmask[c]], axis=0)
            scores = nn(left, right)
            largest = jnp.max(scores, axis=0, keepdims=True)
            powers = jnp.exp(scores - largest).astype(BF)
            prob[h, c] = powers
            values = jnp.concatenate([kvt[h, 64:128, :], ones], axis=0)
            got = nn(values, powers)
            scale = 1.0 / got[64:65, :]
            rtot[h, c] = scale
            att_t[c, rows(h * HEAD, HEAD), :] = (got[0:64, :] * scale).astype(BF)
            return inner

        lax.fori_loop(0, chunks, chunk, 0)
        return carry

    lax.fori_loop(0, HEADS, attend, 0)
    second1()

    def middle(c, carry):
        at = rows(c * QC, QC)
        att = att_t[c].T
        att_n[at, :] = att
        value = x_s[at, :].astype(F32) + nt(att, wot[...]) + shift(5)
        mid[at, :] = value
        vhat, _ = norm_parts(value)
        low = (vhat * gain(2) + shift(6)).astype(BF)
        bn[at, :] = low
        bn_t[:, pl.ds(pl.multiple_of(c * QC, QC), QC)] = low.T
        return carry

    lax.fori_loop(0, chunks, middle, 0)

    third1()
    for s in range(4):
        w2t[80 * s : 80 * s + 80, :] = jnp.concatenate(
            [g1[s, i, :, 0 : 4 * rb] for i in range(n)], axis=1
        )
        for v in range(4):
            at = 320 * s + 80 * v
            w1t[at : at + 80, :] = jnp.concatenate(
                [g1[s, i, :, (4 + v) * rb : (5 + v) * rb] for i in range(n)], axis=1
            )

    edge = tokens - side

    def hidden_of(value):
        return (nt(value, w1t[...]) + hp[9:10, :]).astype(BF)

    ends = hidden_of(jnp.concatenate([bn[0:side, :], bn[edge:tokens, :]], axis=0))
    hidp[side : 2 * side, :] = ends[0:side]
    hidp[tokens : tokens + side, :] = ends[side : 2 * side]
    above = lax.rem(j + 3, 4)
    below = lax.rem(j + 1, 4)

    def rim(buf, halo, at):
        return (
            remote(buf.at[pl.ds(side, side)], halo.at[1], ha_s.at[at], ha_r.at[at], me, above),
            remote(
                buf.at[pl.ds(tokens, side)], halo.at[0], ha_s.at[at + 1], ha_r.at[at + 1], me, below
            ),
        )

    def rim_send(buf, halo, at):
        for copy in rim(buf, halo, at):
            copy.start()

    def rim_wait(buf, halo, at):
        for copy in rim(buf, halo, at):
            copy.wait_send()
            copy.wait_recv()
        buf[0:side, :] = (halo[0].astype(F32) * top_ok).astype(BF)
        buf[tokens + side : tokens + 2 * side, :] = (halo[1].astype(F32) * low_ok).astype(BF)

    rim_send(hidp, hidh, 0)

    def inner_hidden(c, carry):
        start = side + c * 2 * side
        hidp[rows(start + side, 2 * side), :] = hidden_of(bn[rows(start, 2 * side), :])
        return carry

    lax.fori_loop(0, (tokens - 2 * side) // (2 * side), inner_hidden, 0)
    rim_wait(hidp, hidh, 0)

    def taps_of(lanes):
        return [hp[k : k + 1, lanes] for k in range(9)]

    def conv_tile(t, carry):
        lanes = pl.ds(pl.multiple_of(t * 128, 128), 128)
        taps = taps_of(lanes)
        base = hp[10:11, lanes]

        def row(r, inner):
            around = [hidp[rows((r + a) * side, side), lanes].astype(F32) for a in range(3)]
            parts = [
                taps[b] * around[0] + taps[3 + b] * around[1] + taps[6 + b] * around[2]
                for b in range(3)
            ]
            z = (
                base
                + parts[1]
                + maskl[...] * pltpu.roll(parts[0], 1, 0)
                + maskr[...] * pltpu.roll(parts[2], side - 1, 0)
            )
            cdf = 0.5 + 0.5 * lax.erf(z * (0.5**0.5))
            pdf = jnp.exp(z * z * -0.5) * 0.3989422804014327
            act[rows((r + 1) * side, side), lanes] = (z * cdf).astype(BF)
            gp[rows(r * side, side), lanes] = (cdf + z * pdf).astype(BF)
            return inner

        lax.fori_loop(0, band, row, 0)
        return carry

    lax.fori_loop(0, FF // 128, conv_tile, 0)

    def out_piece(at, d):
        value = (
            mid[rows(d * piece, piece), :]
            + nt(act[rows(side + d * piece, piece), :], w2t[...])
            + shift(7)
        )
        out_t[at] = (value.T if turned else value).astype(BF)

    def send_out(k, peer, source):
        out_piece(k, peer)
        remote(out_t.at[k], out_ref.at[me], ou_s.at[k], ou_r.at[k], peer, j).start()

    def wait_out(k, peer, source):
        d = remote(out_t.at[k], out_ref.at[source], ou_s.at[k], ou_r.at[k], peer, j)
        d.wait_send()
        d.wait_recv()

    peers(send_out)
    out_piece(0, me)
    own_out = pltpu.make_async_copy(out_t.at[0], out_ref.at[me], loc.at[11])
    own_out.start()

    own_cot.wait()
    peers(wait_cot)
    for i in range(n):
        if turned:
            dy_t[:, i * piece : (i + 1) * piece] = dy_in[i]
            dy[i * piece : (i + 1) * piece, :] = dy_in[i].T
        else:
            dy[i * piece : (i + 1) * piece, :] = dy_in[i]
    if not turned:
        dy_t[...] = dy[...].T
    vg[...] = jnp.zeros(vg.shape, F32)
    vg[10:11, :] = colsum(dy[...].astype(F32))

    sf = g1
    per = 640 // (4 * rb)
    for b in range(2):
        value = nn(dy_t[...], act[side : side + tokens, 640 * b : 640 * b + 640]).astype(BF)
        for ii in range(per):
            sf[:, b * per + ii, :, 0 : 4 * rb] = value[:, 4 * rb * ii : 4 * rb * (ii + 1)].reshape(
                4, 80, 4 * rb
            )

    def slope_of(at):
        return nn(dy[at, :], w2t[...])

    dz = act
    for at in (0, edge):
        dz[side + at : 2 * side + at, :] = (
            slope_of(slice(at, at + side)) * gp[at : at + side, :].astype(F32)
        ).astype(BF)
    rim_send(dz, dzh, 2)

    def inner_slope(c, carry):
        at = rows(side + c * 2 * side, 2 * side)
        dz[rows(2 * side + c * 2 * side, 2 * side), :] = (
            slope_of(at) * gp[at, :].astype(F32)
        ).astype(BF)
        return carry

    lax.fori_loop(0, (tokens - 2 * side) // (2 * side), inner_slope, 0)
    rim_wait(dz, dzh, 2)

    dhid = gp

    def fold(v):
        return jnp.sum(v.reshape(side // 8, 8, 128), axis=0)

    def back_tile(t, carry):
        lanes = pl.ds(pl.multiple_of(t * 128, 128), 128)
        taps = taps_of(lanes)

        def row(r, sums):
            around = [dz[rows((r + a) * side, side), lanes].astype(F32) for a in range(3)]
            parts = [
                taps[b] * around[2] + taps[3 + b] * around[1] + taps[6 + b] * around[0]
                for b in range(3)
            ]
            low = (
                parts[1]
                + maskr[...] * pltpu.roll(parts[0], side - 1, 0)
                + maskl[...] * pltpu.roll(parts[2], 1, 0)
            ).astype(BF)
            dhid[rows(r * side, side), lanes] = low
            here = around[1]
            moved = [
                maskr[...] * pltpu.roll(here, side - 1, 0),
                here,
                maskl[...] * pltpu.roll(here, 1, 0),
            ]
            found = []
            for a in range(3):
                source = hidp[rows((r + a) * side, side), lanes].astype(F32)
                for b in range(3):
                    found.append(fold(moved[b] * source))
            found.append(fold(low.astype(F32)))
            found.append(fold(here))
            return tuple(s + f for s, f in zip(sums, found))

        sums = lax.fori_loop(0, band, row, tuple(jnp.zeros((8, 128), F32) for _ in range(11)))
        hg[:, lanes] = jnp.concatenate(
            [colsum(s) for s in sums] + [jnp.zeros((5, 128), F32)], axis=0
        )
        return carry

    lax.fori_loop(0, FF // 128, back_tile, 0)

    for b in range(2):
        value = nn(bn_t[...], dhid[:, 640 * b : 640 * b + 640]).T.astype(BF)
        value = value.reshape(2, 4, 80, D)
        for i in range(n):
            sf[2 * b : 2 * b + 2, i, :, 4 * rb : 8 * rb] = jnp.concatenate(
                [value[:, v, :, rb * i : rb * i + rb] for v in range(4)], axis=2
            )

    def scatter(at, s, r1, r2, r3):
        core = [
            remote(s.at[slot], r1.at[t], rs_s.at[at, t], rs_r.at[at, t], me, j1)
            for t, slot in enumerate((j1, j3))
        ]
        over_x = remote(s.at[j2], r2, rs_s.at[at, 2], rs_r.at[at, 2], me, j2)

        def one():
            for copy in core:
                copy.start()

        def two():
            for copy in core:
                copy.wait_send()
                copy.wait_recv()

            def add(i, carry):
                s[j, i] = (s[j, i].astype(F32) + r1[0, i].astype(F32)).astype(BF)
                s[j2, i] = (s[j2, i].astype(F32) + r1[1, i].astype(F32)).astype(BF)
                return carry

            lax.fori_loop(0, n, add, 0)
            over_x.start()

        def dp_copy(k, peer):
            return remote(s.at[j, peer], r3.at[k], rd_s.at[at, k], rd_r.at[at, k], peer, j)

        def three():
            over_x.wait_send()
            over_x.wait_recv()

            def add(i, carry):
                s[j, i] = (s[j, i].astype(F32) + r2[i].astype(F32)).astype(BF)
                return carry

            lax.fori_loop(0, n, add, 0)
            peers(lambda k, peer, source: dp_copy(k, peer).start())

        def four():
            def land(k, peer, source):
                d = dp_copy(k, peer)
                d.wait_send()
                d.wait_recv()

            peers(land)
            return lax.fori_loop(
                1, n, lambda k, total: total + r3[k].astype(F32), s[j, me].astype(F32)
            )

        return one, two, three, four

    f_one, f_two, f_three, f_four = scatter(0, sf, rf1, rf2, rf3)
    f_one()

    zero_row = jnp.zeros((1, D), F32)

    dbr = bn
    dbr_t = dy_t

    def back_middle(c, carry):
        at = rows(c * QC, QC)
        value, in_gain, in_shift = norm_back(mid[at, :], gain(2), nn(dhid[at, :], w1t[...]))
        value = value + dy[at, :].astype(F32)
        mid[at, :] = value
        low = value.astype(BF)
        dbr[at, :] = low
        dbr_t[:, pl.ds(pl.multiple_of(c * QC, QC), QC)] = low.T
        spread = nt(wop[...], low)
        for h in range(HEADS):
            tile = spread[128 * h : 128 * h + 128, :] * rtot[h, c]
            tile_low = tile.astype(BF)
            qt[h, c] = tile_low
            datn[h, at, :] = tile_low.T
            delta[h, c] = colsum(
                tile_low[64:128, :].astype(F32)
                * att_t[c, HEAD * h : HEAD * h + HEAD, :].astype(F32)
            )
        return (carry[0] + in_gain, carry[1] + in_shift, carry[2] + colsum(low.astype(F32)))

    sums = lax.fori_loop(0, chunks, back_middle, (zero_row, zero_row, zero_row))
    vg[2:3, :] = sums[0]
    vg[9:10, :] = sums[1]
    vg[8:9, :] = sums[2]
    f_two()
    value = nn(dbr_t[...], att_n[...]).astype(BF)
    for i in range(n):
        sm[:, i, :, rb : 2 * rb] = value[:, rb * i : rb * i + rb].reshape(4, 80, rb)

    def dkv(h, slot):
        return act.at[rows(slot * keys, keys), 128 * h : 128 * h + 128]

    def dk_core(h):
        return [
            remote(dkv(h, slot), rk1.at[h, t], dk_s.at[h, t], dk_r.at[h, t], me, j1)
            for t, slot in enumerate((j1, j3))
        ]

    def dk_x(h):
        return remote(dkv(h, j2), rk2.at[h], dk_s.at[h, 2], dk_r.at[h, 2], me, j2)

    def dk_two(h):
        for copy in dk_core(h):
            copy.wait_send()
            copy.wait_recv()
        for t, slot in enumerate((j, j2)):
            part = dkv(h, slot)
            part[...] = (part[...].astype(F32) + rk1[h, t].astype(F32)).astype(BF)
        dk_x(h).start()

    def dk_three(h):
        over_x = dk_x(h)
        over_x.wait_send()
        over_x.wait_recv()
        qnat[h, 0:keys, :] = (dkv(h, j)[...].astype(F32) + rk2[h].astype(F32)).astype(BF)

    def back_head(h):
        gkv[...] = jnp.zeros(gkv.shape, F32)

        def chunk(c, inner):
            at = rows(c * QC, QC)
            tile = kv[h].reshape(4 * keys, 128)
            powers = prob[h, c]
            slopes = nn(tile, qt[h, c]) - delta[h, c]
            ds = (powers.astype(F32) * slopes).astype(BF)
            gkv[...] += nn(
                jnp.concatenate([ds, powers], axis=1),
                jnp.concatenate([qnat[h, at, :], datn[h, at, :]], axis=0),
            )
            dq_t[c, rows(h * HEAD, HEAD), :] = (
                nn(kvt[h, 0:64, :], ds) * HEAD**-0.5
            ).astype(BF)
            return inner

        lax.fori_loop(0, chunks, chunk, 0)
        act[0 : 4 * keys, 128 * h : 128 * h + 128] = gkv[...].astype(BF)
        for copy in dk_core(h):
            copy.start()

    for h in range(HEADS):
        back_head(h)
        if h >= 1:
            dk_two(h - 1)
        if h >= 2:
            dk_three(h - 2)
        if h == 1:
            f_three()

    dq = att_n

    def flip(c, total):
        low = dq_t[c].T
        dq[rows(c * QC, QC), :] = low
        return total + colsum(low.astype(F32))

    vg[4:5, :] = lax.fori_loop(0, chunks, flip, zero_row)
    dk_two(HEADS - 1)
    value = nn(dq_t[0], abf[0:QC, :])
    for c in range(1, chunks):
        value = value + nn(dq_t[c], abf[QC * c : QC * c + QC, :])
    value = value.astype(BF)
    for i in range(n):
        sm[:, i, :, 0:rb] = value[:, rb * i : rb * i + rb].reshape(4, 80, rb)
    m_one, m_two, m_three, m_four = scatter(1, sm, rm1, rm2, rm3)
    m_one()
    dk_three(HEADS - 2)
    dk_three(HEADS - 1)

    dm = jnp.concatenate([qnat[h, 0:keys, :] for h in range(HEADS)], axis=1)
    dm_sum = colsum(dm.astype(F32))
    vg[7:8, :] = jnp.concatenate(
        [dm_sum[:, 128 * h + 64 : 128 * h + 128] for h in range(HEADS)], axis=1
    )
    dv, in_gain, in_shift = norm_back(red_s[...], gain(1), nn(dm, wmt[...]))
    vg[1:2, :] = in_gain
    vg[6:7, :] = in_shift
    dred = dv.astype(BF)
    vg[5:6, :] = colsum(dred.astype(F32))
    dred_t = dred.T
    for dd in range(4):
        value = nn(dred_t, pat[dd]).astype(BF)
        count = n // 4
        for ii in range(count):
            st[:, dd * count + ii, :, 0 : 4 * rb] = value[
                :, 4 * rb * ii : 4 * rb * (ii + 1)
            ].reshape(4, 80, 4 * rb)
    value = nn(dm.T, memin[...]).astype(BF)
    value = jnp.concatenate(
        [value[128 * h : 128 * h + 64] for h in range(HEADS)]
        + [value[128 * h + 64 : 128 * h + 128] for h in range(HEADS)],
        axis=0,
    ).reshape(4, 2, 80, D)
    for i in range(n):
        st[:, i, :, 4 * rb : 6 * rb] = jnp.concatenate(
            [value[:, v, :, rb * i : rb * i + rb] for v in range(2)], axis=2
        )
    t_one, t_two, t_three, t_four = scatter(2, st, rt1, rt2, rt3)
    t_one()
    m_two()

    for dd in range(4):
        back = nn(dred, wrt[dd])
        back = jnp.concatenate([back, jnp.zeros((keys, 64), F32)], axis=1)
        for i in range(band // 2):
            start = (2 * i + dd // 2) * side + dd % 2
            for t in range(3):
                a3[t, pl.ds(start, half, stride=2), :] = back[
                    i * half : (i + 1) * half, 128 * t : 128 * t + 128
                ]
    t_two()

    def back_first(c, carry):
        at = rows(c * QC, QC)
        e = nn(dq[at, :], wqt[...]) + jnp.concatenate([a3[t, at, :] for t in range(3)], axis=1)[:, 0:D]
        value, in_gain, in_shift = norm_back(x_s[at, :].astype(F32), gain(0), e)
        bn[at, :] = (mid[at, :] + value).astype(BF)
        return (carry[0] + in_gain, carry[1] + in_shift)

    sums = lax.fori_loop(0, chunks, back_first, (zero_row, zero_row))
    token_out = pltpu.make_async_copy(bn, tgrad_ref, loc.at[12])
    token_out.start()
    vg[0:1, :] = sums[0]
    vg[3:4, :] = sums[1]
    for i in range(n):
        sv[i, :, 0 : 4 * rb] = hg[:, 4 * rb * i : 4 * rb * (i + 1)].astype(BF)
        sv[i, :, 4 * rb : 5 * rb] = vg[:, rb * i : rb * i + rb].astype(BF)

    v_core = remote(sv, rv1, rs_s.at[3, 0], rs_r.at[3, 0], me, j1)
    v_core.start()
    m_three()
    v_core.wait_send()
    v_core.wait_recv()
    sv[...] = (sv[...].astype(F32) + rv1[...].astype(F32)).astype(BF)
    v_x = remote(sv, rv2, rs_s.at[3, 1], rs_r.at[3, 1], me, j2)
    v_x.start()
    t_three()
    v_x.wait_send()
    v_x.wait_recv()
    sv[...] = (sv[...].astype(F32) + rv2[...].astype(F32)).astype(BF)

    def v_copy(k, peer):
        return remote(sv.at[peer], rv3.at[k], rd_s.at[3, k], rd_r.at[3, k], peer, j)

    peers(lambda k, peer, source: v_copy(k, peer).start())

    own_f = f_four()
    own_ref[0:80, tl + ml : tl + ml + own_f.shape[1]] = own_f
    squares = jnp.sum(own_f[:, 0 : 8 * rb] * own_f[:, 0 : 8 * rb])
    own_m = m_four()
    own_ref[0:80, tl : tl + ml] = own_m
    squares += jnp.sum(own_m[:, 0 : 2 * rb] * own_m[:, 0 : 2 * rb])

    def land_vec(k, peer, source):
        d = v_copy(k, peer)
        d.wait_send()
        d.wait_recv()

    peers(land_vec)
    own_v = lax.fori_loop(
        1, n, lambda k, total: total + rv3[k].astype(F32), sv[me].astype(F32)
    )
    own_ref[80:96, 0:vl] = own_v
    first_band = (j == 0).astype(jnp.int32).astype(F32)
    vec_squares = jnp.sum(own_v[0:11, 0 : 5 * rb] * own_v[0:11, 0 : 5 * rb])
    own_t = t_four()
    own_ref[0:80, 0:tl] = own_t
    squares += jnp.sum(own_t[:, 0 : 6 * rb] * own_t[:, 0 : 6 * rb])
    squares += first_band * vec_squares

    nrm[me] = jnp.full((8, 128), squares, F32)

    def send_norm(k, peer, source):
        remote(nrm.at[me], nrm.at[me], nd_s.at[k], nd_r.at[k], peer, j).start()

    def wait_norm(k, peer, source):
        d = remote(nrm.at[source], nrm.at[source], nd_s.at[k], nd_r.at[k], peer, j)
        d.wait_send()
        d.wait_recv()

    peers(send_norm)
    peers(wait_norm)
    nrs[j] = lax.fori_loop(1, n, lambda k, total: total + nrm[k], nrm[0])
    for t, other in enumerate((j1, j2, j3)):
        remote(nrs.at[j], nrs.at[j], ns_s.at[t], ns_r.at[t], me, other).start()
    for t, other in enumerate((j1, j2, j3)):
        d = remote(nrs.at[other], nrs.at[other], ns_s.at[t], ns_r.at[t], me, other)
        d.wait_send()
        d.wait_recv()
    own_ref[80:88, vl : vl + 128] = nrs[0] + nrs[1] + nrs[2] + nrs[3]

    peers(wait_out)
    own_out.wait()
    token_out.wait()


def update_kernel(rb, vl, tl, ml, rates, decays, own_ref, outt_ref, tg_ref, *refs):
    weights, firsts, seconds = refs[0:9], refs[9:18], refs[18:27]
    out_ref, tok_ref, norm_ref = refs[27:30]
    news = refs[30:57]
    sems = refs[57]
    copies = [
        pltpu.make_async_copy(outt_ref, out_ref, sems.at[0]),
        pltpu.make_async_copy(tg_ref, tok_ref, sems.at[1]),
    ]
    for copy in copies:
        copy.start()
    total = own_ref[80:81, vl : vl + 128]
    norm = jnp.sqrt(total)
    norm_ref[...] = norm
    clip = jnp.minimum(1.0, MAX_NORM / (norm + 1e-06))[:, 0:1]
    turned_t = own_ref[0:80, 0:tl].T
    turned_m = own_ref[0:80, tl : tl + ml].T
    turned_f = own_ref[0:80, tl + ml :].T
    grads = (
        turned_m[0:rb],
        turned_t[0 : 4 * rb],
        jnp.concatenate([turned_t[(4 + v) * rb : (5 + v) * rb] for v in range(2)], axis=1),
        turned_m[rb : 2 * rb],
        jnp.concatenate([turned_f[(4 + v) * rb : (5 + v) * rb] for v in range(4)], axis=1),
        turned_f[0 : 4 * rb],
        own_ref[80:83, 4 * rb : 5 * rb],
        own_ref[83:91, 4 * rb : 5 * rb],
        own_ref[80:91, 0 : 4 * rb],
    )
    for at in range(9):
        clipped = clip * grads[at]
        weight = weights[at][...]
        first = BETA_ONE * firsts[at][...] + (1.0 - BETA_ONE) * clipped
        second = BETA_TWO * seconds[at][...] + (1.0 - BETA_TWO) * clipped * clipped
        direction = (
            first
            / (1.0 - BETA_ONE**STEP)
            / (jnp.sqrt(second / (1.0 - BETA_TWO**STEP)) + ADAM_EPS)
        )
        news[at][...] = weight - rates[at] * (direction + decays[at] * weight)
        news[9 + at][...] = first
        news[18 + at][...] = second
    for copy in copies:
        copy.wait()


def on_device(n, *args):
    tokens, buckets, cotangent = args[0:3]
    weights, firsts, seconds = args[3:12], args[12:21], args[21:30]
    band, side, width = tokens.shape[1:4]
    count = band * side
    keys = count // 4
    rb = weights[0].shape[0]
    piece = cotangent.shape[3]
    chunks = count // QC
    wide = up(8 * rb, 128)
    tl = up(6 * rb, 128)
    ml = up(2 * rb, 128)
    vl = up(5 * rb, 128)
    total = tl + ml + wide
    turned = piece % 128 == 0
    block = (n, D, piece) if turned else (n, piece, D)
    vm = pltpu.VMEM
    dma = pltpu.SemaphoreType.DMA
    scratch = [
        vm((count, D), BF),
        *[vm(weights[at].shape, F32) for at in (0, 1, 2, 3, 4, 5, 6, 7, 8)],
        vm((n, 16, vl), BF),
        vm((4, n, 80, max(wide, tl + ml)), BF),
        vm((4, n, 80, wide), BF),
        vm((16, D), F32),
        vm((16, FF), F32),
        vm((D, D), BF),
        vm((2 * D, D), BF),
        vm((D, D), BF),
        vm((2 * D, D), BF),
        vm((2 * D, D), BF),
        vm((4, D, D), BF),
        vm((FF, D), BF),
        vm((D, FF), BF),
        vm((3, count, 128), F32),
        vm((count, D), BF),
        vm((4, keys, D), BF),
        vm((keys, D), F32),
        vm((keys, D), BF),
        vm((HEADS, 4, keys, 128), BF),
        vm((HEADS, 128, count), BF),
        vm((count, 128), BF),
        vm((chunks, 128, QC), BF),
        vm((HEADS, count, 128), BF),
        vm((HEADS, chunks, 128, QC), BF),
        vm((HEADS, chunks, count, QC), BF),
        vm((chunks, D, QC), BF),
        vm((count, D), BF),
        vm((HEADS, chunks, 1, QC), F32),
        vm((HEADS, chunks, 1, QC), F32),
        vm((count, D), F32),
        vm((count, D), BF),
        vm((D, count), BF),
        vm((count + 2 * side, FF), BF),
        vm((2, side, FF), BF),
        vm((count + 2 * side, FF), BF),
        vm((count, FF), BF),
        vm(block, BF),
        vm(block, BF),
        vm((D, count), BF),
        vm((count, D), BF),
        vm((2, side, FF), BF),
        vm((HEADS, count, 128), BF),
        vm((count, 128), F32),
        vm((HEADS, 2, keys, 128), BF),
        vm((HEADS, keys, 128), BF),
        vm((chunks, D, QC), BF),
        vm((16, FF), F32),
        vm((16, D), F32),
        vm((2, n, 80, wide), BF),
        vm((n, 80, wide), BF),
        vm((n, 80, wide), BF),
        vm((2, n, 80, tl), BF),
        vm((n, 80, tl), BF),
        vm((n, 80, tl), BF),
        vm((2, n, 80, ml), BF),
        vm((n, 80, ml), BF),
        vm((n, 80, ml), BF),
        vm((n, 16, vl), BF),
        vm((n, 16, vl), BF),
        vm((n, 16, vl), BF),
        vm((n, 16, vl), BF),
        vm((n, 8, 128), F32),
        vm((4, 8, 128), F32),
        vm((side, 128), F32),
        vm((side, 128), F32),
        dma((13,)),
        *[dma((n,)) for _ in range(6)],
        dma((2, 3)),
        dma((2, 3)),
        *[dma((n,)) for _ in range(4)],
        dma((HEADS, 3)),
        dma((HEADS, 3)),
        dma((4,)),
        dma((4,)),
        dma((HEADS, 3)),
        dma((HEADS, 3)),
        dma((4, 3)),
        dma((4, 3)),
        dma((4, n)),
        dma((4, n)),
        dma((n,)),
        dma((n,)),
        dma((3,)),
        dma((3,)),
    ]
    anywhere = pl.BlockSpec(memory_space=pl.ANY)
    in_vmem = pl.BlockSpec(memory_space=pltpu.VMEM)
    out_t, token_grad, own = pl.pallas_call(
        functools.partial(block_kernel, n, side, band),
        out_shape=(
            jax.ShapeDtypeStruct(block, BF),
            jax.ShapeDtypeStruct((count, D), BF),
            jax.ShapeDtypeStruct((96, total), F32),
        ),
        in_specs=[pl.BlockSpec(memory_space=pltpu.SMEM)] + [anywhere] * 11,
        out_specs=(anywhere, anywhere, in_vmem),
        scratch_shapes=scratch,
        compiler_params=pltpu.CompilerParams(
            collective_id=0, has_side_effects=True, vmem_limit_bytes=VMEM_LIMIT
        ),
    )(
        buckets,
        tokens.reshape(count, width),
        jnp.swapaxes(cotangent, 3, 4).reshape(block) if turned else cotangent.reshape(block),
        *weights,
    )
    rates = (
        D ** (-0.5),
        (4 * D) ** (-0.5),
        D ** (-0.5),
        OUT_FAN ** (-0.5),
        D ** (-0.5),
        FF ** (-0.5),
        GAIN_RATE,
        VECTOR_RATE,
        VECTOR_RATE,
    )
    decays = (DECAY_RATE,) * 6 + (0.0,) * 3
    shapes = tuple(jax.ShapeDtypeStruct(w.shape, F32) for w in weights)
    results = pl.pallas_call(
        functools.partial(update_kernel, rb, vl, tl, ml, rates, decays),
        out_shape=(
            jax.ShapeDtypeStruct(block, BF),
            jax.ShapeDtypeStruct((count, D), BF),
            jax.ShapeDtypeStruct((1, 128), F32),
        )
        + shapes * 3,
        in_specs=[in_vmem, anywhere, anywhere] + [in_vmem] * 27,
        out_specs=(anywhere, anywhere) + (in_vmem,) * 28,
        scratch_shapes=[dma((2,))],
    )(own, out_t, token_grad, *weights, *firsts, *seconds)
    if turned:
        block_output = jnp.swapaxes(results[0].reshape(n, 1, 1, width, piece), 3, 4)
    else:
        block_output = results[0].reshape(n, 1, 1, piece, width)
    return (
        block_output,
        results[1].reshape(1, band, side, width),
        results[2][0, 0],
        *results[3:],
    )


def solution(mesh):
    matrix = (P("dp", "seq"),) * 6 + (P(None, "dp"),) * 3
    return jax.shard_map(
        functools.partial(on_device, mesh.shape["dp"]),
        mesh=mesh,
        in_specs=(
            P("dp", "seq", None, None),
            P("dp"),
            P(None, "seq", "dp", None, None),
            *(matrix * 3),
        ),
        out_specs=(
            P(None, "seq", "dp", None, None),
            P("dp", "seq", None, None),
            P(),
            *(matrix * 3),
        ),
        check_vma=False,
    )
```

time: 1080 us -> 220 us (0.20)
  waiting for transfers between devices: 434 us -> 0 us
  blocking collectives: 355 us -> 0 us
  Pallas kernels: 0 us -> 218 us
  other arithmetic: 84.2 us -> 0 us
  matrix products: 84 us -> 0 us
  local copies, waits for them, and re-layouts: 71.5 us -> 0 us
  between operations: 25.7 us -> 1.48 us
  starting transfers between devices: 20.2 us -> 0 us
    all_gather x15 -> x0, blocking collectives: 305 us -> none  [the longest x1 35.3 us: on_device(): lax.all_gather(column_parts[5], 'dp', axis=0, tiled=True)]
    unnamed x20 -> x0, waiting for transfers between devices: 304 us -> none
    pallas_call x0 -> x2, Pallas kernels: none -> 218 us  [the longest x1 171 us: on_device(): pl.pallas_call(functools.partial(block_kernel, n, side, band), out_shape=...]
    reduce_scatter x7 -> x0, waiting for transfers between devices: 127 us -> none  [the longest x1 54.1 us: on_device(): lax.psum_scatter(column_sums[2].astype(jnp.bfloat16), 'dp', scatter_dimen...]
    dot_general x48 -> x0, matrix products: 84 us -> none  [the longest x5 13.4 us: on_device(): jnp.einsum('qk,qe->ke', probs_low, out_slope, preferred_element_type=jnp....]
    psum x2 -> x0, blocking collectives: 50.2 us -> none  [the longest x1 40.1 us: on_device(): lax.psum(matrix_squares + first_band * vector_squares, ('dp', 'seq'))]
    unnamed x364 -> x0, local copies, waits for them, and re-layouts: 40 us -> none
    reduce_sum x29 -> x0, other arithmetic: 34.9 us -> none  [the longest x1 12.8 us: on_device(): grad_expand_shift = jnp.sum(hidden_slope_low.astype(jnp.float32), axis=0)]
  transfers between devices with their start and end apart: 20 -> 0, of which waited for: 13 -> 0; matrix products, arithmetic and copies ran while one was open for 14% -> 0% of each run, Pallas kernels for 0% -> 0%
where the time goes in v1:
time: 220 us; the launch traced here: 219 us
  Pallas kernels  218 us (99%)
    pallas_call x1, Pallas kernels, on_device(): pl.pallas_call(functools.partial(block_kernel, n, side, band), out_shape=...  171 us
    pallas_call x1, Pallas kernels, on_device(): pl.pallas_call(functools.partial(update_kernel, rb, vl, tl, ml, rates, de...  47.3 us

profile of v1, /device:TPU:0, one launch (start us, length us, event | category | flops | bytes accessed | tf_op | source)
XLA Modules:
  0.0 219.4 jit_solution(18159752986885027493)
XLA Ops:
  1.3 170.6 %shard_map.517 = (bf16[8,320,128]{2,1,0:T(8,128)(2,1)}, bf16[1024,320]{1,0:T(8,128)(2,1)}, f32[96,768]{1,0:T(8,128)}) custom-call(s32[1]{0:T(128)S(6)} %copy.62.bucket_ref, bf16[1024,320]{1,0:T(8,128)(2,1)} %bitcast.14, bf16[8,320,128]{2,1,0:T(8,128)(2,1)} %bitcast.15, f32[40,80]{1,0:T(8,128)} %refs_0_.1, f32[160,80]{1,0:T(8,128)} %refs_1_.1, ...), custom_call_target="tpu_custom_call" | custom-call | tf_op jit(solution)/shard_map/pallas_call | solution.py:1199
  171.9 47.3 %shard_map.518 = (bf16[8,320,128]{2,1,0:T(8,128)(2,1)}, bf16[1024,320]{1,0:T(8,128)(2,1)}, f32[1,128]{1,0:T(1,128)}, f32[40,80]{1,0:T(8,128)}, f32[160,80]{1,0:T...) custom-call(f32[96,768]{1,0:T(8,128)} %get-tuple-element.63.own_ref,, ...), custom_call_target="tpu_custom_call" | custom-call | tf_op jit(solution)/shard_map/pallas_call | solution.py:1231

commit v2 on v1

v2 whole, which is shorter than its diff:
```python
import functools

import jax
import jax.numpy as jnp
from jax import lax
from jax.experimental import pallas as pl
from jax.experimental.pallas import tpu as pltpu
from jax.sharding import PartitionSpec as P

D = 320
HEADS = 5
HEAD = 64
FF = 1280
STEP = 10
OUT_FAN = 5

NORM_EPS = 1e-06
MAX_NORM = 1.0
BETA_ONE = 0.9
BETA_TWO = 0.95
ADAM_EPS = 1e-08
DECAY_RATE = 0.01
VECTOR_RATE = 0.3
GAIN_RATE = 0.8
MASKED = -1e30

BF = jnp.bfloat16
F32 = jnp.float32
MESH = pl.DeviceIdType.MESH
QC = 256
CUT = 48
VMEM_LIMIT = 63 * 1024 * 1024


def nn(a, b):
    return lax.dot_general(a, b, (((1,), (0,)), ((), ())), preferred_element_type=F32)


def nt(a, b):
    return lax.dot_general(a, b, (((1,), (1,)), ((), ())), preferred_element_type=F32)


def up(n, m):
    return (n + m - 1) // m * m


def norm_parts(v):
    centered = v - jnp.mean(v, axis=-1, keepdims=True)
    rstd = lax.rsqrt(jnp.mean(centered * centered, axis=-1, keepdims=True) + NORM_EPS)
    return centered * rstd, rstd


def norm_back(v, gain, e):
    vhat, rstd = norm_parts(v)
    u = e * gain
    dv = rstd * (
        u
        - jnp.mean(u, axis=-1, keepdims=True)
        - vhat * jnp.mean(u * vhat, axis=-1, keepdims=True)
    )
    return dv, jnp.sum(e * vhat, axis=0, keepdims=True), jnp.sum(e, axis=0, keepdims=True)


def colsum(v):
    return jnp.sum(v, axis=0, keepdims=True)


def rows(start, size):
    return pl.ds(pl.multiple_of(start, 16), size)


def block_kernel(
    n,
    side,
    band,
    qa,
    bucket_ref,
    tok_ref,
    cot_ref,
    wq_ref,
    wr_ref,
    wm_ref,
    wo_ref,
    w1_ref,
    w2_ref,
    gains_ref,
    biases_ref,
    hidden_ref,
    out_ref,
    tgrad_ref,
    own_ref,
    x_s,
    fq,
    fr,
    fm,
    fo,
    f1,
    f2,
    fg,
    fb,
    fh,
    gvec,
    gt,
    gm,
    gf,
    vp,
    hp,
    wqt,
    wqp,
    wot,
    wop,
    wmt,
    wrt,
    w1t,
    w2t,
    a3,
    abf,
    pat,
    red_s,
    memin,
    kv,
    kvt,
    kmask,
    qmask,
    qnat,
    qt,
    prob,
    att_t,
    att_n,
    rtot,
    delta,
    mid,
    bn,
    bn_t,
    hidp,
    hidh,
    act,
    gp,
    out_t,
    dy_in,
    dy_t,
    dy,
    dzh,
    datn,
    rk1,
    rk2,
    dq_t,
    hg,
    vg,
    rf1,
    rf4,
    rf5,
    rt1,
    rt2,
    rt3,
    rt4,
    rt5,
    rm1,
    rm2,
    rm3,
    sv,
    rv1,
    rv2,
    rv3,
    nrm,
    nrs,
    maskl,
    maskr,
    loc,
    vg_s,
    vg_r,
    gd_s,
    gd_r,
    gx_s,
    gx_r,
    co_s,
    co_r,
    ou_s,
    ou_r,
    kv_s,
    kv_r,
    ha_s,
    ha_r,
    dk_s,
    dk_r,
    rs_s,
    rs_r,
    rd_s,
    rd_r,
    nd_s,
    nd_r,
    ns_s,
    ns_r,
):
    me = lax.axis_index("dp")
    j = lax.axis_index("seq")
    j1 = j + 1 - 2 * lax.rem(j, 2)
    j2 = lax.rem(j + 2, 4)
    j3 = 3 - j
    tokens = band * side
    chunks = tokens // QC
    rb = wq_ref.shape[0]
    piece = tokens // n
    keys = kv.shape[2]
    turned = cot_ref.shape[1] == D
    tl = gt.shape[3]
    fl = gf.shape[3]
    vl = gvec.shape[2]

    def remote(src, dst, ss, rs, dp, seq):
        return pltpu.make_async_remote_copy(
            src_ref=src,
            dst_ref=dst,
            send_sem=ss,
            recv_sem=rs,
            device_id=(dp, seq),
            device_id_type=MESH,
        )

    def both(copy):
        copy.wait_send()
        copy.wait_recv()

    def peers(body):
        def step(k, carry):
            body(k, lax.rem(me + k, n), lax.rem(me + n - k, n))
            return carry

        lax.fori_loop(1, n, step, 0)

    loads = [
        pltpu.make_async_copy(src, dst, loc.at[at])
        for at, (src, dst) in enumerate(
            (
                (gains_ref, fg),
                (biases_ref, fb),
                (hidden_ref, fh),
                (wr_ref, fr),
                (wm_ref, fm),
                (wq_ref, fq),
                (wo_ref, fo),
                (w1_ref, f1),
                (w2_ref, f2),
                (tok_ref, x_s),
            )
        )
    ]
    for copy in loads:
        copy.start()
    own_cot = pltpu.make_async_copy(cot_ref.at[me], dy_in.at[me], loc.at[10])
    own_cot.start()

    barrier = pltpu.get_barrier_semaphore()

    def greet(k, peer, source):
        pl.semaphore_signal(barrier, inc=1, device_id=(peer, j), device_id_type=MESH)

    peers(greet)
    for other in (j1, j2, j3):
        pl.semaphore_signal(barrier, inc=1, device_id=(me, other), device_id_type=MESH)

    for copy in loads[:5]:
        copy.wait()
    hidden16 = jnp.concatenate([fh[...], jnp.zeros((5, 4 * rb), F32)], axis=0)
    small16 = jnp.concatenate([fg[...], fb[...], jnp.zeros((5, rb), F32)], axis=0)
    gvec[me] = jnp.concatenate(
        [hidden16, small16, jnp.zeros((16, vl - 5 * rb), F32)], axis=1
    ).astype(BF)
    wm_t = fm[...].T
    gt[j, me] = jnp.concatenate(
        [fr[...].T, wm_t[0:80], wm_t[80:160], jnp.zeros((80, tl - 6 * rb), F32)], axis=1
    ).astype(BF)

    def send_vec(k, peer, source):
        remote(gvec.at[me], gvec.at[me], vg_s.at[k], vg_r.at[k], peer, j).start()

    def wait_vec(k, peer, source):
        both(remote(gvec.at[source], gvec.at[source], vg_s.at[k], vg_r.at[k], peer, j))

    def to_peers(at, piece_of, slot):
        def start():
            def body(k, peer, source):
                remote(
                    piece_of(slot, me), piece_of(slot, me), gd_s.at[at, k], gd_r.at[at, k], peer, j
                ).start()

            peers(body)

        def wait():
            def body(k, peer, source):
                ref = piece_of(slot, source)
                both(remote(ref, ref, gd_s.at[at, k], gd_r.at[at, k], peer, j))

            peers(body)

        return start, wait

    def swap(at, t, mine, theirs, other):
        def start():
            remote(mine, mine, gx_s.at[at, t], gx_r.at[at, t], me, other).start()

        def wait():
            remote(mine, mine, gx_s.at[at, t], gx_r.at[at, t], me, other).wait_send()
            remote(theirs, theirs, gx_s.at[at, t], gx_r.at[at, t], me, other).wait_recv()

        return start, wait

    def t_low(slot, i):
        return gt.at[slot, i, 0:CUT]

    def t_high(slot, i):
        return gt.at[slot, i, CUT:80]

    def whole_m(slot, i):
        return gm.at[slot, i]

    def whole_f(slot, i):
        return gf.at[slot, i]

    t_dp, t_dp_wait = to_peers(0, t_low, j)
    t_dpa, t_dpa_wait = to_peers(1, t_high, j)
    t_dpb, t_dpb_wait = to_peers(2, t_high, j2)
    m_dp, m_dp_wait = to_peers(3, whole_m, j)
    f_dpa, f_dpa_wait = to_peers(4, whole_f, j)
    f_dpb, f_dpb_wait = to_peers(5, whole_f, j2)
    t_x, t_x_wait = swap(0, 0, gt.at[j, :, 0:CUT], gt.at[j2, :, 0:CUT], j2)
    t_x0, t_x0_wait = swap(0, 1, t_high(j, me), t_high(j2, me), j2)
    t_ca, t_ca_wait = swap(0, 2, gt.at[j], gt.at[j1], j1)
    t_cb, t_cb_wait = swap(0, 3, gt.at[j2], gt.at[j3], j1)
    m_x, m_x_wait = swap(1, 0, gm.at[j], gm.at[j2], j2)
    m_ca, m_ca_wait = swap(1, 2, gm.at[j], gm.at[j1], j1)
    m_cb, m_cb_wait = swap(1, 3, gm.at[j2], gm.at[j3], j1)
    f_x0, f_x0_wait = swap(2, 1, gf.at[j, me], gf.at[j2, me], j2)
    f_ca, f_ca_wait = swap(2, 2, gf.at[j], gf.at[j1], j1)
    f_cb, f_cb_wait = swap(2, 3, gf.at[j2], gf.at[j3], j1)

    pl.semaphore_wait(barrier, n - 1 + 3)
    t_x0()
    peers(send_vec)
    t_dp()

    for copy in loads[5:9]:
        copy.wait()
    wq_t = fq[...].T
    gm[j, me] = jnp.concatenate(
        [
            wq_t[0:32],
            wq_t[32:64],
            jnp.concatenate([wq_t[64:80], jnp.zeros((16, rb), F32)], axis=0),
            jnp.zeros((32, 128 - 3 * rb), F32),
        ],
        axis=1,
    ).astype(BF)
    w1_t = f1[...].T
    gf[j, me] = jnp.concatenate(
        [f2[...].T]
        + [w1_t[80 * v : 80 * v + 80] for v in range(4)]
        + [fo[...].T, jnp.zeros((80, fl - 9 * rb), F32)],
        axis=1,
    ).astype(BF)
    f_x0()
    t_x0_wait()
    t_dpa()
    t_dpb()
    m_dp()

    peers(wait_vec)
    hp[...] = jnp.concatenate([gvec[i, :, 0 : 4 * rb] for i in range(n)], axis=1).astype(F32)
    vp[...] = jnp.concatenate(
        [gvec[i, :, 4 * rb : 5 * rb] for i in range(n)], axis=1
    ).astype(F32)

    def gain(k):
        return vp[k : k + 1, :]

    def shift(k):
        return vp[3 + k : 4 + k, :]

    loads[9].wait()

    def norm_one(c, carry):
        at = rows(c * QC, QC)
        vhat, _ = norm_parts(x_s[at, :].astype(F32))
        low = (vhat * gain(0) + shift(0)).astype(BF)
        abf[at, :] = low
        wide = jnp.concatenate([low.astype(F32), jnp.zeros((QC, 64), F32)], axis=1)
        for t in range(3):
            a3[t, at, :] = wide[:, 128 * t : 128 * t + 128]
        return carry

    lax.fori_loop(0, chunks, norm_one, 0)
    half = side // 2
    for dd in range(4):
        for i in range(band // 2):
            start = (2 * i + dd // 2) * side + dd % 2
            cut = jnp.concatenate(
                [a3[t, pl.ds(start, half, stride=2), :] for t in range(3)], axis=1
            )
            pat[dd, i * half : (i + 1) * half, :] = cut[:, 0:D].astype(BF)

    bucket = bucket_ref[0]
    k_row = lax.broadcasted_iota(jnp.int32, (4 * keys, 128), 0)
    k_lane = lax.broadcasted_iota(jnp.int32, (4 * keys, 128), 1)
    k_id = (lax.div(k_row, half) >= half // 2).astype(jnp.int32) * 2 + (
        lax.rem(k_row, half) >= half // 2
    ).astype(jnp.int32)
    off = (k_id != k_lane).astype(jnp.int32) * bucket * (k_lane < 4).astype(jnp.int32)
    kmask[...] = (off.astype(F32) * MASKED).astype(BF)
    q_row = lax.broadcasted_iota(jnp.int32, (128, tokens), 0)
    place = lax.broadcasted_iota(jnp.int32, (128, tokens), 1)
    q_id = (lax.div(place, side) + j * band >= half).astype(jnp.int32) * 2 + (
        lax.rem(place, side) >= half
    ).astype(jnp.int32)
    qmask[...] = (q_id == q_row).astype(F32).astype(BF)
    col = lax.broadcasted_iota(jnp.int32, (side, 128), 0)
    maskl[...] = (
        (col > 0).astype(jnp.int32) * (1 - bucket * (col == half).astype(jnp.int32))
    ).astype(F32)
    maskr[...] = (
        (col < side - 1).astype(jnp.int32) * (1 - bucket * (col == half - 1).astype(jnp.int32))
    ).astype(F32)
    top_ok = (
        (j > 0).astype(jnp.int32) * (1 - bucket * (j * band == half).astype(jnp.int32))
    ).astype(F32)
    low_ok = (
        (j < 3).astype(jnp.int32) * (1 - bucket * ((j + 1) * band == half).astype(jnp.int32))
    ).astype(F32)

    t_dp_wait()
    t_x()
    t_dpa_wait()
    t_dpb_wait()
    m_dp_wait()
    m_x()
    f_x0_wait()
    f_dpa()
    f_dpb()
    t_x_wait()
    t_ca()
    t_cb()
    m_x_wait()
    m_ca()
    m_cb()
    t_ca_wait()
    t_cb_wait()

    for s in range(4):
        span = slice(80 * s, 80 * s + 80)

        def lanes(lo, hi, over):
            return jnp.concatenate([gt[s, i, :, lo:hi] for i in over], axis=1)

        for dd in range(4):
            wrt[dd, span, :] = lanes(0, 4 * rb, range(dd * n // 4, (dd + 1) * n // 4))
        for v in range(2):
            wop[160 * s + 80 * v : 160 * s + 80 * v + 80, :] = lanes(
                (4 + v) * rb, (5 + v) * rb, range(n)
            )
    for h in range(HEADS):
        wmt[128 * h : 128 * h + 64, :] = wop[HEAD * h : HEAD * h + HEAD, :]
        wmt[128 * h + 64 : 128 * h + 128, :] = wop[D + HEAD * h : D + HEAD * h + HEAD, :]

    red = shift(2) + nt(pat[0], wrt[0])
    for dd in range(1, 4):
        red = red + nt(pat[dd], wrt[dd])
    red_s[...] = red
    vhat, _ = norm_parts(red)
    low = (vhat * gain(1) + shift(3)).astype(BF)
    memin[...] = low
    zero64 = jnp.zeros((1, HEAD), F32)
    value_shift = jnp.concatenate(
        [
            part
            for h in range(HEADS)
            for part in (zero64, shift(4)[:, HEAD * h : HEAD * h + HEAD])
        ],
        axis=1,
    )
    memory = (nt(low, wmt[...]) + value_shift).astype(BF)
    for h in range(HEADS):
        kv[h, j] = memory[:, 128 * h : 128 * h + 128]

    def kv_copy(h, slot, t, other):
        return remote(
            kv.at[h, slot], kv.at[h, slot], kv_s.at[h, t], kv_r.at[h, t], me, other
        )

    def kv_send(h, carry):
        kv_copy(h, j, 0, j2).start()
        kv_copy(h, j, 1, j1).start()
        return carry

    lax.fori_loop(0, HEADS, kv_send, 0)

    m_ca_wait()
    m_cb_wait()
    for s in range(4):
        at = 80 * s
        wqt[at : at + 32, :] = jnp.concatenate([gm[s, i, :, 0:rb] for i in range(n)], axis=1)
        wqt[at + 32 : at + 64, :] = jnp.concatenate(
            [gm[s, i, :, rb : 2 * rb] for i in range(n)], axis=1
        )
        wqt[at + 64 : at + 80, :] = jnp.concatenate(
            [gm[s, i, 0:16, 2 * rb : 3 * rb] for i in range(n)], axis=1
        )
    for h in range(HEADS):
        wqp[128 * h : 128 * h + 64, :] = wqt[HEAD * h : HEAD * h + HEAD, :]
        wqp[128 * h + 64 : 128 * h + 128, :] = jnp.zeros((64, D), BF)

    query_shift = jnp.concatenate(
        [
            part
            for h in range(HEADS)
            for part in (shift(1)[:, HEAD * h : HEAD * h + HEAD], zero64)
        ],
        axis=1,
    )

    def across(c):
        return pl.ds(pl.multiple_of(c * QC, QC), QC)

    def queries(c, carry):
        at = rows(c * QC, QC)
        q = (nt(abf[at, :], wqp[...]) + query_shift).astype(BF) * jnp.asarray(HEAD**-0.5, BF)
        for h in range(HEADS):
            tile = q[:, 128 * h : 128 * h + 128]
            qnat[h, at, :] = tile
            qt[h, :, across(c)] = tile.T
        return carry

    lax.fori_loop(0, chunks, queries, 0)

    def send_cot(k, peer, source):
        remote(cot_ref.at[peer], dy_in.at[me], co_s.at[k], co_r.at[k], peer, j).start()

    def wait_cot(k, peer, source):
        both(remote(cot_ref.at[peer], dy_in.at[source], co_s.at[k], co_r.at[k], peer, j))

    def kv_forward(h):
        kv_copy(h, j2, 0, j2).wait_recv()
        kv_copy(h, j2, 2, j1).start()

    kv_forward(0)

    def attend(h, carry):
        @pl.when(h < HEADS - 1)
        def _():
            kv_forward(h + 1)

        @pl.when(h == HEADS - 1)
        def _():
            f_dpa_wait()
            f_dpb_wait()
            f_ca()
            f_cb()
            peers(send_cot)

        kv_copy(h, j, 0, j2).wait_send()
        kv_copy(h, j, 1, j1).wait_send()
        kv_copy(h, j2, 2, j1).wait_send()
        kv_copy(h, j1, 1, j1).wait_recv()
        kv_copy(h, j3, 2, j1).wait_recv()
        tile = kv[h].reshape(4 * keys, 128)
        kvt[h] = tile.T
        left = jnp.concatenate([tile, kmask[...]], axis=1)
        values = jnp.concatenate([kvt[h, 64:128, :], jnp.ones((16, 4 * keys), BF)], axis=0)
        for c in range(tokens // qa):
            cut = slice(c * qa, (c + 1) * qa)
            scores = nn(left, jnp.concatenate([qt[h, :, cut], qmask[:, cut]], axis=0))
            largest = jnp.max(scores, axis=0, keepdims=True)
            powers = jnp.exp(scores - largest).astype(BF)
            prob[h, :, cut] = powers
            got = nn(values, powers)
            scale = 1.0 / got[64:65, :]
            rtot[h, :, cut] = scale
            att_t[rows(h * HEAD, HEAD), cut] = (got[0:64, :] * scale).astype(BF)
        return carry

    lax.fori_loop(0, HEADS, attend, 0)

    f_ca_wait()
    f_cb_wait()
    for s in range(4):
        span = slice(80 * s, 80 * s + 80)
        w2t[span, :] = jnp.concatenate([gf[s, i, :, 0 : 4 * rb] for i in range(n)], axis=1)
        for v in range(4):
            at = 320 * s + 80 * v
            w1t[at : at + 80, :] = jnp.concatenate(
                [gf[s, i, :, (4 + v) * rb : (5 + v) * rb] for i in range(n)], axis=1
            )
        wot[span, :] = jnp.concatenate(
            [gf[s, i, :, 8 * rb : 9 * rb] for i in range(n)], axis=1
        )
    wop_full = wot[...].T
    for h in range(HEADS):
        wop[128 * h : 128 * h + 64, :] = jnp.zeros((64, D), BF)
        wop[128 * h + 64 : 128 * h + 128, :] = wop_full[HEAD * h : HEAD * h + HEAD, :]

    def middle(c, carry):
        at = rows(c * QC, QC)
        att = att_t[:, across(c)].T
        att_n[at, :] = att
        value = x_s[at, :].astype(F32) + nt(att, wot[...]) + shift(5)
        mid[at, :] = value
        vhat, _ = norm_parts(value)
        low = (vhat * gain(2) + shift(6)).astype(BF)
        bn[at, :] = low
        bn_t[:, across(c)] = low.T
        return carry

    lax.fori_loop(0, chunks, middle, 0)

    edge = tokens - side

    def hidden_of(value):
        return (nt(value, w1t[...]) + hp[9:10, :]).astype(BF)

    ends = hidden_of(jnp.concatenate([bn[0:side, :], bn[edge:tokens, :]], axis=0))
    hidp[side : 2 * side, :] = ends[0:side]
    hidp[tokens : tokens + side, :] = ends[side : 2 * side]
    above = lax.rem(j + 3, 4)
    below = lax.rem(j + 1, 4)

    def rim(buf, halo, at):
        return (
            remote(buf.at[pl.ds(side, side)], halo.at[1], ha_s.at[at], ha_r.at[at], me, above),
            remote(
                buf.at[pl.ds(tokens, side)], halo.at[0], ha_s.at[at + 1], ha_r.at[at + 1], me, below
            ),
        )

    def rim_send(buf, halo, at):
        for copy in rim(buf, halo, at):
            copy.start()

    def rim_wait(buf, halo, at):
        for copy in rim(buf, halo, at):
            both(copy)
        buf[0:side, :] = (halo[0].astype(F32) * top_ok).astype(BF)
        buf[tokens + side : tokens + 2 * side, :] = (halo[1].astype(F32) * low_ok).astype(BF)

    rim_send(hidp, hidh, 0)

    def inner_hidden(c, carry):
        start = side + c * 2 * side
        hidp[rows(start + side, 2 * side), :] = hidden_of(bn[rows(start, 2 * side), :])
        return carry

    lax.fori_loop(0, (tokens - 2 * side) // (2 * side), inner_hidden, 0)

    def tile_at(t):
        return pl.ds(pl.multiple_of(t * 128, 128), 128)

    def taps_of(lanes):
        return [hp[k : k + 1, lanes] for k in range(9)]

    def conv_over(lo, hi, step):
        def conv_tile(t, carry):
            lanes = tile_at(t)
            taps = taps_of(lanes)
            base = hp[10:11, lanes]

            def row(at, inner):
                r = lo + at * step
                around = [hidp[rows((r + a) * side, side), lanes].astype(F32) for a in range(3)]
                parts = [
                    taps[b] * around[0] + taps[3 + b] * around[1] + taps[6 + b] * around[2]
                    for b in range(3)
                ]
                z = (
                    base
                    + parts[1]
                    + maskl[...] * pltpu.roll(parts[0], 1, 0)
                    + maskr[...] * pltpu.roll(parts[2], side - 1, 0)
                )
                cdf = 0.5 + 0.5 * lax.erf(z * (0.5**0.5))
                pdf = jnp.exp(z * z * -0.5) * 0.3989422804014327
                act[rows((r + 1) * side, side), lanes] = (z * cdf).astype(BF)
                gp[rows(r * side, side), lanes] = (cdf + z * pdf).astype(BF)
                return inner

            lax.fori_loop(0, (hi - lo) // step, row, 0)
            return carry

        lax.fori_loop(0, FF // 128, conv_tile, 0)

    conv_over(1, band - 1, 1)
    rim_wait(hidp, hidh, 0)
    conv_over(0, 2 * (band - 1), band - 1)

    def out_chunk(c, carry):
        at = rows(c * QC, QC)
        value = mid[at, :] + nt(act[rows(side + c * QC, QC), :], w2t[...]) + shift(7)
        for p in range(QC // piece):
            part = value[p * piece : (p + 1) * piece, :]
            out_t[c * (QC // piece) + p] = (part.T if turned else part).astype(BF)
        return carry

    lax.fori_loop(0, chunks, out_chunk, 0)

    def send_out(k, peer, source):
        remote(out_t.at[peer], out_ref.at[me], ou_s.at[k], ou_r.at[k], peer, j).start()

    def wait_out(k, peer, source):
        both(remote(out_t.at[peer], out_ref.at[source], ou_s.at[k], ou_r.at[k], peer, j))

    peers(send_out)
    own_out = pltpu.make_async_copy(out_t.at[me], out_ref.at[me], loc.at[11])
    own_out.start()

    own_cot.wait()
    peers(wait_cot)
    for i in range(n):
        if turned:
            dy_t[:, i * piece : (i + 1) * piece] = dy_in[i]
            dy[i * piece : (i + 1) * piece, :] = dy_in[i].T
        else:
            dy[i * piece : (i + 1) * piece, :] = dy_in[i]
    if not turned:
        dy_t[...] = dy[...].T
    vg[...] = jnp.zeros(vg.shape, F32)
    vg[10:11, :] = colsum(dy[...].astype(F32))

    per = 640 // (4 * rb)
    for b in range(2):
        value = nn(dy_t[...], act[side : side + tokens, 640 * b : 640 * b + 640]).astype(BF)
        for ii in range(per):
            gf[:, b * per + ii, :, 0 : 4 * rb] = value[:, 4 * rb * ii : 4 * rb * (ii + 1)].reshape(
                4, 80, 4 * rb
            )

    def slope_of(at):
        return nn(dy[at, :], w2t[...])

    dz = act
    for at in (0, edge):
        dz[side + at : 2 * side + at, :] = (
            slope_of(slice(at, at + side)) * gp[at : at + side, :].astype(F32)
        ).astype(BF)
    rim_send(dz, dzh, 2)

    def inner_slope(c, carry):
        at = rows(side + c * 2 * side, 2 * side)
        dz[rows(2 * side + c * 2 * side, 2 * side), :] = (
            slope_of(at) * gp[at, :].astype(F32)
        ).astype(BF)
        return carry

    lax.fori_loop(0, (tokens - 2 * side) // (2 * side), inner_slope, 0)

    dhid = gp

    def fold(v):
        return jnp.sum(v.reshape(side // 8, 8, 128), axis=0)

    def back_over(lo, hi, step, first):
        def back_tile(t, carry):
            lanes = tile_at(t)
            taps = taps_of(lanes)

            def row(at, sums):
                r = lo + at * step
                around = [dz[rows((r + a) * side, side), lanes].astype(F32) for a in range(3)]
                parts = [
                    taps[b] * around[2] + taps[3 + b] * around[1] + taps[6 + b] * around[0]
                    for b in range(3)
                ]
                low = (
                    parts[1]
                    + maskr[...] * pltpu.roll(parts[0], side - 1, 0)
                    + maskl[...] * pltpu.roll(parts[2], 1, 0)
                ).astype(BF)
                dhid[rows(r * side, side), lanes] = low
                here = around[1]
                moved = [
                    maskr[...] * pltpu.roll(here, side - 1, 0),
                    here,
                    maskl[...] * pltpu.roll(here, 1, 0),
                ]
                found = []
                for a in range(3):
                    source = hidp[rows((r + a) * side, side), lanes].astype(F32)
                    for b in range(3):
                        found.append(fold(moved[b] * source))
                found.append(fold(low.astype(F32)))
                found.append(fold(here))
                return tuple(s + f for s, f in zip(sums, found))

            sums = lax.fori_loop(
                0, (hi - lo) // step, row, tuple(jnp.zeros((8, 128), F32) for _ in range(11))
            )
            found = jnp.concatenate([colsum(s) for s in sums] + [jnp.zeros((5, 128), F32)], axis=0)
            hg[:, lanes] = found if first else hg[:, lanes] + found
            return carry

        lax.fori_loop(0, FF // 128, back_tile, 0)

    back_over(1, band - 1, 1, True)
    rim_wait(dz, dzh, 2)
    back_over(0, 2 * (band - 1), band - 1, False)

    for b in range(2):
        value = nn(bn_t[...], dhid[:, 640 * b : 640 * b + 640]).T.astype(BF)
        value = value.reshape(2, 4, 80, D)
        for i in range(n):
            gf[2 * b : 2 * b + 2, i, :, 4 * rb : 8 * rb] = jnp.concatenate(
                [value[:, v, :, rb * i : rb * i + rb] for v in range(4)], axis=2
            )

    def scatter(at, s, cut, r1, r2, r3, r4, r5, own):
        high = s.shape[2]

        def core():
            return [
                remote(s.at[slot], r1.at[t], rs_s.at[at, t], rs_r.at[at, t], me, j1)
                for t, slot in enumerate((j1, j3))
            ]

        def over_x():
            return remote(
                s.at[j2, :, 0:cut], r2, rs_s.at[at, 2], rs_r.at[at, 2], me, j2
            )

        def high_x():
            return remote(
                s.at[j2, me, cut:high], r5, rs_s.at[at, 3], rs_r.at[at, 3], me, j2
            )

        def low_dp(k, peer):
            return remote(
                s.at[j, peer, 0:cut], r3.at[k], rd_s.at[3 * at, k], rd_r.at[3 * at, k], peer, j
            )

        def high_dp(k, peer, t, slot):
            return remote(
                s.at[slot, peer, cut:high],
                r4.at[t, k],
                rd_s.at[3 * at + 1 + t, k],
                rd_r.at[3 * at + 1 + t, k],
                peer,
                j,
            )

        def one():
            for copy in core():
                copy.start()

        def two():
            for copy in core():
                both(copy)

            def add(i, carry):
                s[j, i] = (s[j, i].astype(F32) + r1[0, i].astype(F32)).astype(BF)
                s[j2, i] = (s[j2, i].astype(F32) + r1[1, i].astype(F32)).astype(BF)
                return carry

            lax.fori_loop(0, n, add, 0)
            if cut > 0:
                over_x().start()
            if cut < high:

                def send(k, peer, source):
                    high_dp(k, peer, 0, j).start()
                    high_dp(k, peer, 1, j2).start()

                peers(send)

        def low_three():
            both(over_x())

            def add(i, carry):
                s[j, i, 0:cut] = (s[j, i, 0:cut].astype(F32) + r2[i].astype(F32)).astype(BF)
                return carry

            lax.fori_loop(0, n, add, 0)
            peers(lambda k, peer, source: low_dp(k, peer).start())

        def high_three():
            def land(k, peer, source):
                both(high_dp(k, peer, 0, j))
                both(high_dp(k, peer, 1, j2))

            peers(land)
            for t, slot in enumerate((j, j2)):
                total = lax.fori_loop(
                    1,
                    n,
                    lambda k, v: v + r4[t, k].astype(F32),
                    s[slot, me, cut:high].astype(F32),
                )
                if t == 0:
                    own[cut:high, :] = total
                else:
                    s[j2, me, cut:high] = total.astype(BF)
            high_x().start()

        def low_four():
            def land(k, peer, source):
                both(low_dp(k, peer))

            peers(land)
            own[0:cut, :] = lax.fori_loop(
                1, n, lambda k, v: v + r3[k].astype(F32), s[j, me, 0:cut].astype(F32)
            )

        def high_four():
            both(high_x())
            own[cut:high, :] = own[cut:high, :] + r5[...].astype(F32)

        return one, two, low_three, high_three, low_four, high_four

    own_t = own_ref.at[0:80, 0:tl]
    own_f = own_ref.at[0:80, tl : tl + fl]
    own_m = own_ref.at[96:128, 0:128]
    f_one, f_two, _, f_three, _, f_four = scatter(
        0, gf, 0, rf1, None, None, rf4, rf5, own_f
    )
    m_one, m_two, m_three, _, m_four, _ = scatter(1, gm, 32, rm1, rm2, rm3, None, None, own_m)
    t_one, t_two, t_low_three, t_high_three, t_low_four, t_high_four = scatter(
        2, gt, CUT, rt1, rt2, rt3, rt4, rt5, own_t
    )

    zero_row = jnp.zeros((1, D), F32)
    dbr = bn
    dbr_t = dy_t

    def back_middle(c, carry):
        at = rows(c * QC, QC)
        value, in_gain, in_shift = norm_back(mid[at, :], gain(2), nn(dhid[at, :], w1t[...]))
        value = value + dy[at, :].astype(F32)
        mid[at, :] = value
        low = value.astype(BF)
        dbr[at, :] = low
        dbr_t[:, across(c)] = low.T
        spread = nt(wop[...], low)
        for h in range(HEADS):
            tile = spread[128 * h : 128 * h + 128, :] * rtot[h, :, across(c)]
            tile_low = tile.astype(BF)
            qt[h, :, across(c)] = tile_low
            datn[h, at, :] = tile_low.T
            delta[h, :, across(c)] = colsum(
                tile_low[64:128, :].astype(F32)
                * att_t[HEAD * h : HEAD * h + HEAD, across(c)].astype(F32)
            )
        return (carry[0] + in_gain, carry[1] + in_shift, carry[2] + colsum(low.astype(F32)))

    sums = lax.fori_loop(0, chunks, back_middle, (zero_row, zero_row, zero_row))
    vg[2:3, :] = sums[0]
    vg[9:10, :] = sums[1]
    vg[8:9, :] = sums[2]
    value = nn(dbr_t[...], att_n[...]).astype(BF)
    for i in range(n):
        gf[:, i, :, 8 * rb : 9 * rb] = value[:, rb * i : rb * i + rb].reshape(4, 80, rb)
    f_one()

    def dkv(h, slot):
        return act.at[rows(slot * keys, keys), tile_at(h)]

    def dk_core(h):
        return [
            remote(dkv(h, slot), rk1.at[h, t], dk_s.at[h, t], dk_r.at[h, t], me, j1)
            for t, slot in enumerate((j1, j3))
        ]

    def dk_x(h):
        return remote(dkv(h, j2), rk2.at[h], dk_s.at[h, 2], dk_r.at[h, 2], me, j2)

    def dk_two(h):
        for copy in dk_core(h):
            both(copy)
        for t, slot in enumerate((j, j2)):
            part = dkv(h, slot)
            part[...] = (part[...].astype(F32) + rk1[h, t].astype(F32)).astype(BF)
        dk_x(h).start()

    def dk_three(h):
        both(dk_x(h))
        qnat[h, 0:keys, :] = (dkv(h, j)[...].astype(F32) + rk2[h].astype(F32)).astype(BF)

    def back_head(h, carry):
        tile = kv[h].reshape(4 * keys, 128)
        total = None
        for c in range(tokens // qa):
            cut = slice(c * qa, (c + 1) * qa)
            powers = prob[h, :, cut]
            slopes = nn(tile, qt[h, :, cut]) - delta[h, :, cut]
            ds = (powers.astype(F32) * slopes).astype(BF)
            part = nn(ds, qnat[h, cut, :]) + nn(powers, datn[h, cut, :])
            prob[h, :, cut] = ds
            total = part if total is None else total + part
        act[0 : 4 * keys, tile_at(h)] = total.astype(BF)
        for copy in dk_core(h):
            copy.start()

        @pl.when(h == 1)
        def _():
            f_two()

        @pl.when(h >= 1)
        def _():
            dk_two(h - 1)

        @pl.when(h >= 2)
        def _():
            dk_three(h - 2)

        return carry

    lax.fori_loop(0, HEADS, back_head, 0)

    def back_query(h, carry):
        for c in range(tokens // qa):
            cut = slice(c * qa, (c + 1) * qa)
            dq_t[rows(h * HEAD, HEAD), cut] = (
                nn(kvt[h, 0:64, :], prob[h, :, cut]) * HEAD**-0.5
            ).astype(BF)
        return carry

    lax.fori_loop(0, 2, back_query, 0)
    dk_two(HEADS - 1)
    dk_three(HEADS - 2)
    lax.fori_loop(2, HEADS, back_query, 0)
    dk_three(HEADS - 1)

    dm = jnp.concatenate([qnat[h, 0:keys, :] for h in range(HEADS)], axis=1)
    dm_sum = colsum(dm.astype(F32))
    vg[7:8, :] = jnp.concatenate(
        [dm_sum[:, 128 * h + 64 : 128 * h + 128] for h in range(HEADS)], axis=1
    )
    dv, in_gain, in_shift = norm_back(red_s[...], gain(1), nn(dm, wmt[...]))
    vg[1:2, :] = in_gain
    vg[6:7, :] = in_shift
    dred = dv.astype(BF)
    vg[5:6, :] = colsum(dred.astype(F32))
    dred_t = dred.T
    for dd in range(4):
        value = nn(dred_t, pat[dd]).astype(BF)
        count = n // 4
        for ii in range(count):
            gt[:, dd * count + ii, :, 0 : 4 * rb] = value[
                :, 4 * rb * ii : 4 * rb * (ii + 1)
            ].reshape(4, 80, 4 * rb)
    value = nn(dm.T, memin[...]).astype(BF)
    value = jnp.concatenate(
        [value[128 * h : 128 * h + 64] for h in range(HEADS)]
        + [value[128 * h + 64 : 128 * h + 128] for h in range(HEADS)],
        axis=0,
    ).reshape(4, 2, 80, D)
    for i in range(n):
        gt[:, i, :, 4 * rb : 6 * rb] = jnp.concatenate(
            [value[:, v, :, rb * i : rb * i + rb] for v in range(2)], axis=2
        )
    t_one()

    dq = att_n

    def flip(c, total):
        low = dq_t[:, across(c)].T
        dq[rows(c * QC, QC), :] = low
        return total + colsum(low.astype(F32))

    vg[4:5, :] = lax.fori_loop(0, chunks, flip, zero_row)
    value = nn(dq_t[...], abf[...]).astype(BF)
    for i in range(n):
        part = value[:, rb * i : rb * i + rb].reshape(4, 80, rb)
        gm[:, i, :, 0 : 3 * rb] = jnp.concatenate(
            [
                part[:, 0:32],
                part[:, 32:64],
                jnp.concatenate([part[:, 64:80], jnp.zeros((4, 16, rb), BF)], axis=1),
            ],
            axis=2,
        )
    m_one()
    t_two()

    for dd in range(4):
        back = nn(dred, wrt[dd])
        back = jnp.concatenate([back, jnp.zeros((keys, 64), F32)], axis=1)
        for i in range(band // 2):
            start = (2 * i + dd // 2) * side + dd % 2
            for t in range(3):
                a3[t, pl.ds(start, half, stride=2), :] = back[
                    i * half : (i + 1) * half, 128 * t : 128 * t + 128
                ]
    m_two()

    def back_first(c, carry):
        at = rows(c * QC, QC)
        e = nn(dq[at, :], wqt[...]) + jnp.concatenate([a3[t, at, :] for t in range(3)], axis=1)[:, 0:D]
        value, in_gain, in_shift = norm_back(x_s[at, :].astype(F32), gain(0), e)
        bn[at, :] = (mid[at, :] + value).astype(BF)
        return (carry[0] + in_gain, carry[1] + in_shift)

    sums = lax.fori_loop(0, chunks, back_first, (zero_row, zero_row))
    token_out = pltpu.make_async_copy(bn, tgrad_ref, loc.at[12])
    token_out.start()
    vg[0:1, :] = sums[0]
    vg[3:4, :] = sums[1]
    for i in range(n):
        sv[i, :, 0 : 4 * rb] = hg[:, 4 * rb * i : 4 * rb * (i + 1)].astype(BF)
        sv[i, :, 4 * rb : 5 * rb] = vg[:, rb * i : rb * i + rb].astype(BF)

    def v_swap(t, to, other):
        return remote(sv, to, rs_s.at[3, t], rs_r.at[3, t], me, other)

    v_swap(0, rv1, j1).start()
    f_three()
    both(v_swap(0, rv1, j1))
    sv[...] = (sv[...].astype(F32) + rv1[...].astype(F32)).astype(BF)
    v_swap(1, rv2, j2).start()
    m_three()
    both(v_swap(1, rv2, j2))
    sv[...] = (sv[...].astype(F32) + rv2[...].astype(F32)).astype(BF)

    def v_copy(k, peer):
        return remote(sv.at[peer], rv3.at[k], rd_s.at[9, k], rd_r.at[9, k], peer, j)

    peers(lambda k, peer, source: v_copy(k, peer).start())
    t_low_three()
    t_high_three()
    f_four()
    squares = jnp.sum(own_f[:, 0 : 9 * rb] * own_f[:, 0 : 9 * rb])
    m_four()
    squares += jnp.sum(own_m[:, 0 : 2 * rb] * own_m[:, 0 : 2 * rb])
    squares += jnp.sum(own_m[0:16, 2 * rb : 3 * rb] * own_m[0:16, 2 * rb : 3 * rb])

    def land_vec(k, peer, source):
        both(v_copy(k, peer))

    peers(land_vec)
    own_v = lax.fori_loop(
        1, n, lambda k, total: total + rv3[k].astype(F32), sv[me].astype(F32)
    )
    own_ref[80:96, 0:vl] = own_v
    first_band = (j == 0).astype(jnp.int32).astype(F32)
    squares += first_band * jnp.sum(own_v[0:11, 0 : 5 * rb] * own_v[0:11, 0 : 5 * rb])
    t_high_four()
    t_low_four()
    squares += jnp.sum(own_t[:, 0 : 6 * rb] * own_t[:, 0 : 6 * rb])

    nrm[me] = jnp.full((8, 128), squares, F32)

    def send_norm(k, peer, source):
        remote(nrm.at[me], nrm.at[me], nd_s.at[k], nd_r.at[k], peer, j).start()

    def wait_norm(k, peer, source):
        both(remote(nrm.at[source], nrm.at[source], nd_s.at[k], nd_r.at[k], peer, j))

    peers(send_norm)
    peers(wait_norm)
    nrs[j] = lax.fori_loop(1, n, lambda k, total: total + nrm[k], nrm[0])
    for t, other in enumerate((j1, j2, j3)):
        remote(nrs.at[j], nrs.at[j], ns_s.at[t], ns_r.at[t], me, other).start()
    for t, other in enumerate((j1, j2, j3)):
        both(remote(nrs.at[other], nrs.at[other], ns_s.at[t], ns_r.at[t], me, other))
    own_ref[80:88, vl : vl + 128] = nrs[0] + nrs[1] + nrs[2] + nrs[3]

    peers(wait_out)
    own_out.wait()
    token_out.wait()


def update_kernel(rb, vl, tl, rates, decays, *refs):
    own_hbm, outt_hbm, tg_hbm = refs[0:3]
    in_hbm = refs[3:30]
    out_hbm, tok_hbm, norm_hbm = refs[30:33]
    new_hbm = refs[33:60]
    own_ref, out_v, tok_v, norm_v = refs[60:64]
    in_v, new_v = refs[64:91], refs[91:118]
    in_sem, out_sem = refs[118:120]
    loads = [
        pltpu.make_async_copy(src, dst, in_sem.at[at])
        for at, (src, dst) in enumerate(
            [(own_hbm, own_ref), *zip(in_hbm, in_v), (outt_hbm, out_v), (tg_hbm, tok_v)]
        )
    ]
    for load in loads:
        load.start()
    stores = [
        pltpu.make_async_copy(src, dst, out_sem.at[at])
        for at, (src, dst) in enumerate(
            [*zip(new_v, new_hbm), (out_v, out_hbm), (tok_v, tok_hbm), (norm_v, norm_hbm)]
        )
    ]
    loads[0].wait()
    total = own_ref[80:81, vl : vl + 128]
    norm = jnp.sqrt(total)
    norm_v[...] = norm
    stores[29].start()
    clip = jnp.minimum(1.0, MAX_NORM / (norm + 1e-06))[:, 0:1]
    turned_t = own_ref[0:80, 0:tl].T
    turned_f = own_ref[0:80, tl:].T
    turned_q = jnp.concatenate(
        [
            own_ref[96:128, 0:rb],
            own_ref[96:128, rb : 2 * rb],
            own_ref[96:112, 2 * rb : 3 * rb],
        ],
        axis=0,
    ).T
    grads = (
        turned_q,
        turned_t[0 : 4 * rb],
        jnp.concatenate([turned_t[(4 + v) * rb : (5 + v) * rb] for v in range(2)], axis=1),
        turned_f[8 * rb : 9 * rb],
        jnp.concatenate([turned_f[(4 + v) * rb : (5 + v) * rb] for v in range(4)], axis=1),
        turned_f[0 : 4 * rb],
        own_ref[80:83, 4 * rb : 5 * rb],
        own_ref[83:91, 4 * rb : 5 * rb],
        own_ref[80:91, 0 : 4 * rb],
    )
    for at in range(9):
        for part in range(3):
            loads[1 + at + 9 * part].wait()
        clipped = clip * grads[at]
        weight = in_v[at][...]
        first = BETA_ONE * in_v[9 + at][...] + (1.0 - BETA_ONE) * clipped
        second = BETA_TWO * in_v[18 + at][...] + (1.0 - BETA_TWO) * clipped * clipped
        direction = (
            first
            / (1.0 - BETA_ONE**STEP)
            / (jnp.sqrt(second / (1.0 - BETA_TWO**STEP)) + ADAM_EPS)
        )
        new_v[at][...] = weight - rates[at] * (direction + decays[at] * weight)
        new_v[9 + at][...] = first
        new_v[18 + at][...] = second
        for part in range(3):
            stores[at + 9 * part].start()
    for at in (28, 29):
        loads[at].wait()
        stores[at - 1].start()
    for store in stores:
        store.wait()


def on_device(n, *args):
    tokens, buckets, cotangent = args[0:3]
    weights, firsts, seconds = args[3:12], args[12:21], args[21:30]
    band, side, width = tokens.shape[1:4]
    count = band * side
    keys = count // 4
    rb = weights[0].shape[0]
    piece = cotangent.shape[3]
    wide = up(9 * rb, 128)
    tl = up(6 * rb, 128)
    vl = up(5 * rb, 128)
    total = tl + wide
    qa = count if n <= 8 else QC
    turned = piece % 128 == 0
    block = (n, D, piece) if turned else (n, piece, D)
    vm = pltpu.VMEM
    dma = pltpu.SemaphoreType.DMA
    scratch = [
        vm((count, D), BF),
        *[vm(weights[at].shape, F32) for at in range(9)],
        vm((n, 16, vl), BF),
        vm((4, n, 80, tl), BF),
        vm((4, n, 32, 128), BF),
        vm((4, n, 80, wide), BF),
        vm((16, D), F32),
        vm((16, FF), F32),
        vm((D, D), BF),
        vm((2 * D, D), BF),
        vm((D, D), BF),
        vm((2 * D, D), BF),
        vm((2 * D, D), BF),
        vm((4, D, D), BF),
        vm((FF, D), BF),
        vm((D, FF), BF),
        vm((3, count, 128), F32),
        vm((count, D), BF),
        vm((4, keys, D), BF),
        vm((keys, D), F32),
        vm((keys, D), BF),
        vm((HEADS, 4, keys, 128), BF),
        vm((HEADS, 128, 4 * keys), BF),
        vm((4 * keys, 128), BF),
        vm((128, count), BF),
        vm((HEADS, count, 128), BF),
        vm((HEADS, 128, count), BF),
        vm((HEADS, 4 * keys, count), BF),
        vm((D, count), BF),
        vm((count, D), BF),
        vm((HEADS, 1, count), F32),
        vm((HEADS, 1, count), F32),
        vm((count, D), F32),
        vm((count, D), BF),
        vm((D, count), BF),
        vm((count + 2 * side, FF), BF),
        vm((2, side, FF), BF),
        vm((count + 2 * side, FF), BF),
        vm((count, FF), BF),
        vm(block, BF),
        vm(block, BF),
        vm((D, count), BF),
        vm((count, D), BF),
        vm((2, side, FF), BF),
        vm((HEADS, count, 128), BF),
        vm((HEADS, 2, keys, 128), BF),
        vm((HEADS, keys, 128), BF),
        vm((D, count), BF),
        vm((16, FF), F32),
        vm((16, D), F32),
        vm((2, n, 80, wide), BF),
        vm((2, n, 80, wide), BF),
        vm((80, wide), BF),
        vm((2, n, 80, tl), BF),
        vm((n, CUT, tl), BF),
        vm((n, CUT, tl), BF),
        vm((2, n, 80 - CUT, tl), BF),
        vm((80 - CUT, tl), BF),
        vm((2, n, 32, 128), BF),
        vm((n, 32, 128), BF),
        vm((n, 32, 128), BF),
        vm((n, 16, vl), BF),
        vm((n, 16, vl), BF),
        vm((n, 16, vl), BF),
        vm((n, 16, vl), BF),
        vm((n, 8, 128), F32),
        vm((4, 8, 128), F32),
        vm((side, 128), F32),
        vm((side, 128), F32),
        dma((13,)),
        *[dma((n,)) for _ in range(2)],
        *[dma((6, n)) for _ in range(2)],
        *[dma((3, 4)) for _ in range(2)],
        *[dma((n,)) for _ in range(4)],
        *[dma((HEADS, 3)) for _ in range(2)],
        *[dma((4,)) for _ in range(2)],
        *[dma((HEADS, 3)) for _ in range(2)],
        *[dma((4, 4)) for _ in range(2)],
        *[dma((10, n)) for _ in range(2)],
        *[dma((n,)) for _ in range(2)],
        *[dma((3,)) for _ in range(2)],
    ]
    anywhere = pl.BlockSpec(memory_space=pl.ANY)
    in_vmem = pl.BlockSpec(memory_space=pltpu.VMEM)
    out_t, token_grad, own = pl.pallas_call(
        functools.partial(block_kernel, n, side, band, qa),
        out_shape=(
            jax.ShapeDtypeStruct(block, BF),
            jax.ShapeDtypeStruct((count, D), BF),
            jax.ShapeDtypeStruct((128, total), F32),
        ),
        in_specs=[pl.BlockSpec(memory_space=pltpu.SMEM)] + [anywhere] * 11,
        out_specs=(anywhere, anywhere, in_vmem),
        scratch_shapes=scratch,
        compiler_params=pltpu.CompilerParams(
            collective_id=0, has_side_effects=True, vmem_limit_bytes=VMEM_LIMIT
        ),
    )(
        buckets,
        tokens.reshape(count, width),
        jnp.swapaxes(cotangent, 3, 4).reshape(block) if turned else cotangent.reshape(block),
        *weights,
    )
    rates = (
        D ** (-0.5),
        (4 * D) ** (-0.5),
        D ** (-0.5),
        OUT_FAN ** (-0.5),
        D ** (-0.5),
        FF ** (-0.5),
        GAIN_RATE,
        VECTOR_RATE,
        VECTOR_RATE,
    )
    decays = (DECAY_RATE,) * 6 + (0.0,) * 3
    shapes = tuple(jax.ShapeDtypeStruct(w.shape, F32) for w in weights)
    results = pl.pallas_call(
        functools.partial(update_kernel, rb, vl, tl, rates, decays),
        out_shape=(
            jax.ShapeDtypeStruct(block, BF),
            jax.ShapeDtypeStruct((count, D), BF),
            jax.ShapeDtypeStruct((1, 128), F32),
        )
        + shapes * 3,
        in_specs=[anywhere] * 30,
        out_specs=(anywhere,) * 30,
        scratch_shapes=[
            vm((128, total), F32),
            vm(block, BF),
            vm((count, D), BF),
            vm((1, 128), F32),
            *[vm(w.shape, F32) for w in weights * 6],
            dma((30,)),
            dma((30,)),
        ],
    )(own, out_t, token_grad, *weights, *firsts, *seconds)
    if turned:
        block_output = jnp.swapaxes(results[0].reshape(n, 1, 1, width, piece), 3, 4)
    else:
        block_output = results[0].reshape(n, 1, 1, piece, width)
    return (
        block_output,
        results[1].reshape(1, band, side, width),
        results[2][0, 0],
        *results[3:],
    )


def solution(mesh):
    matrix = (P("dp", "seq"),) * 6 + (P(None, "dp"),) * 3
    return jax.shard_map(
        functools.partial(on_device, mesh.shape["dp"]),
        mesh=mesh,
        in_specs=(
            P("dp", "seq", None, None),
            P("dp"),
            P(None, "seq", "dp", None, None),
            *(matrix * 3),
        ),
        out_specs=(
            P(None, "seq", "dp", None, None),
            P("dp", "seq", None, None),
            P(),
            *(matrix * 3),
        ),
        check_vma=False,
    )
```

time: 220 us -> 146 us (0.66)
  Pallas kernels: 218 us -> 144 us
    pallas_call x2, Pallas kernels: 218 us -> 144 us  [the longest x1 140 us: on_device(): pl.pallas_call(functools.partial(block_kernel, n, side, band, qa), out_sh...]
where the time goes in v2:
time: 146 us; the launch traced here: 145 us
  Pallas kernels  144 us (99%)
  between operations  1.48 us (1%)
    pallas_call x1, Pallas kernels, on_device(): pl.pallas_call(functools.partial(block_kernel, n, side, band, qa), out_sh...  140 us
    pallas_call x1, Pallas kernels, on_device(): pl.pallas_call(functools.partial(update_kernel, rb, vl, tl, rates, decays...  3.69 us

profile of v2, /device:TPU:0, one launch (start us, length us, event | category | flops | bytes accessed | tf_op | source)
XLA Modules:
  0.0 145.4 jit_solution(15677664599302375557)
XLA Ops:
  1.3 140.3 %shard_map.517 = (bf16[8,320,128]{2,1,0:T(8,128)(2,1)}, bf16[1024,320]{1,0:T(8,128)(2,1)}, f32[128,640]{1,0:T(8,128)}) custom-call(s32[1]{0:T(128)S(6)} %copy.62.bucket_ref, bf16[1024,320]{1,0:T(8,128)(2,1)} %bitcast.14, bf16[8,320,128]{2,1,0:T(8,128)(2,1)} %bitcast.15, f32[40,80]{1,0:T(8,128)} %refs_3_.1, f32[160,80]{1,0:T(8,128)} %refs_4_.1, ...), custom_call_target="tpu_custom_call" | custom-call | tf_op jit(solution)/shard_map/pallas_call | solution.py:1339
  141.6 3.7 %shard_map.518 = (bf16[8,320,128]{2,1,0:T(8,128)(2,1)}, bf16[1024,320]{1,0:T(8,128)(2,1)}, f32[1,128]{1,0:T(1,128)}, f32[40,80]{1,0:T(8,128)}, f32[160,80]{1,0:T...) custom-call(f32[128,640]{1,0:T(8,128)} %get-tuple-element.63.refs_0_, ...), custom_call_target="tpu_custom_call" | custom-call | tf_op jit(solution)/shard_map/pallas_call | solution.py:1371

commit v3 on v2

v3 whole, which is shorter than its diff:
```python
import functools

import jax
import jax.numpy as jnp
from jax import lax
from jax.experimental import pallas as pl
from jax.experimental.pallas import tpu as pltpu
from jax.sharding import PartitionSpec as P

D = 320
HEADS = 5
HEAD = 64
FF = 1280
STEP = 10
OUT_FAN = 5

NORM_EPS = 1e-06
MAX_NORM = 1.0
BETA_ONE = 0.9
BETA_TWO = 0.95
ADAM_EPS = 1e-08
DECAY_RATE = 0.01
VECTOR_RATE = 0.3
GAIN_RATE = 0.8
MASKED = -1e30

BF = jnp.bfloat16
F32 = jnp.float32
MESH = pl.DeviceIdType.MESH
QC = 512
CUT = 48
VMEM_LIMIT = 63 * 1024 * 1024


def nn(a, b):
    return lax.dot_general(a, b, (((1,), (0,)), ((), ())), preferred_element_type=F32)


def nt(a, b):
    return lax.dot_general(a, b, (((1,), (1,)), ((), ())), preferred_element_type=F32)


def up(n, m):
    return (n + m - 1) // m * m


def norm_parts(v):
    centered = v - jnp.mean(v, axis=-1, keepdims=True)
    rstd = lax.rsqrt(jnp.mean(centered * centered, axis=-1, keepdims=True) + NORM_EPS)
    return centered * rstd, rstd


def norm_back(v, gain, e):
    vhat, rstd = norm_parts(v)
    u = e * gain
    dv = rstd * (
        u
        - jnp.mean(u, axis=-1, keepdims=True)
        - vhat * jnp.mean(u * vhat, axis=-1, keepdims=True)
    )
    return dv, jnp.sum(e * vhat, axis=0, keepdims=True), jnp.sum(e, axis=0, keepdims=True)


def colsum(v):
    return jnp.sum(v, axis=0, keepdims=True)


def rows(start, size):
    return pl.ds(pl.multiple_of(start, 16), size)


def block_kernel(
    n,
    side,
    band,
    qa,
    bucket_ref,
    tok_ref,
    cot_ref,
    wq_ref,
    wr_ref,
    wm_ref,
    wo_ref,
    w1_ref,
    w2_ref,
    gains_ref,
    biases_ref,
    hidden_ref,
    out_ref,
    tgrad_ref,
    own_ref,
    norm_ref,
    x_s,
    fq,
    fr,
    fm,
    fo,
    f1,
    f2,
    fg,
    fb,
    fh,
    gvec,
    gt,
    gm,
    gf,
    vp,
    hp,
    wqt,
    wot,
    wop,
    wmt,
    wrt,
    w1t,
    w2t,
    a3,
    abf,
    pat,
    red_s,
    memin,
    kv,
    kvt,
    qnat,
    qt,
    prob,
    att_t,
    att_n,
    rtot,
    delta,
    mid,
    bn,
    hidp,
    hidh,
    act,
    gp,
    out_t,
    dy_in,
    dy_t,
    dy,
    dzh,
    datn,
    rk1,
    rk2,
    hg,
    vg,
    own_s,
    sb,
    ra0,
    ra1,
    ra2,
    ra3,
    ra4,
    ra5,
    ra6,
    rb0,
    rb1,
    rb2,
    rb3,
    rb4,
    rb5,
    rb6,
    rt0,
    rt1,
    rt2,
    rt3,
    rt4,
    rt5,
    rt6,
    rm0,
    rm1,
    rm2,
    rm3,
    rm4,
    rm5,
    rm6,
    sv,
    rv1,
    rv2,
    nrm,
    shift_f,
    shift_b,
    shift_m,
    loc,
    gd_s,
    gd_r,
    gx_s,
    gx_r,
    co_s,
    co_r,
    ou_s,
    ou_r,
    kv_s,
    kv_r,
    ha_s,
    ha_r,
    dk_s,
    dk_r,
    rs_s,
    rs_r,
    nd_s,
    nd_r,
):
    me = lax.axis_index("dp")
    j = lax.axis_index("seq")
    y0 = lax.rem(me, 2)
    y1 = 1 - y0
    z0 = lax.div(me, 2)
    beside = me + 1 - 2 * y0
    zn = n // 2
    here = y0 * zn + z0

    def place_of(i):
        return i % 2 * zn + i // 2

    def spot(i):
        return lax.rem(i, 2) * zn + lax.div(i, 2)

    j1 = j + 1 - 2 * lax.rem(j, 2)
    j2 = lax.rem(j + 2, 4)
    j3 = 3 - j
    tokens = band * side
    chunks = tokens // QC
    rb = wq_ref.shape[0]
    piece = tokens // n
    keys = kv.shape[2]
    turned = cot_ref.shape[1] == D
    tl = gt.shape[3]
    fl = gf.shape[3]
    vl = gvec.shape[2]
    al = up(4 * rb, 128)
    bl = sb.shape[3]

    def remote(src, dst, ss, rs, dp, seq):
        return pltpu.make_async_remote_copy(
            src_ref=src,
            dst_ref=dst,
            send_sem=ss,
            recv_sem=rs,
            device_id=(dp, seq),
            device_id_type=MESH,
        )

    def both(copy):
        copy.wait_send()
        copy.wait_recv()

    def peers(body):
        def step(k, carry):
            body(k, lax.rem(me + k, n), lax.rem(me + n - k, n))
            return carry

        lax.fori_loop(1, n, step, 0)

    def z_peers(body):
        def step(k, carry):
            body(k, lax.rem(me + 2 * k, n), lax.rem(z0 + k, zn), lax.rem(z0 + zn - k, zn))
            return carry

        lax.fori_loop(1, zn, step, 0)

    loads = [
        pltpu.make_async_copy(src, dst, loc.at[at])
        for at, (src, dst) in enumerate(
            (
                (gains_ref, fg),
                (biases_ref, fb),
                (hidden_ref, fh),
                (wr_ref, fr),
                (wm_ref, fm),
                (wq_ref, fq),
                (wo_ref, fo),
                (w1_ref, f1),
                (w2_ref, f2),
                (tok_ref, x_s),
            )
        )
    ]
    for copy in loads:
        copy.start()
    def incoming(i):
        return dy_in.at[i] if turned else dy.at[rows(i * piece, piece)]

    own_cot = pltpu.make_async_copy(cot_ref.at[me], incoming(me), loc.at[10])
    own_cot.start()

    barrier = pltpu.get_barrier_semaphore()

    def greet(k, carry):
        to = lax.rem(4 * me + j + k, 4 * n)
        pl.semaphore_signal(
            barrier, inc=1, device_id=(lax.div(to, 4), lax.rem(to, 4)), device_id_type=MESH
        )
        return carry

    lax.fori_loop(1, 4 * n, greet, 0)

    for copy in loads[:5]:
        copy.wait()
    hidden16 = jnp.concatenate([fh[...], jnp.zeros((5, 4 * rb), F32)], axis=0)
    small16 = jnp.concatenate([fg[...], fb[...], jnp.zeros((5, rb), F32)], axis=0)
    gvec[here] = jnp.concatenate(
        [hidden16, small16, jnp.zeros((16, vl - 5 * rb), F32)], axis=1
    ).astype(BF)
    wm_t = fm[...].T
    gt[j, here] = jnp.concatenate(
        [fr[...].T, wm_t[0:80], wm_t[80:160], jnp.zeros((80, tl - 6 * rb), F32)], axis=1
    ).astype(BF)

    def group(at, one_of, all_but_one, each):
        def start():
            def send(peer):
                ref = one_of(here)
                remote(ref, ref, gd_s.at[at], gd_r.at[at], peer, j).start()

            each(send)

        def wait():
            both(remote(all_but_one, all_but_one, gd_s.at[at], gd_r.at[at], beside, j))

        return start, wait

    def each_peer(send):
        peers(lambda k, peer, source: send(peer))

    def each_z(send):
        z_peers(lambda k, peer, to, source: send(peer))

    def over_dp(at, buf, rows_of):
        return group(
            at, lambda i: buf.at[i, rows_of], buf.at[pl.ds(0, n - 1), rows_of], each_peer
        )

    def over_z(at, buf, rows_of):
        return group(
            at, lambda i: buf.at[i, rows_of], buf.at[pl.ds(0, zn - 1), rows_of], each_z
        )

    def swap(at, mine, theirs, dp, seq):
        def start():
            remote(mine, mine, gx_s.at[at], gx_r.at[at], dp, seq).start()

        def wait():
            remote(mine, mine, gx_s.at[at], gx_r.at[at], dp, seq).wait_send()
            remote(theirs, theirs, gx_s.at[at], gx_r.at[at], dp, seq).wait_recv()

        return start, wait

    def over_y(at, buf, rows_of):
        mine = buf.at[pl.ds(y0 * zn, zn), rows_of]
        theirs = buf.at[pl.ds(y1 * zn, zn), rows_of]
        return swap(at, mine, theirs, beside, j)

    lower = slice(0, CUT)
    upper = slice(CUT, 80)
    every = slice(0, 16)
    v_dp, v_dp_wait = over_dp(0, gvec, every)
    t_dp, t_dp_wait = over_dp(1, gt.at[j], lower)
    t_x, t_x_wait = swap(0, gt.at[j, :, lower], gt.at[j2, :, lower], me, j2)
    t_x0, t_x0_wait = swap(1, gt.at[j, here, upper], gt.at[j2, here, upper], me, j2)
    t_za, t_za_wait = over_z(2, gt.at[j], upper)
    t_zb, t_zb_wait = over_z(3, gt.at[j2], upper)
    t_ya, t_ya_wait = over_y(2, gt.at[j], upper)
    t_yb, t_yb_wait = over_y(3, gt.at[j2], upper)
    t_ca, t_ca_wait = swap(4, gt.at[j], gt.at[j1], me, j1)
    t_cb, t_cb_wait = swap(5, gt.at[j2], gt.at[j3], me, j1)
    m_dp, m_dp_wait = over_dp(4, gm.at[j], slice(0, 32))
    m_x, m_x_wait = swap(6, gm.at[j], gm.at[j2], me, j2)
    m_ca, m_ca_wait = swap(7, gm.at[j], gm.at[j1], me, j1)
    m_cb, m_cb_wait = swap(8, gm.at[j2], gm.at[j3], me, j1)
    f_x0, f_x0_wait = swap(9, gf.at[j, here], gf.at[j2, here], me, j2)
    fl_za, fl_za_wait = over_z(5, gf.at[j], lower)
    fl_zb, fl_zb_wait = over_z(6, gf.at[j2], lower)
    fh_za, fh_za_wait = over_z(7, gf.at[j], upper)
    fh_zb, fh_zb_wait = over_z(8, gf.at[j2], upper)
    fl_ya, fl_ya_wait = over_y(10, gf.at[j], lower)
    fl_yb, fl_yb_wait = over_y(11, gf.at[j2], lower)
    fh_ya, fh_ya_wait = over_y(12, gf.at[j], upper)
    fh_yb, fh_yb_wait = over_y(13, gf.at[j2], upper)
    f_ca, f_ca_wait = swap(14, gf.at[j], gf.at[j1], me, j1)
    f_cb, f_cb_wait = swap(15, gf.at[j2], gf.at[j3], me, j1)

    pl.semaphore_wait(barrier, 4 * n - 1)
    t_x0()
    v_dp()
    t_dp()

    for copy in loads[5:9]:
        copy.wait()
    wq_t = fq[...].T
    gm[j, here] = jnp.concatenate(
        [
            wq_t[0:32],
            wq_t[32:64],
            jnp.concatenate([wq_t[64:80], jnp.zeros((16, rb), F32)], axis=0),
            jnp.zeros((32, 128 - 3 * rb), F32),
        ],
        axis=1,
    ).astype(BF)
    w1_t = f1[...].T
    gf[j, here] = jnp.concatenate(
        [f2[...].T]
        + [w1_t[80 * v : 80 * v + 80] for v in range(4)]
        + [fo[...].T, jnp.zeros((80, fl - 9 * rb), F32)],
        axis=1,
    ).astype(BF)
    f_x0()
    t_x0_wait()
    t_za()
    t_zb()
    m_dp()

    v_dp_wait()
    hp[...] = jnp.concatenate([gvec[place_of(i), :, 0 : 4 * rb] for i in range(n)], axis=1).astype(F32)
    vp[...] = jnp.concatenate(
        [gvec[place_of(i), :, 4 * rb : 5 * rb] for i in range(n)], axis=1
    ).astype(F32)

    def gain(k):
        return vp[k : k + 1, :]

    def shift(k):
        return vp[3 + k : 4 + k, :]

    loads[9].wait()

    def norm_one(c, carry):
        at = rows(c * QC, QC)
        vhat, _ = norm_parts(x_s[at, :].astype(F32))
        low = (vhat * gain(0) + shift(0)).astype(BF)
        abf[at, :] = low
        wide = jnp.concatenate([low.astype(F32), jnp.zeros((QC, 64), F32)], axis=1)
        for t in range(3):
            a3[t, at, :] = wide[:, 128 * t : 128 * t + 128]
        return carry

    lax.fori_loop(0, chunks, norm_one, 0)
    half = side // 2
    for dd in range(4):
        for i in range(band // 2):
            start = (2 * i + dd // 2) * side + dd % 2
            cut = jnp.concatenate(
                [a3[t, pl.ds(start, half, stride=2), :] for t in range(3)], axis=1
            )
            pat[dd, i * half : (i + 1) * half, :] = cut[:, 0:D].astype(BF)

    bucket = bucket_ref[0]
    k_row = lax.broadcasted_iota(jnp.int32, (4 * keys, 128), 0)
    k_lane = lax.broadcasted_iota(jnp.int32, (4 * keys, 128), 1)
    k_id = (lax.div(k_row, half) >= half // 2).astype(jnp.int32) * 2 + (
        lax.rem(k_row, half) >= half // 2
    ).astype(jnp.int32)
    off = (k_id != k_lane).astype(jnp.int32) * bucket * (k_lane < 4).astype(jnp.int32)
    kmask = datn.at[0]
    qmask = dy_t.at[0:128]
    kmask[...] = (off.astype(F32) * MASKED).astype(BF)
    q_row = lax.broadcasted_iota(jnp.int32, (128, tokens), 0)
    place = lax.broadcasted_iota(jnp.int32, (128, tokens), 1)
    q_id = (lax.div(place, side) + j * band >= half).astype(jnp.int32) * 2 + (
        lax.rem(place, side) >= half
    ).astype(jnp.int32)
    qmask[...] = (q_id == q_row).astype(F32).astype(BF)
    col = lax.broadcasted_iota(jnp.int32, (side, side), 0)
    ok_l = (col > 0).astype(jnp.int32) * (1 - bucket * (col == half).astype(jnp.int32))
    ok_r = (col < side - 1).astype(jnp.int32) * (
        1 - bucket * (col == half - 1).astype(jnp.int32)
    )
    lane = lax.broadcasted_iota(jnp.int32, (side, side), 1)
    from_l = (ok_l * (lane == col - 1).astype(jnp.int32)).astype(F32).astype(BF)
    from_r = (ok_r * (lane == col + 1).astype(jnp.int32)).astype(F32).astype(BF)
    shift_f[...] = jnp.concatenate([from_l, from_r], axis=1)
    shift_b[...] = jnp.concatenate([from_r, from_l], axis=1)
    shift_m[...] = jnp.concatenate([from_r, from_l], axis=0)
    top_ok = (
        (j > 0).astype(jnp.int32) * (1 - bucket * (j * band == half).astype(jnp.int32))
    ).astype(F32)
    low_ok = (
        (j < 3).astype(jnp.int32) * (1 - bucket * ((j + 1) * band == half).astype(jnp.int32))
    ).astype(F32)

    t_dp_wait()
    t_x()
    t_za_wait()
    t_zb_wait()
    t_ya()
    t_yb()
    f_x0_wait()
    fl_za()
    fl_zb()
    fh_za()
    fh_zb()
    t_ya_wait()
    t_yb_wait()
    m_dp_wait()
    m_x()
    t_x_wait()
    t_ca()
    t_cb()
    m_x_wait()
    m_ca()
    m_cb()
    t_ca_wait()
    t_cb_wait()

    for s in range(4):
        span = slice(80 * s, 80 * s + 80)

        def lanes(lo, hi, over):
            return jnp.concatenate([gt[s, place_of(i), :, lo:hi] for i in over], axis=1)

        for dd in range(4):
            wrt[dd, span, :] = lanes(0, 4 * rb, range(dd * n // 4, (dd + 1) * n // 4))
        for v in range(2):
            wop[160 * s + 80 * v : 160 * s + 80 * v + 80, :] = lanes(
                (4 + v) * rb, (5 + v) * rb, range(n)
            )
    for h in range(HEADS):
        wmt[128 * h : 128 * h + 64, :] = wop[HEAD * h : HEAD * h + HEAD, :]
        wmt[128 * h + 64 : 128 * h + 128, :] = wop[D + HEAD * h : D + HEAD * h + HEAD, :]

    red = shift(2) + nt(pat[0], wrt[0])
    for dd in range(1, 4):
        red = red + nt(pat[dd], wrt[dd])
    red_s[...] = red
    vhat, _ = norm_parts(red)
    low = (vhat * gain(1) + shift(3)).astype(BF)
    memin[...] = low
    zero64 = jnp.zeros((1, HEAD), F32)
    value_shift = jnp.concatenate(
        [
            part
            for h in range(HEADS)
            for part in (zero64, shift(4)[:, HEAD * h : HEAD * h + HEAD])
        ],
        axis=1,
    )
    memory = (nt(low, wmt[...]) + value_shift).astype(BF)
    for h in range(HEADS):
        kv[h, j] = memory[:, 128 * h : 128 * h + 128]

    def kv_copy(h, slot, t, other):
        return remote(
            kv.at[h, slot], kv.at[h, slot], kv_s.at[h, t], kv_r.at[h, t], me, other
        )

    def kv_send(h, carry):
        kv_copy(h, j, 0, j2).start()
        kv_copy(h, j, 1, j1).start()
        return carry

    lax.fori_loop(0, HEADS, kv_send, 0)

    fl_za_wait()
    fl_zb_wait()
    fl_ya()
    fl_yb()
    wqp = wop
    m_ca_wait()
    m_cb_wait()
    for s in range(4):
        at = 80 * s
        wqt[at : at + 32, :] = jnp.concatenate([gm[s, place_of(i), :, 0:rb] for i in range(n)], axis=1)
        wqt[at + 32 : at + 64, :] = jnp.concatenate(
            [gm[s, place_of(i), :, rb : 2 * rb] for i in range(n)], axis=1
        )
        wqt[at + 64 : at + 80, :] = jnp.concatenate(
            [gm[s, place_of(i), 0:16, 2 * rb : 3 * rb] for i in range(n)], axis=1
        )
    for h in range(HEADS):
        wqp[128 * h : 128 * h + 64, :] = wqt[HEAD * h : HEAD * h + HEAD, :]
        wqp[128 * h + 64 : 128 * h + 128, :] = jnp.zeros((64, D), BF)

    query_shift = jnp.concatenate(
        [
            part
            for h in range(HEADS)
            for part in (shift(1)[:, HEAD * h : HEAD * h + HEAD], zero64)
        ],
        axis=1,
    )

    def across(c):
        return pl.ds(pl.multiple_of(c * QC, QC), QC)

    def queries(c, carry):
        at = rows(c * QC, QC)
        q = (nt(abf[at, :], wqp[...]) + query_shift).astype(BF) * jnp.asarray(HEAD**-0.5, BF)
        for h in range(HEADS):
            tile = q[:, 128 * h : 128 * h + 128]
            qnat[h, at, :] = tile
            qt[h, :, across(c)] = tile.T
        return carry

    lax.fori_loop(0, chunks, queries, 0)

    def send_cot(k, peer, source):
        remote(cot_ref.at[peer], incoming(me), co_s.at[0], co_r.at[0], peer, j).start()

    def wait_cot():
        part = cot_ref.at[pl.ds(0, n - 1)]
        both(remote(part, part, co_s.at[0], co_r.at[0], beside, j))

    def kv_forward(h):
        kv_copy(h, j2, 0, j2).wait_recv()
        kv_copy(h, j2, 2, j1).start()

    kv_forward(0)

    def attend(h, carry):
        @pl.when(h == 1)
        def _():
            fh_za_wait()
            fh_zb_wait()
            fh_ya()
            fh_yb()

        @pl.when(h == HEADS - 1)
        def _():
            fl_ya_wait()
            fl_yb_wait()
            fh_ya_wait()
            fh_yb_wait()
            f_ca()
            f_cb()
            peers(send_cot)

        kv_copy(h, j, 0, j2).wait_send()
        kv_copy(h, j, 1, j1).wait_send()
        kv_copy(h, j2, 2, j1).wait_send()
        kv_copy(h, j1, 1, j1).wait_recv()
        kv_copy(h, j3, 2, j1).wait_recv()
        tile = kv[h].reshape(4 * keys, 128)
        kvt[h] = tile.T
        left = jnp.concatenate([tile, kmask[...]], axis=1)
        values = jnp.concatenate([kvt[h, 64:128, :], jnp.ones((16, 4 * keys), BF)], axis=0)
        for c in range(tokens // qa):
            cut = slice(c * qa, (c + 1) * qa)
            scores = nn(left, jnp.concatenate([qt[h, :, cut], qmask[:, cut]], axis=0))
            if c == 0:

                @pl.when(h < HEADS - 1)
                def _():
                    kv_forward(h + 1)

            largest = jnp.max(scores, axis=0, keepdims=True)
            powers = jnp.exp(scores - largest).astype(BF)
            prob[h, :, cut] = powers
            got = nn(values, powers)
            scale = 1.0 / got[64:65, :]
            rtot[h, :, cut] = scale
            att_t[rows(h * HEAD, HEAD), cut] = (got[0:64, :] * scale).astype(BF)
        return carry

    lax.fori_loop(0, HEADS, attend, 0)

    f_ca_wait()
    f_cb_wait()
    for s in range(4):
        span = slice(80 * s, 80 * s + 80)
        w2t[span, :] = jnp.concatenate([gf[s, place_of(i), :, 0 : 4 * rb] for i in range(n)], axis=1)
        for v in range(4):
            at = 320 * s + 80 * v
            w1t[at : at + 80, :] = jnp.concatenate(
                [gf[s, place_of(i), :, (4 + v) * rb : (5 + v) * rb] for i in range(n)], axis=1
            )
        wot[span, :] = jnp.concatenate(
            [gf[s, place_of(i), :, 8 * rb : 9 * rb] for i in range(n)], axis=1
        )
    wop_full = wot[...].T
    for h in range(HEADS):
        wop[128 * h : 128 * h + 64, :] = jnp.zeros((64, D), BF)
        wop[128 * h + 64 : 128 * h + 128, :] = wop_full[HEAD * h : HEAD * h + HEAD, :]

    def middle(c, carry):
        at = rows(c * QC, QC)
        att = att_t[:, across(c)].T
        att_n[at, :] = att
        value = x_s[at, :].astype(F32) + nt(att, wot[...]) + shift(5)
        mid[at, :] = value
        vhat, _ = norm_parts(value)
        low = (vhat * gain(2) + shift(6)).astype(BF)
        bn[at, :] = low
        return carry

    lax.fori_loop(0, chunks, middle, 0)

    edge = tokens - side

    def hidden_of(value):
        return (nt(value, w1t[...]) + hp[9:10, :]).astype(BF)

    ends = hidden_of(jnp.concatenate([bn[0:side, :], bn[edge:tokens, :]], axis=0))
    hidp[side : 2 * side, :] = ends[0:side]
    hidp[tokens : tokens + side, :] = ends[side : 2 * side]
    above = lax.rem(j + 3, 4)
    below = lax.rem(j + 1, 4)

    def rim_up(buf, halo, at):
        return remote(buf.at[pl.ds(side, side)], halo.at[1], ha_s.at[at], ha_r.at[at], me, above)

    def rim_down(buf, halo, at):
        return remote(
            buf.at[pl.ds(tokens, side)], halo.at[0], ha_s.at[at + 1], ha_r.at[at + 1], me, below
        )

    def rim_send(buf, halo, at):
        @pl.when(j > 0)
        def _():
            rim_up(buf, halo, at).start()

        @pl.when(j < 3)
        def _():
            rim_down(buf, halo, at).start()

    def rim_wait(buf, halo, at):
        @pl.when(j > 0)
        def _():
            rim_up(buf, halo, at).wait_send()
            rim_down(buf, halo, at).wait_recv()

        @pl.when(j < 3)
        def _():
            rim_down(buf, halo, at).wait_send()
            rim_up(buf, halo, at).wait_recv()

        for t, (to, ok) in enumerate(((0, top_ok), (tokens + side, low_ok))):
            seen = jnp.full((side, FF), ok, F32) > 0.5
            buf[to : to + side, :] = jnp.where(seen, halo[t].astype(F32), 0.0).astype(BF)

    rim_send(hidp, hidh, 0)

    inner = (tokens - 2 * side) // 2

    def inner_hidden(c, carry):
        start = side + c * inner
        hidp[rows(start + side, inner), :] = hidden_of(bn[rows(start, inner), :])
        return carry

    lax.fori_loop(0, 2, inner_hidden, 0)

    def tile_at(t):
        return pl.ds(pl.multiple_of(t * 128, 128), 128)

    def taps_of(lanes):
        return [hp[k : k + 1, lanes] for k in range(9)]

    def conv_over(lo, hi, step, tiles):
        def conv_tile(t, carry):
            lanes = tile_at(t)
            taps = taps_of(lanes)
            base = hp[10:11, lanes]

            def row(at, inner):
                r = lo + at * step
                around = [hidp[rows((r + a) * side, side), lanes].astype(F32) for a in range(3)]
                parts = [
                    taps[b] * around[0] + taps[3 + b] * around[1] + taps[6 + b] * around[2]
                    for b in range(3)
                ]
                moved = jnp.concatenate([parts[0].astype(BF), parts[2].astype(BF)], axis=0)
                z = base + parts[1] + nn(shift_f[...], moved)
                cdf = 0.5 + 0.5 * lax.erf(z * (0.5**0.5))
                pdf = jnp.exp(z * z * -0.5) * 0.3989422804014327
                act[rows((r + 1) * side, side), lanes] = (z * cdf).astype(BF)
                gp[rows(r * side, side), lanes] = (cdf + z * pdf).astype(BF)
                return inner

            lax.fori_loop(0, (hi - lo) // step, row, 0, unroll=True)
            return carry

        lax.fori_loop(0, FF // 128, conv_tile, 0, unroll=tiles)

    conv_over(1, band - 1, 1, 1)
    rim_wait(hidp, hidh, 0)
    conv_over(0, 2 * (band - 1), band - 1, 5)

    def out_chunk(c, carry):
        at = rows(c * QC, QC)
        value = mid[at, :] + nt(act[rows(side + c * QC, QC), :], w2t[...]) + shift(7)
        for p in range(QC // piece):
            part = value[p * piece : (p + 1) * piece, :]
            out_t[c * (QC // piece) + p] = (part.T if turned else part).astype(BF)
        return carry

    lax.fori_loop(0, chunks, out_chunk, 0)

    def send_out(k, peer, source):
        remote(out_t.at[peer], out_ref.at[me], ou_s.at[0], ou_r.at[0], peer, j).start()

    def wait_out():
        part = out_t.at[pl.ds(0, n - 1)]
        both(remote(part, part, ou_s.at[0], ou_r.at[0], beside, j))

    peers(send_out)
    own_out = pltpu.make_async_copy(out_t.at[me], out_ref.at[me], loc.at[11])
    own_out.start()

    own_cot.wait()
    wait_cot()
    for i in range(n):
        if turned:
            dy_t[:, i * piece : (i + 1) * piece] = dy_in[i]
            dy[i * piece : (i + 1) * piece, :] = dy_in[i].T
    if not turned:
        dy_t[...] = dy[...].T
    vg[...] = jnp.zeros(vg.shape, F32)
    vg[10:11, :] = colsum(dy[...].astype(F32))

    def scatter(sems, s, cut, direct, bufs, own):
        top = s.shape[2]
        r1, xl, yl, dl, yh, dh, xh = bufs
        low, high = slice(0, cut), slice(cut, top)
        slots = (j, j2)
        count = n if direct else zn
        mine = pl.ds(y0 * zn, zn)
        theirs = pl.ds(y1 * zn, zn)

        def copy(src, dst, t, dp, seq):
            at = sems[t]
            return remote(src, dst, rs_s.at[at], rs_r.at[at], dp, seq)

        def core():
            return [copy(s.at[slot], r1.at[t], t, me, j1) for t, slot in enumerate((j1, j3))]

        def low_x():
            return copy(s.at[j2, :, low], xl, 2, me, j2)

        def low_y():
            return copy(s.at[j, theirs, low], yl, 3, beside, j)

        def high_y():
            return [
                copy(s.at[slot, theirs, high], yh.at[t], 4 + t, beside, j)
                for t, slot in enumerate(slots)
            ]

        def high_x():
            return copy(s.at[j2, here, high], xh, 6, me, j2)

        def out(slot, rows_of, land, t):
            def send(k, peer, to):
                copy(s.at[slot, to, rows_of], land.at[k], t, peer, j).start()

            if direct:
                peers(lambda k, peer, source: send(k, peer, spot(peer)))
            else:
                z_peers(lambda k, peer, to, source: send(k, peer, y0 * zn + to))

        def landed(slot, rows_of, land, t):
            part = land.at[pl.ds(1, count - 1)]
            both(copy(part, part, t, beside, j))
            return lax.fori_loop(
                1,
                count,
                lambda k, v: v + land[k].astype(F32),
                s[slot, here, rows_of].astype(F32),
            )

        def add(slot, start, rows_of, extra):
            def body(i, carry):
                s[slot, start + i, rows_of] = (
                    s[slot, start + i, rows_of].astype(F32) + extra[i].astype(F32)
                ).astype(BF)
                return carry

            lax.fori_loop(0, extra.shape[0], body, 0)

        def one():
            for c in core():
                c.start()

        def two():
            for c in core():
                both(c)
            for t, slot in enumerate(slots):
                add(slot, 0, slice(0, top), r1.at[t])
            if cut < top:
                if direct:
                    for t, slot in enumerate(slots):
                        out(slot, high, dh.at[t], 4 + t)
                else:
                    for c in high_y():
                        c.start()
            if cut > 0:
                low_x().start()

        def low_three():
            both(low_x())
            add(j, 0, low, xl)
            if direct:
                out(j, low, dl, 3)
            else:
                low_y().start()

        def high_three():
            for c in high_y():
                both(c)
            for t, slot in enumerate(slots):
                add(slot, y0 * zn, high, yh.at[t])
                out(slot, high, dh.at[t], 7 + t)

        def low_four():
            both(low_y())
            add(j, y0 * zn, low, yl)
            out(j, low, dl, 9)

        def high_four():
            first = 4 if direct else 7
            own[high, :] = landed(j, high, dh.at[0], first)
            s[j2, here, high] = landed(j2, high, dh.at[1], first + 1).astype(BF)
            high_x().start()

        def low_five():
            own[low, :] = landed(j, low, dl, 3 if direct else 9)

        def high_five():
            both(high_x())
            own[high, :] = own[high, :] + xh[...].astype(F32)

        return one, two, low_three, low_four, low_five, high_three, high_four, high_five

    own_t = own_s.at[0:80, 0:tl]
    own_a = own_s.at[0:80, tl : tl + al]
    own_b = own_s.at[0:80, tl + al : tl + al + bl]
    own_m = own_s.at[96:128, 0:128]
    a_one, a_two, a_three, a_four, a_five, _, _, _ = scatter(
        (0, 1, 2, 3, 0, 0, 0, 0, 0, 4), gf.at[:, :, :, 0:al], 80, False, (ra0, ra1, ra2, ra3, ra4, ra5, ra6), own_a
    )
    b_one, b_two, _, _, _, b_three, b_four, b_five = scatter(
        (5, 6, 0, 0, 7, 8, 9, 10, 11), sb, 0, False, (rb0, rb1, rb2, rb3, rb4, rb5, rb6), own_b
    )
    m_one, m_two, m_three, _, m_five, _, _, _ = scatter(
        (12, 13, 14, 15), gm, 32, True, (rm0, rm1, rm2, rm3, rm4, rm5, rm6), own_m
    )
    t_one, t_two, tl_three, _, tl_five, _, th_four, th_five = scatter(
        (16, 17, 18, 19, 20, 21, 22), gt, CUT, True, (rt0, rt1, rt2, rt3, rt4, rt5, rt6), own_t
    )

    per = 640 // (4 * rb)
    for b in range(2):
        value = nn(dy_t[...], act[side : side + tokens, 640 * b : 640 * b + 640]).astype(BF)
        for ii in range(per):
            i = b * per + ii
            gf[:, place_of(i), :, 0 : 4 * rb] = value[
                :, 4 * rb * ii : 4 * rb * (ii + 1)
            ].reshape(4, 80, 4 * rb)

    a_one()

    def slope_of(at):
        return nn(dy[at, :], w2t[...])

    dz = act
    for at in (0, edge):
        dz[side + at : 2 * side + at, :] = (
            slope_of(slice(at, at + side)) * gp[at : at + side, :].astype(F32)
        ).astype(BF)
    rim_send(dz, dzh, 2)

    def inner_slope(c, carry):
        at = rows(side + c * inner, inner)
        dz[rows(2 * side + c * inner, inner), :] = (
            slope_of(at) * gp[at, :].astype(F32)
        ).astype(BF)
        return carry

    lax.fori_loop(0, 2, inner_slope, 0)

    a_two()

    dhid = gp

    def fold(v):
        return jnp.sum(v.reshape(side // 8, 8, 128), axis=0)

    def back_over(lo, hi, step, first, tiles):
        def back_tile(t, carry):
            lanes = tile_at(t)
            taps = taps_of(lanes)

            def row(at, sums):
                r = lo + at * step
                around = [dz[rows((r + a) * side, side), lanes].astype(F32) for a in range(3)]
                parts = [
                    taps[b] * around[2] + taps[3 + b] * around[1] + taps[6 + b] * around[0]
                    for b in range(3)
                ]
                both_ways = jnp.concatenate([parts[0].astype(BF), parts[2].astype(BF)], axis=0)
                low = (parts[1] + nn(shift_b[...], both_ways)).astype(BF)
                dhid[rows(r * side, side), lanes] = low
                here = around[1]
                sides = nn(shift_m[...], dz[rows((r + 1) * side, side), lanes])
                moved = [sides[0:side], here, sides[side : 2 * side]]
                found = []
                for a in range(3):
                    source = hidp[rows((r + a) * side, side), lanes].astype(F32)
                    for b in range(3):
                        found.append(fold(moved[b] * source))
                found.append(fold(low.astype(F32)))
                found.append(fold(here))
                return tuple(s + f for s, f in zip(sums, found))

            sums = lax.fori_loop(
                0,
                (hi - lo) // step,
                row,
                tuple(jnp.zeros((8, 128), F32) for _ in range(11)),
                unroll=True,
            )
            found = jnp.concatenate([colsum(s) for s in sums] + [jnp.zeros((5, 128), F32)], axis=0)
            hg[:, lanes] = found if first else hg[:, lanes] + found
            return carry

        lax.fori_loop(0, FF // 128, back_tile, 0, unroll=tiles)

    back_over(1, band - 1, 1, True, 1)
    rim_wait(dz, dzh, 2)
    back_over(0, 2 * (band - 1), band - 1, False, 5)

    a_three()
    bn_t = dy_t
    bn_t[...] = bn[...].T
    for b in range(2):
        value = nn(bn_t[...], dhid[:, 640 * b : 640 * b + 640]).T.astype(BF)
        value = value.reshape(2, 4, 80, D)
        for i in range(n):
            sb[2 * b : 2 * b + 2, place_of(i), :, 0 : 4 * rb] = jnp.concatenate(
                [value[:, v, :, rb * i : rb * i + rb] for v in range(4)], axis=2
            )

    zero_row = jnp.zeros((1, D), F32)
    dbr = bn
    dbr_t = dy_t

    def back_middle(c, carry):
        at = rows(c * QC, QC)
        value, in_gain, in_shift = norm_back(mid[at, :], gain(2), nn(dhid[at, :], w1t[...]))
        value = value + dy[at, :].astype(F32)
        mid[at, :] = value
        low = value.astype(BF)
        dbr[at, :] = low
        dbr_t[:, across(c)] = low.T
        spread = nt(wop[...], low)
        for h in range(HEADS):
            tile = spread[128 * h : 128 * h + 128, :] * rtot[h, :, across(c)]
            tile_low = tile.astype(BF)
            qt[h, :, across(c)] = tile_low
            datn[h, at, :] = tile_low.T
            delta[h, :, across(c)] = colsum(
                tile_low[64:128, :].astype(F32)
                * att_t[HEAD * h : HEAD * h + HEAD, across(c)].astype(F32)
            )
        return (carry[0] + in_gain, carry[1] + in_shift, carry[2] + colsum(low.astype(F32)))

    sums = lax.fori_loop(0, chunks, back_middle, (zero_row, zero_row, zero_row))
    vg[2:3, :] = sums[0]
    vg[9:10, :] = sums[1]
    vg[8:9, :] = sums[2]
    value = nn(dbr_t[...], att_n[...]).astype(BF)
    for i in range(n):
        sb[:, place_of(i), :, 4 * rb : 5 * rb] = value[:, rb * i : rb * i + rb].reshape(
            4, 80, rb
        )
    b_one()
    a_four()

    def dkv(h, slot):
        return act.at[rows(slot * keys, keys), tile_at(h)]

    def dk_core(h):
        return [
            remote(dkv(h, slot), rk1.at[h, t], dk_s.at[h, t], dk_r.at[h, t], me, j1)
            for t, slot in enumerate((j1, j3))
        ]

    def dk_x(h):
        return remote(dkv(h, j2), rk2.at[h], dk_s.at[h, 2], dk_r.at[h, 2], me, j2)

    def dk_two(h):
        for copy in dk_core(h):
            both(copy)
        for t, slot in enumerate((j, j2)):
            part = dkv(h, slot)
            part[...] = (part[...].astype(F32) + rk1[h, t].astype(F32)).astype(BF)
        dk_x(h).start()

    def dk_three(h):
        both(dk_x(h))
        qnat[h, 0:keys, :] = (dkv(h, j)[...].astype(F32) + rk2[h].astype(F32)).astype(BF)

    def back_head(h, carry):
        tile = kv[h].reshape(4 * keys, 128)
        total = None
        for c in range(tokens // qa):
            cut = slice(c * qa, (c + 1) * qa)
            powers = prob[h, :, cut]
            slopes = nn(tile, qt[h, :, cut]) - delta[h, :, cut]
            ds = (powers.astype(F32) * slopes).astype(BF)
            part = nn(ds, qnat[h, cut, :]) + nn(powers, datn[h, cut, :])
            prob[h, :, cut] = ds
            total = part if total is None else total + part
        act[0 : 4 * keys, tile_at(h)] = total.astype(BF)
        for copy in dk_core(h):
            copy.start()

        @pl.when(h == 1)
        def _():
            b_two()

        @pl.when(h >= 1)
        def _():
            dk_two(h - 1)

        return carry

    lax.fori_loop(0, HEADS, back_head, 0)

    dq_t = att_t

    def back_query(h, carry):
        for c in range(tokens // qa):
            cut = slice(c * qa, (c + 1) * qa)
            dq_t[rows(h * HEAD, HEAD), cut] = (
                nn(kvt[h, 0:64, :], prob[h, :, cut]) * HEAD**-0.5
            ).astype(BF)
        return carry

    lax.fori_loop(0, 2, back_query, 0)
    dk_two(HEADS - 1)
    b_three()
    for h in range(HEADS - 2):
        dk_three(h)
    lax.fori_loop(2, HEADS, back_query, 0)
    dq = att_n

    def flip(c, total):
        low = dq_t[:, across(c)].T
        dq[rows(c * QC, QC), :] = low
        return total + colsum(low.astype(F32))

    vg[4:5, :] = lax.fori_loop(0, chunks, flip, zero_row)
    value = nn(dq_t[...], abf[...]).astype(BF)
    for i in range(n):
        part = value[:, rb * i : rb * i + rb].reshape(4, 80, rb)
        gm[:, place_of(i), :, 0 : 3 * rb] = jnp.concatenate(
            [
                part[:, 0:32],
                part[:, 32:64],
                jnp.concatenate([part[:, 64:80], jnp.zeros((4, 16, rb), BF)], axis=1),
            ],
            axis=2,
        )
    dk_three(HEADS - 2)
    dk_three(HEADS - 1)

    dm = jnp.concatenate([qnat[h, 0:keys, :] for h in range(HEADS)], axis=1)
    dm_sum = colsum(dm.astype(F32))
    vg[7:8, :] = jnp.concatenate(
        [dm_sum[:, 128 * h + 64 : 128 * h + 128] for h in range(HEADS)], axis=1
    )
    dv, in_gain, in_shift = norm_back(red_s[...], gain(1), nn(dm, wmt[...]))
    vg[1:2, :] = in_gain
    vg[6:7, :] = in_shift
    dred = dv.astype(BF)
    vg[5:6, :] = colsum(dred.astype(F32))
    dred_t = dred.T
    for dd in range(4):
        value = nn(dred_t, pat[dd]).astype(BF)
        count = n // 4
        for ii in range(count):
            i = dd * count + ii
            gt[:, place_of(i), :, 0 : 4 * rb] = value[
                :, 4 * rb * ii : 4 * rb * (ii + 1)
            ].reshape(4, 80, 4 * rb)
    value = nn(dm.T, memin[...]).astype(BF)
    value = jnp.concatenate(
        [value[128 * h : 128 * h + 64] for h in range(HEADS)]
        + [value[128 * h + 64 : 128 * h + 128] for h in range(HEADS)],
        axis=0,
    ).reshape(4, 2, 80, D)
    for i in range(n):
        gt[:, place_of(i), :, 4 * rb : 6 * rb] = jnp.concatenate(
            [value[:, v, :, rb * i : rb * i + rb] for v in range(2)], axis=2
        )
    t_one()

    m_one()
    t_two()

    for dd in range(4):
        back = nn(dred, wrt[dd])
        back = jnp.concatenate([back, jnp.zeros((keys, 64), F32)], axis=1)
        for i in range(band // 2):
            start = (2 * i + dd // 2) * side + dd % 2
            for t in range(3):
                a3[t, pl.ds(start, half, stride=2), :] = back[
                    i * half : (i + 1) * half, 128 * t : 128 * t + 128
                ]
    m_two()

    def back_first(c, carry):
        at = rows(c * QC, QC)
        e = nn(dq[at, :], wqt[...]) + jnp.concatenate([a3[t, at, :] for t in range(3)], axis=1)[:, 0:D]
        value, in_gain, in_shift = norm_back(x_s[at, :].astype(F32), gain(0), e)
        bn[at, :] = (mid[at, :] + value).astype(BF)
        return (carry[0] + in_gain, carry[1] + in_shift)

    sums = lax.fori_loop(0, chunks, back_first, (zero_row, zero_row))
    token_out = pltpu.make_async_copy(bn, tgrad_ref, loc.at[12])
    token_out.start()
    vg[0:1, :] = sums[0]
    vg[3:4, :] = sums[1]
    for i in range(n):
        sv[place_of(i), :, 0 : 4 * rb] = hg[:, 4 * rb * i : 4 * rb * (i + 1)].astype(BF)
        sv[place_of(i), :, 4 * rb : 5 * rb] = vg[:, rb * i : rb * i + rb].astype(BF)

    def v_out(k, peer, source):
        remote(sv.at[spot(peer)], rv1.at[k], rs_s.at[23], rs_r.at[23], peer, j).start()

    peers(v_out)
    tl_three()
    b_four()
    m_three()
    part = rv1.at[pl.ds(1, n - 1)]
    both(remote(part, part, rs_s.at[23], rs_r.at[23], beside, j))
    rv2[j] = lax.fori_loop(
        1, n, lambda k, total: total + rv1[k].astype(F32), sv[here].astype(F32)
    ).astype(BF)

    def v_seq(t, slot, other):
        ref = rv2.at[slot]
        return remote(ref, ref, rs_s.at[24 + t], rs_r.at[24 + t], me, other)

    for t, other in enumerate((j1, j2, j3)):
        v_seq(t, j, other).start()
    th_four()
    a_five()
    b_five()
    squares = jnp.sum(own_a[:, 0 : 4 * rb] * own_a[:, 0 : 4 * rb])
    squares += jnp.sum(own_b[:, 0 : 5 * rb] * own_b[:, 0 : 5 * rb])
    th_five()
    m_five()
    squares += jnp.sum(own_m[:, 0 : 2 * rb] * own_m[:, 0 : 2 * rb])
    squares += jnp.sum(own_m[0:16, 2 * rb : 3 * rb] * own_m[0:16, 2 * rb : 3 * rb])
    tl_five()
    squares += jnp.sum(own_t[:, 0 : 6 * rb] * own_t[:, 0 : 6 * rb])
    for t, other in enumerate((j1, j2, j3)):
        v_seq(t, other, other).wait_send()
        v_seq(t, other, other).wait_recv()
    own_v = (rv2[0].astype(F32) + rv2[1].astype(F32)) + (rv2[2].astype(F32) + rv2[3].astype(F32))
    own_s[80:96, 0:vl] = own_v
    first_band = (j == 0).astype(jnp.int32).astype(F32)
    squares += first_band * jnp.sum(own_v[0:11, 0 : 5 * rb] * own_v[0:11, 0 : 5 * rb])

    nrm[4 * me + j] = jnp.full((8, 128), squares, F32)
    own_out_copy = pltpu.make_async_copy(own_s, own_ref, loc.at[13])
    own_out_copy.start()

    def send_norm(k, carry):
        mine = 4 * me + j
        to = lax.rem(mine + k, 4 * n)
        remote(
            nrm.at[mine], nrm.at[mine], nd_s.at[0], nd_r.at[0], lax.div(to, 4), lax.rem(to, 4)
        ).start()
        return carry

    lax.fori_loop(1, 4 * n, send_norm, 0)
    part = nrm.at[pl.ds(0, 4 * n - 1)]
    both(remote(part, part, nd_s.at[0], nd_r.at[0], beside, j))
    nrm[4 * n] = lax.fori_loop(1, 4 * n, lambda k, total: total + nrm[k], nrm[0])
    norm_out = pltpu.make_async_copy(nrm.at[4 * n], norm_ref, loc.at[14])
    norm_out.start()

    wait_out()
    own_out.wait()
    token_out.wait()
    own_out_copy.wait()
    norm_out.wait()


def update_kernel(rb, tl, al, rates, decays, *refs):
    own_hbm, total_hbm, outt_hbm, tg_hbm = refs[0:4]
    in_hbm = refs[4:31]
    out_hbm, tok_hbm, norm_hbm = refs[31:34]
    new_hbm = refs[34:61]
    own_ref, total_ref, out_v, tok_v, norm_v = refs[61:66]
    in_v, new_v = refs[66:93], refs[93:120]
    in_sem, out_sem = refs[120:122]
    loads = [
        pltpu.make_async_copy(src, dst, in_sem.at[at])
        for at, (src, dst) in enumerate(
            [
                (own_hbm, own_ref),
                *zip(in_hbm, in_v),
                (outt_hbm, out_v),
                (tg_hbm, tok_v),
                (total_hbm, total_ref),
            ]
        )
    ]
    for load in loads:
        load.start()
    stores = [
        pltpu.make_async_copy(src, dst, out_sem.at[at])
        for at, (src, dst) in enumerate(
            [*zip(new_v, new_hbm), (out_v, out_hbm), (tok_v, tok_hbm), (norm_v, norm_hbm)]
        )
    ]
    loads[0].wait()
    loads[30].wait()
    total = total_ref[0:1, :]
    norm = jnp.sqrt(total)
    norm_v[...] = norm
    stores[29].start()
    clip = jnp.minimum(1.0, MAX_NORM / (norm + 1e-06))[:, 0:1]
    turned_t = own_ref[0:80, 0:tl].T
    turned_a = own_ref[0:80, tl : tl + al].T
    turned_b = own_ref[0:80, tl + al :].T
    turned_q = jnp.concatenate(
        [
            own_ref[96:128, 0:rb],
            own_ref[96:128, rb : 2 * rb],
            own_ref[96:112, 2 * rb : 3 * rb],
        ],
        axis=0,
    ).T
    grads = (
        turned_q,
        turned_t[0 : 4 * rb],
        jnp.concatenate([turned_t[(4 + v) * rb : (5 + v) * rb] for v in range(2)], axis=1),
        turned_b[4 * rb : 5 * rb],
        jnp.concatenate([turned_b[v * rb : (v + 1) * rb] for v in range(4)], axis=1),
        turned_a[0 : 4 * rb],
        own_ref[80:83, 4 * rb : 5 * rb],
        own_ref[83:91, 4 * rb : 5 * rb],
        own_ref[80:91, 0 : 4 * rb],
    )
    for at in range(9):
        for part in range(3):
            loads[1 + at + 9 * part].wait()
        clipped = clip * grads[at]
        weight = in_v[at][...]
        first = BETA_ONE * in_v[9 + at][...] + (1.0 - BETA_ONE) * clipped
        second = BETA_TWO * in_v[18 + at][...] + (1.0 - BETA_TWO) * clipped * clipped
        direction = (
            first
            / (1.0 - BETA_ONE**STEP)
            / (jnp.sqrt(second / (1.0 - BETA_TWO**STEP)) + ADAM_EPS)
        )
        new_v[at][...] = weight - rates[at] * (direction + decays[at] * weight)
        new_v[9 + at][...] = first
        new_v[18 + at][...] = second
        for part in range(3):
            stores[at + 9 * part].start()
    for at in (28, 29):
        loads[at].wait()
        stores[at - 1].start()
    for store in stores:
        store.wait()


def on_device(n, *args):
    tokens, buckets, cotangent = args[0:3]
    weights, firsts, seconds = args[3:12], args[12:21], args[21:30]
    band, side, width = tokens.shape[1:4]
    count = band * side
    keys = count // 4
    rb = weights[0].shape[0]
    piece = cotangent.shape[3]
    wide = up(9 * rb, 128)
    tl = up(6 * rb, 128)
    al = up(4 * rb, 128)
    bl = up(5 * rb, 128)
    h = n // 2
    vl = up(5 * rb, 128)
    total = tl + al + bl
    qa = count if n <= 8 else 256
    turned = piece % 128 == 0
    block = (n, D, piece) if turned else (n, piece, D)
    vm = pltpu.VMEM
    dma = pltpu.SemaphoreType.DMA
    def landing(height, lanes, cut, direct):
        rest = height - cut
        count = n if direct else h
        shapes = (
            (2, n, height, lanes),
            (n, cut, lanes),
            (0 if direct else h, cut, lanes),
            (count, cut, lanes),
            (0 if direct else 2, h, rest, lanes),
            (2, count, rest, lanes),
            (rest, lanes),
        )
        return [vm(shape if 0 not in shape else (8, 128), BF) for shape in shapes]

    scratch = [
        vm((count, D), BF),
        *[vm(weights[at].shape, F32) for at in range(9)],
        vm((n, 16, vl), BF),
        vm((4, n, 80, tl), BF),
        vm((4, n, 32, 128), BF),
        vm((4, n, 80, wide), BF),
        vm((16, D), F32),
        vm((16, FF), F32),
        vm((D, D), BF),
        vm((D, D), BF),
        vm((2 * D, D), BF),
        vm((2 * D, D), BF),
        vm((4, D, D), BF),
        vm((FF, D), BF),
        vm((D, FF), BF),
        vm((3, count, 128), F32),
        vm((count, D), BF),
        vm((4, keys, D), BF),
        vm((keys, D), F32),
        vm((keys, D), BF),
        vm((HEADS, 4, keys, 128), BF),
        vm((HEADS, 128, 4 * keys), BF),
        vm((HEADS, count, 128), BF),
        vm((HEADS, 128, count), BF),
        vm((HEADS, 4 * keys, count), BF),
        vm((D, count), BF),
        vm((count, D), BF),
        vm((HEADS, 1, count), F32),
        vm((HEADS, 1, count), F32),
        vm((count, D), F32),
        vm((count, D), BF),
        vm((count + 2 * side, FF), BF),
        vm((2, side, FF), BF),
        vm((count + 2 * side, FF), BF),
        vm((count, FF), BF),
        vm(block, BF),
        vm(block if turned else (8, 128), BF),
        vm((D, count), BF),
        vm((count, D), BF),
        vm((2, side, FF), BF),
        vm((HEADS, count, 128), BF),
        vm((HEADS, 2, keys, 128), BF),
        vm((HEADS, keys, 128), BF),
        vm((16, FF), F32),
        vm((16, D), F32),
        vm((128, total), F32),
        vm((4, n, 80, bl), BF),
        *landing(80, al, 80, False),
        *landing(80, bl, 0, False),
        *landing(80, tl, CUT, True),
        *landing(32, 128, 32, True),
        vm((n, 16, vl), BF),
        vm((n, 16, vl), BF),
        vm((4, 16, vl), BF),
        vm((4 * n + 1, 8, 128), F32),
        vm((side, 2 * side), BF),
        vm((side, 2 * side), BF),
        vm((2 * side, side), BF),
        dma((15,)),
        *[dma((9,)) for _ in range(2)],
        *[dma((16,)) for _ in range(2)],
        *[dma((1,)) for _ in range(4)],
        *[dma((HEADS, 3)) for _ in range(2)],
        *[dma((4,)) for _ in range(2)],
        *[dma((HEADS, 3)) for _ in range(2)],
        *[dma((27,)) for _ in range(2)],
        *[dma((1,)) for _ in range(2)],
    ]
    anywhere = pl.BlockSpec(memory_space=pl.ANY)
    out_t, token_grad, own, total_squares = pl.pallas_call(
        functools.partial(block_kernel, n, side, band, qa),
        out_shape=(
            jax.ShapeDtypeStruct(block, BF),
            jax.ShapeDtypeStruct((count, D), BF),
            jax.ShapeDtypeStruct((128, total), F32),
            jax.ShapeDtypeStruct((8, 128), F32),
        ),
        in_specs=[pl.BlockSpec(memory_space=pltpu.SMEM)] + [anywhere] * 11,
        out_specs=(anywhere,) * 4,
        scratch_shapes=scratch,
        compiler_params=pltpu.CompilerParams(
            collective_id=0, has_side_effects=True, vmem_limit_bytes=VMEM_LIMIT
        ),
    )(
        buckets,
        tokens.reshape(count, width),
        jnp.swapaxes(cotangent, 3, 4).reshape(block) if turned else cotangent.reshape(block),
        *weights,
    )
    rates = (
        D ** (-0.5),
        (4 * D) ** (-0.5),
        D ** (-0.5),
        OUT_FAN ** (-0.5),
        D ** (-0.5),
        FF ** (-0.5),
        GAIN_RATE,
        VECTOR_RATE,
        VECTOR_RATE,
    )
    decays = (DECAY_RATE,) * 6 + (0.0,) * 3
    shapes = tuple(jax.ShapeDtypeStruct(w.shape, F32) for w in weights)
    results = pl.pallas_call(
        functools.partial(update_kernel, rb, tl, al, rates, decays),
        out_shape=(
            jax.ShapeDtypeStruct(block, BF),
            jax.ShapeDtypeStruct((count, D), BF),
            jax.ShapeDtypeStruct((1, 128), F32),
        )
        + shapes * 3,
        in_specs=[anywhere] * 31,
        out_specs=(anywhere,) * 30,
        scratch_shapes=[
            vm((128, total), F32),
            vm((8, 128), F32),
            vm(block, BF),
            vm((count, D), BF),
            vm((1, 128), F32),
            *[vm(w.shape, F32) for w in weights * 6],
            dma((31,)),
            dma((30,)),
        ],
    )(own, total_squares, out_t, token_grad, *weights, *firsts, *seconds)
    if turned:
        block_output = jnp.swapaxes(results[0].reshape(n, 1, 1, width, piece), 3, 4)
    else:
        block_output = results[0].reshape(n, 1, 1, piece, width)
    return (
        block_output,
        results[1].reshape(1, band, side, width),
        results[2][0, 0],
        *results[3:],
    )


def solution(mesh):
    matrix = (P("dp", "seq"),) * 6 + (P(None, "dp"),) * 3
    return jax.shard_map(
        functools.partial(on_device, mesh.shape["dp"]),
        mesh=mesh,
        in_specs=(
            P("dp", "seq", None, None),
            P("dp"),
            P(None, "seq", "dp", None, None),
            *(matrix * 3),
        ),
        out_specs=(
            P(None, "seq", "dp", None, None),
            P("dp", "seq", None, None),
            P(),
            *(matrix * 3),
        ),
        check_vma=False,
    )
```

time: 146 us -> 125 us (0.86)
  Pallas kernels: 144 us -> 123 us
    pallas_call x1, Pallas kernels: 140 us -> 119 us  [on_device(): pl.pallas_call(functools.partial(block_kernel, n, side, band, qa), out_sh...]
where the time goes in v3:
time: 125 us
  Pallas kernels  123 us (98%)
  between operations  1.48 us (1%)
    pallas_call x1, Pallas kernels, on_device(): pl.pallas_call(functools.partial(block_kernel, n, side, band, qa), out_sh...  119 us
    pallas_call x1, Pallas kernels, on_device(): pl.pallas_call(functools.partial(update_kernel, rb, tl, al, rates, decays...  4.29 us

profile of v3, /device:TPU:0, one launch (start us, length us, event | category | flops | bytes accessed | tf_op | source)
XLA Modules:
  0.0 124.8 jit_solution(12314033416085581452)
XLA Ops:
  1.3 119.0 %shard_map.517 = (bf16[8,320,128]{2,1,0:T(8,128)(2,1)}, bf16[1024,320]{1,0:T(8,128)(2,1)}, f32[128,768]{1,0:T(8,128)}, f32[8,128]{1,0:T(8,128)}) custom-call(s32[1]{0:T(128)S(6)} %copy.62.bucket_ref, bf16[1024,320]{1,0:T(8,128)(2,1)} %bitcast.14, bf16[8,320,128]{2,1,0:T(8,128)(2,1)} %bitcast.15, f32[40,80]{1,0:T(8,128)} %refs_4_.1, f32[160,80]{1,0:T(8,128)} %refs_5_.1, ...), custom_call_target="tpu_custom_call" | custom-call | tf_op jit(solution)/shard_map/pallas_call | solution.py:1465
  120.3 4.3 %shard_map.518 = (bf16[8,320,128]{2,1,0:T(8,128)(2,1)}, bf16[1024,320]{1,0:T(8,128)(2,1)}, f32[1,128]{1,0:T(1,128)}, f32[40,80]{1,0:T(8,128)}, f32[160,80]{1,0:T...) custom-call(f32[128,768]{1,0:T(8,128)} %get-tuple-element.64.refs_0_, ...), custom_call_target="tpu_custom_call" | custom-call | tf_op jit(solution)/shard_map/pallas_call | solution.py:1498

commit v4 on v3

--- a/solution.py
+++ b/solution.py
@@ -116,7 +116,6 @@
     a3,
     abf,
     pat,
-    red_s,
     memin,
     kv,
     kvt,
@@ -183,6 +182,8 @@
     loc,
     gd_s,
     gd_r,
+    tl_r,
+    th_r,
     gx_s,
     gx_r,
     co_s,
@@ -193,8 +194,6 @@
     kv_r,
     ha_s,
     ha_r,
-    dk_s,
-    dk_r,
     rs_s,
     rs_r,
     nd_s,
@@ -220,6 +219,7 @@
     j3 = 3 - j
     tokens = band * side
     chunks = tokens // QC
+    deep = band if qa == tokens else 4
     rb = wq_ref.shape[0]
     piece = tokens // n
     keys = kv.shape[2]
@@ -229,6 +229,8 @@
     vl = gvec.shape[2]
     al = up(4 * rb, 128)
     bl = sb.shape[3]
+    ml = gm.shape[3]
+    mo = 128 if ml > 128 else 3 * rb
 
     def remote(src, dst, ss, rs, dp, seq):
         return pltpu.make_async_remote_copy(
@@ -354,19 +356,73 @@
     upper = slice(CUT, 80)
     every = slice(0, 16)
     v_dp, v_dp_wait = over_dp(0, gvec, every)
-    t_dp, t_dp_wait = over_dp(1, gt.at[j], lower)
-    t_x, t_x_wait = swap(0, gt.at[j, :, lower], gt.at[j2, :, lower], me, j2)
+
+    def t_low(i):
+        return gt.at[j, i, lower]
+
+    def t_low_copy(k, i, peer):
+        return remote(t_low(i), t_low(i), gd_s.at[1], tl_r.at[k], peer, j)
+
+    def t_low_on(i):
+        remote(t_low(i), t_low(i), gx_s.at[0], gx_r.at[0], me, j2).start()
+
+    def t_low_start():
+        t_low_on(here)
+        peers(lambda k, peer, source: t_low_copy(k, here, peer).start())
+
+    def t_low_forward():
+        def body(k, peer, source):
+            t_low_copy(k, spot(source), peer).wait_recv()
+            t_low_on(spot(source))
+
+        peers(body)
+
+    def t_low_wait():
+        part = gt.at[j, pl.ds(0, n - 1), lower]
+        remote(part, part, gd_s.at[1], tl_r.at[0], beside, j).wait_send()
+        both(remote(gt.at[j, :, lower], gt.at[j2, :, lower], gx_s.at[0], gx_r.at[0], me, j2))
+
     t_x0, t_x0_wait = swap(1, gt.at[j, here, upper], gt.at[j2, here, upper], me, j2)
-    t_za, t_za_wait = over_z(2, gt.at[j], upper)
-    t_zb, t_zb_wait = over_z(3, gt.at[j2], upper)
-    t_ya, t_ya_wait = over_y(2, gt.at[j], upper)
-    t_yb, t_yb_wait = over_y(3, gt.at[j2], upper)
+
+    def t_high(slot, t):
+        def ref(i):
+            return gt.at[slot, i, upper]
+
+        def copy(k, i, peer):
+            return remote(ref(i), ref(i), gd_s.at[2 + t], th_r.at[t, k], peer, j)
+
+        def on(i):
+            remote(ref(i), ref(i), gx_s.at[2 + t], gx_r.at[2 + t], beside, j).start()
+
+        def start():
+            z_peers(lambda k, peer, to, source: copy(k, here, peer).start())
+            on(here)
+
+        def forward():
+            def body(k, peer, to, source):
+                copy(k, y0 * zn + source, peer).wait_recv()
+                on(y0 * zn + source)
+
+            z_peers(body)
+
+        def wait():
+            part = gt.at[slot, pl.ds(0, zn - 1), upper]
+            remote(part, part, gd_s.at[2 + t], th_r.at[t, 0], beside, j).wait_send()
+            mine = gt.at[slot, pl.ds(y0 * zn, zn), upper]
+            theirs = gt.at[slot, pl.ds(y1 * zn, zn), upper]
+            both(remote(mine, theirs, gx_s.at[2 + t], gx_r.at[2 + t], beside, j))
+
+        return start, forward, wait
+
+    t_za, t_za_forward, t_ya_wait = t_high(j, 0)
+    t_zb, t_zb_forward, t_yb_wait = t_high(j2, 1)
     t_ca, t_ca_wait = swap(4, gt.at[j], gt.at[j1], me, j1)
     t_cb, t_cb_wait = swap(5, gt.at[j2], gt.at[j3], me, j1)
-    m_dp, m_dp_wait = over_dp(4, gm.at[j], slice(0, 32))
-    m_x, m_x_wait = swap(6, gm.at[j], gm.at[j2], me, j2)
-    m_ca, m_ca_wait = swap(7, gm.at[j], gm.at[j1], me, j1)
-    m_cb, m_cb_wait = swap(8, gm.at[j2], gm.at[j3], me, j1)
+    wq_block = gm.at[:, :, :, 0:128]
+    m_dp, m_dp_wait = over_dp(4, wq_block.at[j], slice(0, 32))
+    m_x, m_x_wait = swap(6, wq_block.at[j], wq_block.at[j2], me, j2)
+    m_ca, m_ca_wait = swap(7, wq_block.at[j], wq_block.at[j1], me, j1)
+    m_cb, m_cb_wait = swap(8, wq_block.at[j2], wq_block.at[j3], me, j1)
     f_x0, f_x0_wait = swap(9, gf.at[j, here], gf.at[j2, here], me, j2)
     fl_za, fl_za_wait = over_z(5, gf.at[j], lower)
     fl_zb, fl_zb_wait = over_z(6, gf.at[j2], lower)
@@ -381,13 +437,13 @@
 
     pl.semaphore_wait(barrier, 4 * n - 1)
     t_x0()
-    v_dp()
-    t_dp()
+    t_za()
+    t_low_start()
 
     for copy in loads[5:9]:
         copy.wait()
     wq_t = fq[...].T
-    gm[j, here] = jnp.concatenate(
+    gm[j, here, :, 0:128] = jnp.concatenate(
         [
             wq_t[0:32],
             wq_t[32:64],
@@ -403,12 +459,18 @@
         + [fo[...].T, jnp.zeros((80, fl - 9 * rb), F32)],
         axis=1,
     ).astype(BF)
+    t_x0_wait()
+    t_zb()
+    v_dp()
+    m_dp()
     f_x0()
-    t_x0_wait()
-    t_za()
-    t_zb()
-    m_dp()
-
+
+    t_low_forward()
+    t_za_forward()
+    t_zb_forward()
+    f_x0_wait()
+    fl_za()
+    fl_zb()
     v_dp_wait()
     hp[...] = jnp.concatenate([gvec[place_of(i), :, 0 : 4 * rb] for i in range(n)], axis=1).astype(F32)
     vp[...] = jnp.concatenate(
@@ -477,22 +539,11 @@
         (j < 3).astype(jnp.int32) * (1 - bucket * ((j + 1) * band == half).astype(jnp.int32))
     ).astype(F32)
 
-    t_dp_wait()
-    t_x()
-    t_za_wait()
-    t_zb_wait()
-    t_ya()
-    t_yb()
-    f_x0_wait()
-    fl_za()
-    fl_zb()
-    fh_za()
-    fh_zb()
+    m_dp_wait()
+    m_x()
     t_ya_wait()
     t_yb_wait()
-    m_dp_wait()
-    m_x()
-    t_x_wait()
+    t_low_wait()
     t_ca()
     t_cb()
     m_x_wait()
@@ -520,7 +571,9 @@
     red = shift(2) + nt(pat[0], wrt[0])
     for dd in range(1, 4):
         red = red + nt(pat[dd], wrt[dd])
-    red_s[...] = red
+    wide_red = jnp.concatenate([red, jnp.zeros((keys, 64), F32)], axis=1)
+    for t in range(3):
+        a3[t, 0:keys, :] = wide_red[:, 128 * t : 128 * t + 128]
     vhat, _ = norm_parts(red)
     low = (vhat * gain(1) + shift(3)).astype(BF)
     memin[...] = low
@@ -547,12 +600,8 @@
         kv_copy(h, j, 1, j1).start()
         return carry
 
-    lax.fori_loop(0, HEADS, kv_send, 0)
-
-    fl_za_wait()
-    fl_zb_wait()
-    fl_ya()
-    fl_yb()
+    lax.fori_loop(0, 2, kv_send, 0)
+
     wqp = wop
     m_ca_wait()
     m_cb_wait()
@@ -591,6 +640,7 @@
         return carry
 
     lax.fori_loop(0, chunks, queries, 0)
+    lax.fori_loop(2, HEADS, kv_send, 0)
 
     def send_cot(k, peer, source):
         remote(cot_ref.at[peer], incoming(me), co_s.at[0], co_r.at[0], peer, j).start()
@@ -603,16 +653,15 @@
         kv_copy(h, j2, 0, j2).wait_recv()
         kv_copy(h, j2, 2, j1).start()
 
+    fl_za_wait()
+    fl_zb_wait()
+    fl_ya()
+    fl_yb()
+    fh_za()
+    fh_zb()
     kv_forward(0)
 
     def attend(h, carry):
-        @pl.when(h == 1)
-        def _():
-            fh_za_wait()
-            fh_zb_wait()
-            fh_ya()
-            fh_yb()
-
         @pl.when(h == HEADS - 1)
         def _():
             fl_ya_wait()
@@ -640,6 +689,13 @@
                 @pl.when(h < HEADS - 1)
                 def _():
                     kv_forward(h + 1)
+
+                @pl.when(h == 1)
+                def _():
+                    fh_za_wait()
+                    fh_zb_wait()
+                    fh_ya()
+                    fh_yb()
 
             largest = jnp.max(scores, axis=0, keepdims=True)
             powers = jnp.exp(scores - largest).astype(BF)
@@ -921,19 +977,112 @@
     own_t = own_s.at[0:80, 0:tl]
     own_a = own_s.at[0:80, tl : tl + al]
     own_b = own_s.at[0:80, tl + al : tl + al + bl]
-    own_m = own_s.at[96:128, 0:128]
+    own_m = own_s.at[96:128, 0:ml]
     a_one, a_two, a_three, a_four, a_five, _, _, _ = scatter(
         (0, 1, 2, 3, 0, 0, 0, 0, 0, 4), gf.at[:, :, :, 0:al], 80, False, (ra0, ra1, ra2, ra3, ra4, ra5, ra6), own_a
     )
-    b_one, b_two, _, _, _, b_three, b_four, b_five = scatter(
-        (5, 6, 0, 0, 7, 8, 9, 10, 11), sb, 0, False, (rb0, rb1, rb2, rb3, rb4, rb5, rb6), own_b
+    b_one, b_two, bl_three, bl_four, bl_five, bh_three, bh_four, bh_five = scatter(
+        (5, 6, 27, 28, 7, 8, 9, 10, 11, 29), sb, 32, False, (rb0, rb1, rb2, rb3, rb4, rb5, rb6), own_b
     )
-    m_one, m_two, m_three, _, m_five, _, _, _ = scatter(
-        (12, 13, 14, 15), gm, 32, True, (rm0, rm1, rm2, rm3, rm4, rm5, rm6), own_m
+    m_one, m_two, m_three, m_four, m_five, _, _, _ = scatter(
+        (12, 13, 14, 15, 0, 0, 0, 0, 0, 33), gm, 32, False, (rm0, rm1, rm2, rm3, rm4, rm5, rm6), own_m
     )
-    t_one, t_two, tl_three, _, tl_five, _, th_four, th_five = scatter(
-        (16, 17, 18, 19, 20, 21, 22), gt, CUT, True, (rt0, rt1, rt2, rt3, rt4, rt5, rt6), own_t
-    )
+    def t_core(t, slot, to, rows_of):
+        return remote(
+            gt.at[slot, :, rows_of], rt0.at[to, :, rows_of], rs_s.at[16 + t], rs_r.at[16 + t], me, j1
+        )
+
+    def t_cores():
+        return (
+            t_core(0, j3, 1, lower),
+            t_core(1, j1, 0, upper),
+            t_core(2, j3, 1, upper),
+            t_core(3, j1, 0, lower),
+        )
+
+    def t_add(slot, start, count, rows_of, extra):
+        def body(i, carry):
+            gt[slot, start + i, rows_of] = (
+                gt[slot, start + i, rows_of].astype(F32) + extra[start + i, rows_of].astype(F32)
+            ).astype(BF)
+            return carry
+
+        lax.fori_loop(0, count, body, 0)
+
+    def t_half(t):
+        part = pl.ds((y1 if t == 0 else y0) * zn, zn)
+        return remote(
+            gt.at[j2, part, lower], rt1.at[part], rs_s.at[20 + t], rs_r.at[20 + t], me, j2
+        )
+
+    def t_dp(slot, i, rows_of, land, sem, k, peer):
+        remote(
+            gt.at[slot, i, rows_of], land.at[k], rs_s.at[sem], rs_r.at[sem], peer, j
+        ).start()
+
+    def t_landed(slot, rows_of, land, sem):
+        part = land.at[pl.ds(1, n - 1)]
+        both(remote(part, part, rs_s.at[sem], rs_r.at[sem], beside, j))
+        return lax.fori_loop(
+            1, n, lambda k, v: v + land[k].astype(F32), gt[slot, here, rows_of].astype(F32)
+        )
+
+    def t_one():
+        for c in t_cores():
+            c.start()
+
+    def t_two():
+        cores = t_cores()
+        both(cores[0])
+        t_add(j2, 0, n, lower, rt0.at[1])
+        t_half(0).start()
+        t_half(1).start()
+        both(cores[1])
+        both(cores[2])
+        for t, slot in enumerate((j, j2)):
+            t_add(slot, 0, n, upper, rt0.at[t])
+            peers(
+                lambda k, peer, source: t_dp(
+                    slot, spot(peer), upper, rt5.at[t], 22 + t, k, peer
+                )
+            )
+        both(cores[3])
+        t_add(j, 0, n, lower, rt0.at[0])
+
+    def tl_three(t):
+        both(t_half(t))
+        start = (y1 if t == 0 else y0) * zn
+
+        def body(i, carry):
+            at = start + i
+            gt[j, at, lower] = (gt[j, at, lower].astype(F32) + rt1[at].astype(F32)).astype(BF)
+            return carry
+
+        lax.fori_loop(0, zn, body, 0)
+
+        def send(i, carry):
+            k = 2 * i + (1 if t == 0 else 2)
+            peer = lax.rem(me + k, n)
+            t_dp(j, spot(peer), lower, rt3, 24, k, peer)
+            return carry
+
+        lax.fori_loop(0, zn if t == 0 else zn - 1, send, 0)
+
+    def th_x():
+        return remote(gt.at[j2, here, upper], rt6, rs_s.at[25], rs_r.at[25], me, j2)
+
+    def th_four():
+        own_t[upper, :] = t_landed(j, upper, rt5.at[0], 22)
+        gt[j2, here, upper] = t_landed(j2, upper, rt5.at[1], 23).astype(BF)
+        th_x().start()
+
+    def tl_five():
+        own_t[lower, :] = t_landed(j, lower, rt3, 24)
+
+    def th_five():
+        both(th_x())
+        own_t[upper, :] = own_t[upper, :] + rt6[...].astype(F32)
+
 
     per = 640 // (4 * rb)
     for b in range(2):
@@ -969,15 +1118,12 @@
 
     dhid = gp
 
-    def fold(v):
-        return jnp.sum(v.reshape(side // 8, 8, 128), axis=0)
-
-    def back_over(lo, hi, step, first, tiles):
+    def back_over(lo, hi, step, tiles):
         def back_tile(t, carry):
             lanes = tile_at(t)
             taps = taps_of(lanes)
 
-            def row(at, sums):
+            def row(at, inner):
                 r = lo + at * step
                 around = [dz[rows((r + a) * side, side), lanes].astype(F32) for a in range(3)]
                 parts = [
@@ -987,36 +1133,50 @@
                 both_ways = jnp.concatenate([parts[0].astype(BF), parts[2].astype(BF)], axis=0)
                 low = (parts[1] + nn(shift_b[...], both_ways)).astype(BF)
                 dhid[rows(r * side, side), lanes] = low
-                here = around[1]
-                sides = nn(shift_m[...], dz[rows((r + 1) * side, side), lanes])
-                moved = [sides[0:side], here, sides[side : 2 * side]]
+                return inner
+
+            lax.fori_loop(0, (hi - lo) // step, row, 0, unroll=True)
+            return carry
+
+        lax.fori_loop(0, FF // 128, back_tile, 0, unroll=tiles)
+
+    back_over(1, band - 1, 1, 1)
+    rim_wait(dz, dzh, 2)
+    back_over(0, 2 * (band - 1), band - 1, 5)
+
+    def fold(v):
+        return jnp.sum(v.reshape(-1, 8, 128), axis=0)
+
+    def tap_sums(lo, hi):
+        def tile(t, carry):
+            lanes = tile_at(t)
+
+            def row(r, sums):
+                low = dz[rows((r + 1) * side, side), lanes]
+                here_f = low.astype(F32)
+                sides = nn(shift_m[...], low)
+                moved = [sides[0:side], here_f, sides[side : 2 * side]]
                 found = []
                 for a in range(3):
                     source = hidp[rows((r + a) * side, side), lanes].astype(F32)
                     for b in range(3):
                         found.append(fold(moved[b] * source))
-                found.append(fold(low.astype(F32)))
-                found.append(fold(here))
+                found.append(fold(here_f))
                 return tuple(s + f for s, f in zip(sums, found))
 
             sums = lax.fori_loop(
-                0,
-                (hi - lo) // step,
-                row,
-                tuple(jnp.zeros((8, 128), F32) for _ in range(11)),
-                unroll=True,
+                0, band, row, tuple(jnp.zeros((8, 128), F32) for _ in range(10)), unroll=deep
             )
-            found = jnp.concatenate([colsum(s) for s in sums] + [jnp.zeros((5, 128), F32)], axis=0)
-            hg[:, lanes] = found if first else hg[:, lanes] + found
+            hg[:, lanes] = jnp.concatenate(
+                [colsum(s) for s in sums[0:9]]
+                + [hg[9:10, lanes], colsum(sums[9]), jnp.zeros((5, 128), F32)],
+                axis=0,
+            )
             return carry
 
-        lax.fori_loop(0, FF // 128, back_tile, 0, unroll=tiles)
-
-    back_over(1, band - 1, 1, True, 1)
-    rim_wait(dz, dzh, 2)
-    back_over(0, 2 * (band - 1), band - 1, False, 5)
-
-    a_three()
+        lax.fori_loop(lo, hi, tile, 0)
+
+    hg[9:10, :] = colsum(dhid[...].astype(F32))
     bn_t = dy_t
     bn_t[...] = bn[...].T
     for b in range(2):
@@ -1026,6 +1186,8 @@
             sb[2 * b : 2 * b + 2, place_of(i), :, 0 : 4 * rb] = jnp.concatenate(
                 [value[:, v, :, rb * i : rb * i + rb] for v in range(4)], axis=2
             )
+
+    b_one()
 
     zero_row = jnp.zeros((1, D), F32)
     dbr = bn
@@ -1055,25 +1217,20 @@
     vg[2:3, :] = sums[0]
     vg[9:10, :] = sums[1]
     vg[8:9, :] = sums[2]
-    value = nn(dbr_t[...], att_n[...]).astype(BF)
-    for i in range(n):
-        sb[:, place_of(i), :, 4 * rb : 5 * rb] = value[:, rb * i : rb * i + rb].reshape(
-            4, 80, rb
-        )
-    b_one()
-    a_four()
+    a_three()
+    b_two()
 
     def dkv(h, slot):
-        return act.at[rows(slot * keys, keys), tile_at(h)]
+        return gp.at[rows(slot * keys, keys), tile_at(h)]
 
     def dk_core(h):
         return [
-            remote(dkv(h, slot), rk1.at[h, t], dk_s.at[h, t], dk_r.at[h, t], me, j1)
+            remote(dkv(h, slot), rk1.at[h, t], kv_s.at[h, t], kv_r.at[h, t], me, j1)
             for t, slot in enumerate((j1, j3))
         ]
 
     def dk_x(h):
-        return remote(dkv(h, j2), rk2.at[h], dk_s.at[h, 2], dk_r.at[h, 2], me, j2)
+        return remote(dkv(h, j2), rk2.at[h], kv_s.at[h, 2], kv_r.at[h, 2], me, j2)
 
     def dk_two(h):
         for copy in dk_core(h):
@@ -1098,13 +1255,21 @@
             part = nn(ds, qnat[h, cut, :]) + nn(powers, datn[h, cut, :])
             prob[h, :, cut] = ds
             total = part if total is None else total + part
-        act[0 : 4 * keys, tile_at(h)] = total.astype(BF)
+        gp[0 : 4 * keys, tile_at(h)] = total.astype(BF)
         for copy in dk_core(h):
             copy.start()
 
-        @pl.when(h == 1)
+        @pl.when(h == 2)
         def _():
-            b_two()
+            a_four()
+
+        @pl.when(h == 3)
+        def _():
+            bl_three()
+
+        @pl.when(h == 4)
+        def _():
+            bh_three()
 
         @pl.when(h >= 1)
         def _():
@@ -1126,11 +1291,10 @@
 
     lax.fori_loop(0, 2, back_query, 0)
     dk_two(HEADS - 1)
-    b_three()
-    for h in range(HEADS - 2):
-        dk_three(h)
     lax.fori_loop(2, HEADS, back_query, 0)
-    dq = att_n
+    bl_four()
+
+    dq = dy
 
     def flip(c, total):
         low = dq_t[:, across(c)].T
@@ -1139,25 +1303,32 @@
 
     vg[4:5, :] = lax.fori_loop(0, chunks, flip, zero_row)
     value = nn(dq_t[...], abf[...]).astype(BF)
+    other = nn(dbr_t[...], att_n[...]).astype(BF)
+
+    def folded(v, i):
+        part = v[:, rb * i : rb * i + rb].reshape(4, 80, rb)
+        return [
+            part[:, 0:32],
+            part[:, 32:64],
+            jnp.concatenate([part[:, 64:80], jnp.zeros((4, 16, rb), BF)], axis=1),
+        ]
+
     for i in range(n):
-        part = value[:, rb * i : rb * i + rb].reshape(4, 80, rb)
-        gm[:, place_of(i), :, 0 : 3 * rb] = jnp.concatenate(
-            [
-                part[:, 0:32],
-                part[:, 32:64],
-                jnp.concatenate([part[:, 64:80], jnp.zeros((4, 16, rb), BF)], axis=1),
-            ],
-            axis=2,
-        )
-    dk_three(HEADS - 2)
-    dk_three(HEADS - 1)
+        gm[:, place_of(i), :, 0 : 3 * rb] = jnp.concatenate(folded(value, i), axis=2)
+        gm[:, place_of(i), :, mo : mo + 3 * rb] = jnp.concatenate(folded(other, i), axis=2)
+    m_one()
+    tap_sums(0, FF // 256)
+    m_two()
+    for h in range(HEADS):
+        dk_three(h)
 
     dm = jnp.concatenate([qnat[h, 0:keys, :] for h in range(HEADS)], axis=1)
     dm_sum = colsum(dm.astype(F32))
     vg[7:8, :] = jnp.concatenate(
         [dm_sum[:, 128 * h + 64 : 128 * h + 128] for h in range(HEADS)], axis=1
     )
-    dv, in_gain, in_shift = norm_back(red_s[...], gain(1), nn(dm, wmt[...]))
+    kept = jnp.concatenate([a3[t, 0:keys, :] for t in range(3)], axis=1)[:, 0:D]
+    dv, in_gain, in_shift = norm_back(kept, gain(1), nn(dm, wmt[...]))
     vg[1:2, :] = in_gain
     vg[6:7, :] = in_shift
     dred = dv.astype(BF)
@@ -1183,7 +1354,6 @@
         )
     t_one()
 
-    m_one()
     t_two()
 
     for dd in range(4):
@@ -1195,7 +1365,6 @@
                 a3[t, pl.ds(start, half, stride=2), :] = back[
                     i * half : (i + 1) * half, 128 * t : 128 * t + 128
                 ]
-    m_two()
 
     def back_first(c, carry):
         at = rows(c * QC, QC)
@@ -1209,38 +1378,44 @@
     token_out.start()
     vg[0:1, :] = sums[0]
     vg[3:4, :] = sums[1]
+    m_three()
+    tap_sums(FF // 256, FF // 128)
     for i in range(n):
         sv[place_of(i), :, 0 : 4 * rb] = hg[:, 4 * rb * i : 4 * rb * (i + 1)].astype(BF)
         sv[place_of(i), :, 4 * rb : 5 * rb] = vg[:, rb * i : rb * i + rb].astype(BF)
 
     def v_out(k, peer, source):
-        remote(sv.at[spot(peer)], rv1.at[k], rs_s.at[23], rs_r.at[23], peer, j).start()
+        remote(sv.at[spot(peer)], rv1.at[k], rs_s.at[26], rs_r.at[26], peer, j).start()
 
     peers(v_out)
-    tl_three()
-    b_four()
-    m_three()
+    tl_three(0)
+    tl_three(1)
+    bh_four()
+    m_four()
     part = rv1.at[pl.ds(1, n - 1)]
-    both(remote(part, part, rs_s.at[23], rs_r.at[23], beside, j))
+    both(remote(part, part, rs_s.at[26], rs_r.at[26], beside, j))
     rv2[j] = lax.fori_loop(
         1, n, lambda k, total: total + rv1[k].astype(F32), sv[here].astype(F32)
     ).astype(BF)
 
     def v_seq(t, slot, other):
         ref = rv2.at[slot]
-        return remote(ref, ref, rs_s.at[24 + t], rs_r.at[24 + t], me, other)
+        return remote(ref, ref, rs_s.at[30 + t], rs_r.at[30 + t], me, other)
 
     for t, other in enumerate((j1, j2, j3)):
         v_seq(t, j, other).start()
     th_four()
     a_five()
-    b_five()
+    bl_five()
+    bh_five()
     squares = jnp.sum(own_a[:, 0 : 4 * rb] * own_a[:, 0 : 4 * rb])
-    squares += jnp.sum(own_b[:, 0 : 5 * rb] * own_b[:, 0 : 5 * rb])
+    squares += jnp.sum(own_b[:, 0 : 4 * rb] * own_b[:, 0 : 4 * rb])
     th_five()
     m_five()
-    squares += jnp.sum(own_m[:, 0 : 2 * rb] * own_m[:, 0 : 2 * rb])
-    squares += jnp.sum(own_m[0:16, 2 * rb : 3 * rb] * own_m[0:16, 2 * rb : 3 * rb])
+    for at in (0, mo):
+        full = own_m[:, at : at + 2 * rb]
+        rest = own_m[0:16, at + 2 * rb : at + 3 * rb]
+        squares += jnp.sum(full * full) + jnp.sum(rest * rest)
     tl_five()
     squares += jnp.sum(own_t[:, 0 : 6 * rb] * own_t[:, 0 : 6 * rb])
     for t, other in enumerate((j1, j2, j3)):
@@ -1251,7 +1426,7 @@
     first_band = (j == 0).astype(jnp.int32).astype(F32)
     squares += first_band * jnp.sum(own_v[0:11, 0 : 5 * rb] * own_v[0:11, 0 : 5 * rb])
 
-    nrm[4 * me + j] = jnp.full((8, 128), squares, F32)
+    nrm[4 * me + j] = jnp.full((1, 128), squares, F32)
     own_out_copy = pltpu.make_async_copy(own_s, own_ref, loc.at[13])
     own_out_copy.start()
 
@@ -1277,57 +1452,57 @@
     norm_out.wait()
 
 
-def update_kernel(rb, tl, al, rates, decays, *refs):
+def update_kernel(rb, tl, al, mo, rates, decays, *refs):
     own_hbm, total_hbm, outt_hbm, tg_hbm = refs[0:4]
     in_hbm = refs[4:31]
     out_hbm, tok_hbm, norm_hbm = refs[31:34]
     new_hbm = refs[34:61]
     own_ref, total_ref, out_v, tok_v, norm_v = refs[61:66]
-    in_v, new_v = refs[66:93], refs[93:120]
-    in_sem, out_sem = refs[120:122]
-    loads = [
-        pltpu.make_async_copy(src, dst, in_sem.at[at])
+    in_v, new_v = refs[66:75], refs[75:84]
+    in_sem, out_sem = refs[84:86]
+    own_load, total_load, out_load, tok_load = [
+        pltpu.make_async_copy(src, dst, in_sem.at[9 + at])
         for at, (src, dst) in enumerate(
-            [
-                (own_hbm, own_ref),
-                *zip(in_hbm, in_v),
-                (outt_hbm, out_v),
-                (tg_hbm, tok_v),
-                (total_hbm, total_ref),
-            ]
+            ((own_hbm, own_ref), (total_hbm, total_ref), (outt_hbm, out_v), (tg_hbm, tok_v))
         )
     ]
-    for load in loads:
-        load.start()
-    stores = [
-        pltpu.make_async_copy(src, dst, out_sem.at[at])
-        for at, (src, dst) in enumerate(
-            [*zip(new_v, new_hbm), (out_v, out_hbm), (tok_v, tok_hbm), (norm_v, norm_hbm)]
-        )
+    own_load.start()
+    total_load.start()
+    for at in range(9):
+        for part in range(3):
+            pltpu.make_async_copy(in_hbm[at + 9 * part], in_v[at].at[part], in_sem.at[at]).start()
+    out_load.start()
+    tok_load.start()
+    norm_store, out_store, tok_store = [
+        pltpu.make_async_copy(src, dst, out_sem.at[9 + at])
+        for at, (src, dst) in enumerate(((norm_v, norm_hbm), (out_v, out_hbm), (tok_v, tok_hbm)))
     ]
-    loads[0].wait()
-    loads[30].wait()
-    total = total_ref[0:1, :]
+    own_load.wait()
+    total_load.wait()
+    total = total_ref[...]
     norm = jnp.sqrt(total)
     norm_v[...] = norm
-    stores[29].start()
+    norm_store.start()
     clip = jnp.minimum(1.0, MAX_NORM / (norm + 1e-06))[:, 0:1]
     turned_t = own_ref[0:80, 0:tl].T
     turned_a = own_ref[0:80, tl : tl + al].T
     turned_b = own_ref[0:80, tl + al :].T
-    turned_q = jnp.concatenate(
-        [
-            own_ref[96:128, 0:rb],
-            own_ref[96:128, rb : 2 * rb],
-            own_ref[96:112, 2 * rb : 3 * rb],
-        ],
-        axis=0,
-    ).T
+    turned_q, turned_o = [
+        jnp.concatenate(
+            [
+                own_ref[96:128, at : at + rb],
+                own_ref[96:128, at + rb : at + 2 * rb],
+                own_ref[96:112, at + 2 * rb : at + 3 * rb],
+            ],
+            axis=0,
+        ).T
+        for at in (0, mo)
+    ]
     grads = (
         turned_q,
         turned_t[0 : 4 * rb],
         jnp.concatenate([turned_t[(4 + v) * rb : (5 + v) * rb] for v in range(2)], axis=1),
-        turned_b[4 * rb : 5 * rb],
+        turned_o,
         jnp.concatenate([turned_b[v * rb : (v + 1) * rb] for v in range(4)], axis=1),
         turned_a[0 : 4 * rb],
         own_ref[80:83, 4 * rb : 5 * rb],
@@ -1335,26 +1510,30 @@
         own_ref[80:91, 0 : 4 * rb],
     )
     for at in range(9):
-        for part in range(3):
-            loads[1 + at + 9 * part].wait()
+        pltpu.make_async_copy(in_v[at], in_v[at], in_sem.at[at]).wait()
         clipped = clip * grads[at]
-        weight = in_v[at][...]
-        first = BETA_ONE * in_v[9 + at][...] + (1.0 - BETA_ONE) * clipped
-        second = BETA_TWO * in_v[18 + at][...] + (1.0 - BETA_TWO) * clipped * clipped
+        weight = in_v[at][0]
+        first = BETA_ONE * in_v[at][1] + (1.0 - BETA_ONE) * clipped
+        second = BETA_TWO * in_v[at][2] + (1.0 - BETA_TWO) * clipped * clipped
         direction = (
             first
             / (1.0 - BETA_ONE**STEP)
             / (jnp.sqrt(second / (1.0 - BETA_TWO**STEP)) + ADAM_EPS)
         )
-        new_v[at][...] = weight - rates[at] * (direction + decays[at] * weight)
-        new_v[9 + at][...] = first
-        new_v[18 + at][...] = second
+        new_v[at][0] = weight - rates[at] * (direction + decays[at] * weight)
+        new_v[at][1] = first
+        new_v[at][2] = second
         for part in range(3):
-            stores[at + 9 * part].start()
-    for at in (28, 29):
-        loads[at].wait()
-        stores[at - 1].start()
-    for store in stores:
+            pltpu.make_async_copy(
+                new_v[at].at[part], new_hbm[at + 9 * part], out_sem.at[at]
+            ).start()
+    out_load.wait()
+    out_store.start()
+    tok_load.wait()
+    tok_store.start()
+    for at in range(9):
+        pltpu.make_async_copy(new_v[at], new_v[at], out_sem.at[at]).wait()
+    for store in (norm_store, out_store, tok_store):
         store.wait()
 
 
@@ -1369,11 +1548,12 @@
     wide = up(9 * rb, 128)
     tl = up(6 * rb, 128)
     al = up(4 * rb, 128)
-    bl = up(5 * rb, 128)
+    bl = up(4 * rb, 128)
+    ml = up(6 * rb, 128)
     h = n // 2
     vl = up(5 * rb, 128)
     total = tl + al + bl
-    qa = count if n <= 8 else 256
+    qa = count if n <= 8 else 128
     turned = piece % 128 == 0
     block = (n, D, piece) if turned else (n, piece, D)
     vm = pltpu.VMEM
@@ -1397,7 +1577,7 @@
         *[vm(weights[at].shape, F32) for at in range(9)],
         vm((n, 16, vl), BF),
         vm((4, n, 80, tl), BF),
-        vm((4, n, 32, 128), BF),
+        vm((4, n, 32, ml), BF),
         vm((4, n, 80, wide), BF),
         vm((16, D), F32),
         vm((16, FF), F32),
@@ -1411,7 +1591,6 @@
         vm((3, count, 128), F32),
         vm((count, D), BF),
         vm((4, keys, D), BF),
-        vm((keys, D), F32),
         vm((keys, D), BF),
         vm((HEADS, 4, keys, 128), BF),
         vm((HEADS, 128, 4 * keys), BF),
@@ -1441,24 +1620,25 @@
         vm((128, total), F32),
         vm((4, n, 80, bl), BF),
         *landing(80, al, 80, False),
-        *landing(80, bl, 0, False),
+        *landing(80, bl, 32, False),
         *landing(80, tl, CUT, True),
-        *landing(32, 128, 32, True),
+        *landing(32, ml, 32, False),
         vm((n, 16, vl), BF),
         vm((n, 16, vl), BF),
         vm((4, 16, vl), BF),
-        vm((4 * n + 1, 8, 128), F32),
+        vm((4 * n + 1, 1, 128), F32),
         vm((side, 2 * side), BF),
         vm((side, 2 * side), BF),
         vm((2 * side, side), BF),
         dma((15,)),
         *[dma((9,)) for _ in range(2)],
+        dma((n,)),
+        dma((2, h)),
         *[dma((16,)) for _ in range(2)],
         *[dma((1,)) for _ in range(4)],
         *[dma((HEADS, 3)) for _ in range(2)],
         *[dma((4,)) for _ in range(2)],
-        *[dma((HEADS, 3)) for _ in range(2)],
-        *[dma((27,)) for _ in range(2)],
+        *[dma((34,)) for _ in range(2)],
         *[dma((1,)) for _ in range(2)],
     ]
     anywhere = pl.BlockSpec(memory_space=pl.ANY)
@@ -1468,7 +1648,7 @@
             jax.ShapeDtypeStruct(block, BF),
             jax.ShapeDtypeStruct((count, D), BF),
             jax.ShapeDtypeStruct((128, total), F32),
-            jax.ShapeDtypeStruct((8, 128), F32),
+            jax.ShapeDtypeStruct((1, 128), F32),
         ),
         in_specs=[pl.BlockSpec(memory_space=pltpu.SMEM)] + [anywhere] * 11,
         out_specs=(anywhere,) * 4,
@@ -1496,7 +1676,9 @@
     decays = (DECAY_RATE,) * 6 + (0.0,) * 3
     shapes = tuple(jax.ShapeDtypeStruct(w.shape, F32) for w in weights)
     results = pl.pallas_call(
-        functools.partial(update_kernel, rb, tl, al, rates, decays),
+        functools.partial(
+            update_kernel, rb, tl, al, 128 if ml > 128 else 3 * rb, rates, decays
+        ),
         out_shape=(
             jax.ShapeDtypeStruct(block, BF),
             jax.ShapeDtypeStruct((count, D), BF),
@@ -1507,13 +1689,13 @@
         out_specs=(anywhere,) * 30,
         scratch_shapes=[
             vm((128, total), F32),
-            vm((8, 128), F32),
+            vm((1, 128), F32),
             vm(block, BF),
             vm((count, D), BF),
             vm((1, 128), F32),
-            *[vm(w.shape, F32) for w in weights * 6],
-            dma((31,)),
-            dma((30,)),
+            *[vm((3, *w.shape), F32) for w in weights * 2],
+            dma((13,)),
+            dma((12,)),
         ],
     )(own, total_squares, out_t, token_grad, *weights, *firsts, *seconds)
     if turned:

time: 125 us -> 116 us (0.928)
  Pallas kernels: 123 us -> 115 us
    pallas_call x1, Pallas kernels: 119 us -> 111 us  [on_device(): pl.pallas_call(functools.partial(block_kernel, n, side, band, qa), out_sh...]
where the time goes in v4:
time: 116 us
  Pallas kernels  115 us (99%)
  between operations  1.48 us (1%)
    pallas_call x1, Pallas kernels, on_device(): pl.pallas_call(functools.partial(block_kernel, n, side, band, qa), out_sh...  111 us
    pallas_call x1, Pallas kernels, on_device(): pl.pallas_call(functools.partial(update_kernel, rb, tl, al, 128 if ml > 1...  3.37 us

profile of v4, /device:TPU:0, one launch (start us, length us, event | category | flops | bytes accessed | tf_op | source)
XLA Modules:
  0.0 116.2 jit_solution(3826655593354105906)
XLA Ops:
  1.3 111.4 %shard_map.517 = (bf16[8,320,128]{2,1,0:T(8,128)(2,1)}, bf16[1024,320]{1,0:T(8,128)(2,1)}, f32[128,768]{1,0:T(8,128)}, f32[1,128]{1,0:T(1,128)}) custom-call(s32[1]{0:T(128)S(6)} %copy.62.bucket_ref, bf16[1024,320]{1,0:T(8,128)(2,1)} %bitcast.14, bf16[8,320,128]{2,1,0:T(8,128)(2,1)} %bitcast.15, f32[40,80]{1,0:T(8,128)} %refs_4_.1, f32[160,80]{1,0:T(8,128)} %refs_5_.1, ...), custom_call_target="tpu_custom_call" | custom-call | tf_op jit(solution)/shard_map/pallas_call | solution.py:1645
  112.7 3.4 %shard_map.518 = (bf16[8,320,128]{2,1,0:T(8,128)(2,1)}, bf16[1024,320]{1,0:T(8,128)(2,1)}, f32[1,128]{1,0:T(1,128)}, f32[40,80]{1,0:T(8,128)}, f32[160,80]{1,0:T...) custom-call(f32[128,768]{1,0:T(8,128)} %get-tuple-element.64.refs_0_, ...), custom_call_target="tpu_custom_call" | custom-call | tf_op jit(solution)/shard_map/pallas_call | solution.py:1678

commit v5 on v4

--- a/solution.py
+++ b/solution.py
@@ -28,6 +28,7 @@
 F32 = jnp.float32
 MESH = pl.DeviceIdType.MESH
 QC = 512
+GATHER_CUT = 32
 CUT = 48
 VMEM_LIMIT = 63 * 1024 * 1024
 
@@ -180,8 +181,6 @@
     shift_b,
     shift_m,
     loc,
-    gd_s,
-    gd_r,
     tl_r,
     th_r,
     gx_s,
@@ -194,8 +193,6 @@
     kv_r,
     ha_s,
     ha_r,
-    rs_s,
-    rs_r,
     nd_s,
     nd_r,
 ):
@@ -312,12 +309,12 @@
         def start():
             def send(peer):
                 ref = one_of(here)
-                remote(ref, ref, gd_s.at[at], gd_r.at[at], peer, j).start()
+                remote(ref, ref, gx_s.at[14 + at], gx_r.at[14 + at], peer, j).start()
 
             each(send)
 
         def wait():
-            both(remote(all_but_one, all_but_one, gd_s.at[at], gd_r.at[at], beside, j))
+            both(remote(all_but_one, all_but_one, gx_s.at[14 + at], gx_r.at[14 + at], beside, j))
 
         return start, wait
 
@@ -352,8 +349,8 @@
         theirs = buf.at[pl.ds(y1 * zn, zn), rows_of]
         return swap(at, mine, theirs, beside, j)
 
-    lower = slice(0, CUT)
-    upper = slice(CUT, 80)
+    lower = slice(0, GATHER_CUT)
+    upper = slice(GATHER_CUT, 80)
     every = slice(0, 16)
     v_dp, v_dp_wait = over_dp(0, gvec, every)
 
@@ -361,7 +358,7 @@
         return gt.at[j, i, lower]
 
     def t_low_copy(k, i, peer):
-        return remote(t_low(i), t_low(i), gd_s.at[1], tl_r.at[k], peer, j)
+        return remote(t_low(i), t_low(i), gx_s.at[15], tl_r.at[k], peer, j)
 
     def t_low_on(i):
         remote(t_low(i), t_low(i), gx_s.at[0], gx_r.at[0], me, j2).start()
@@ -379,7 +376,7 @@
 
     def t_low_wait():
         part = gt.at[j, pl.ds(0, n - 1), lower]
-        remote(part, part, gd_s.at[1], tl_r.at[0], beside, j).wait_send()
+        remote(part, part, gx_s.at[15], tl_r.at[0], beside, j).wait_send()
         both(remote(gt.at[j, :, lower], gt.at[j2, :, lower], gx_s.at[0], gx_r.at[0], me, j2))
 
     t_x0, t_x0_wait = swap(1, gt.at[j, here, upper], gt.at[j2, here, upper], me, j2)
@@ -389,7 +386,7 @@
             return gt.at[slot, i, upper]
 
         def copy(k, i, peer):
-            return remote(ref(i), ref(i), gd_s.at[2 + t], th_r.at[t, k], peer, j)
+            return remote(ref(i), ref(i), gx_s.at[16 + t], th_r.at[t, k], peer, j)
 
         def on(i):
             remote(ref(i), ref(i), gx_s.at[2 + t], gx_r.at[2 + t], beside, j).start()
@@ -407,7 +404,7 @@
 
         def wait():
             part = gt.at[slot, pl.ds(0, zn - 1), upper]
-            remote(part, part, gd_s.at[2 + t], th_r.at[t, 0], beside, j).wait_send()
+            remote(part, part, gx_s.at[16 + t], th_r.at[t, 0], beside, j).wait_send()
             mine = gt.at[slot, pl.ds(y0 * zn, zn), upper]
             theirs = gt.at[slot, pl.ds(y1 * zn, zn), upper]
             both(remote(mine, theirs, gx_s.at[2 + t], gx_r.at[2 + t], beside, j))
@@ -426,14 +423,14 @@
     f_x0, f_x0_wait = swap(9, gf.at[j, here], gf.at[j2, here], me, j2)
     fl_za, fl_za_wait = over_z(5, gf.at[j], lower)
     fl_zb, fl_zb_wait = over_z(6, gf.at[j2], lower)
-    fh_za, fh_za_wait = over_z(7, gf.at[j], upper)
-    fh_zb, fh_zb_wait = over_z(8, gf.at[j2], upper)
+    fh_a, fh_a_wait = over_dp(7, gf.at[j], upper)
+    fh_b, fh_b_wait = over_dp(8, gf.at[j2], upper)
     fl_ya, fl_ya_wait = over_y(10, gf.at[j], lower)
     fl_yb, fl_yb_wait = over_y(11, gf.at[j2], lower)
-    fh_ya, fh_ya_wait = over_y(12, gf.at[j], upper)
-    fh_yb, fh_yb_wait = over_y(13, gf.at[j2], upper)
-    f_ca, f_ca_wait = swap(14, gf.at[j], gf.at[j1], me, j1)
-    f_cb, f_cb_wait = swap(15, gf.at[j2], gf.at[j3], me, j1)
+    fl_ca, fl_ca_wait = swap(12, gf.at[j, :, lower], gf.at[j1, :, lower], me, j1)
+    fl_cb, fl_cb_wait = swap(13, gf.at[j2, :, lower], gf.at[j3, :, lower], me, j1)
+    fh_ca, fh_ca_wait = swap(34, gf.at[j, :, upper], gf.at[j1, :, upper], me, j1)
+    fh_cb, fh_cb_wait = swap(35, gf.at[j2, :, upper], gf.at[j3, :, upper], me, j1)
 
     pl.semaphore_wait(barrier, 4 * n - 1)
     t_x0()
@@ -462,10 +459,10 @@
     t_x0_wait()
     t_zb()
     v_dp()
+
+    t_low_forward()
     m_dp()
     f_x0()
-
-    t_low_forward()
     t_za_forward()
     t_zb_forward()
     f_x0_wait()
@@ -539,18 +536,18 @@
         (j < 3).astype(jnp.int32) * (1 - bucket * ((j + 1) * band == half).astype(jnp.int32))
     ).astype(F32)
 
-    m_dp_wait()
-    m_x()
     t_ya_wait()
     t_yb_wait()
     t_low_wait()
     t_ca()
     t_cb()
-    m_x_wait()
-    m_ca()
-    m_cb()
+    m_dp_wait()
+    m_x()
     t_ca_wait()
     t_cb_wait()
+
+    fh_a()
+    fh_b()
 
     for s in range(4):
         span = slice(80 * s, 80 * s + 80)
@@ -602,6 +599,9 @@
 
     lax.fori_loop(0, 2, kv_send, 0)
 
+    m_x_wait()
+    m_ca()
+    m_cb()
     wqp = wop
     m_ca_wait()
     m_cb_wait()
@@ -657,21 +657,9 @@
     fl_zb_wait()
     fl_ya()
     fl_yb()
-    fh_za()
-    fh_zb()
     kv_forward(0)
 
     def attend(h, carry):
-        @pl.when(h == HEADS - 1)
-        def _():
-            fl_ya_wait()
-            fl_yb_wait()
-            fh_ya_wait()
-            fh_yb_wait()
-            f_ca()
-            f_cb()
-            peers(send_cot)
-
         kv_copy(h, j, 0, j2).wait_send()
         kv_copy(h, j, 1, j1).wait_send()
         kv_copy(h, j2, 2, j1).wait_send()
@@ -690,12 +678,20 @@
                 def _():
                     kv_forward(h + 1)
 
-                @pl.when(h == 1)
+                @pl.when(h == HEADS - 2)
                 def _():
-                    fh_za_wait()
-                    fh_zb_wait()
-                    fh_ya()
-                    fh_yb()
+                    fl_ya_wait()
+                    fl_yb_wait()
+                    fl_ca()
+                    fl_cb()
+
+                @pl.when(h == HEADS - 1)
+                def _():
+                    fh_a_wait()
+                    fh_b_wait()
+                    fh_ca()
+                    fh_cb()
+                    peers(send_cot)
 
             largest = jnp.max(scores, axis=0, keepdims=True)
             powers = jnp.exp(scores - largest).astype(BF)
@@ -708,19 +704,28 @@
 
     lax.fori_loop(0, HEADS, attend, 0)
 
-    f_ca_wait()
-    f_cb_wait()
-    for s in range(4):
-        span = slice(80 * s, 80 * s + 80)
-        w2t[span, :] = jnp.concatenate([gf[s, place_of(i), :, 0 : 4 * rb] for i in range(n)], axis=1)
-        for v in range(4):
-            at = 320 * s + 80 * v
-            w1t[at : at + 80, :] = jnp.concatenate(
-                [gf[s, place_of(i), :, (4 + v) * rb : (5 + v) * rb] for i in range(n)], axis=1
-            )
-        wot[span, :] = jnp.concatenate(
-            [gf[s, place_of(i), :, 8 * rb : 9 * rb] for i in range(n)], axis=1
-        )
+    fl_ca_wait()
+    fl_cb_wait()
+
+    def unpack_rows(part, lo, hi):
+        for s in range(4):
+            span = slice(80 * s + lo, 80 * s + hi)
+
+            def lanes(at, width):
+                return jnp.concatenate(
+                    [gf[s, place_of(i), part, at : at + width] for i in range(n)], axis=1
+                )
+
+            w2t[span, :] = lanes(0, 4 * rb)
+            for v in range(4):
+                at = 320 * s + 80 * v
+                w1t[at + lo : at + hi, :] = lanes((4 + v) * rb, rb)
+            wot[span, :] = lanes(8 * rb, rb)
+
+    unpack_rows(lower, 0, GATHER_CUT)
+    fh_ca_wait()
+    fh_cb_wait()
+    unpack_rows(upper, GATHER_CUT, 80)
     wop_full = wot[...].T
     for h in range(HEADS):
         wop[128 * h : 128 * h + 64, :] = jnp.zeros((64, D), BF)
@@ -814,10 +819,11 @@
                 ]
                 moved = jnp.concatenate([parts[0].astype(BF), parts[2].astype(BF)], axis=0)
                 z = base + parts[1] + nn(shift_f[...], moved)
-                cdf = 0.5 + 0.5 * lax.erf(z * (0.5**0.5))
-                pdf = jnp.exp(z * z * -0.5) * 0.3989422804014327
+                root = z * (0.5**0.5)
+                cdf = 0.5 + 0.5 * lax.erf(root)
+                slope = (z * 0.3989422804014327) * jnp.exp2(root * root * -1.4426950408889634)
                 act[rows((r + 1) * side, side), lanes] = (z * cdf).astype(BF)
-                gp[rows(r * side, side), lanes] = (cdf + z * pdf).astype(BF)
+                gp[rows(r * side, side), lanes] = (cdf + slope).astype(BF)
                 return inner
 
             lax.fori_loop(0, (hi - lo) // step, row, 0, unroll=True)
@@ -872,7 +878,7 @@
 
         def copy(src, dst, t, dp, seq):
             at = sems[t]
-            return remote(src, dst, rs_s.at[at], rs_r.at[at], dp, seq)
+            return remote(src, dst, gx_s.at[at], gx_r.at[at], dp, seq)
 
         def core():
             return [copy(s.at[slot], r1.at[t], t, me, j1) for t, slot in enumerate((j1, j3))]
@@ -987,17 +993,20 @@
     m_one, m_two, m_three, m_four, m_five, _, _, _ = scatter(
         (12, 13, 14, 15, 0, 0, 0, 0, 0, 33), gm, 32, False, (rm0, rm1, rm2, rm3, rm4, rm5, rm6), own_m
     )
+    below_cut = slice(0, CUT)
+    above_cut = slice(CUT, 80)
+
     def t_core(t, slot, to, rows_of):
         return remote(
-            gt.at[slot, :, rows_of], rt0.at[to, :, rows_of], rs_s.at[16 + t], rs_r.at[16 + t], me, j1
+            gt.at[slot, :, rows_of], rt0.at[to, :, rows_of], gx_s.at[16 + t], gx_r.at[16 + t], me, j1
         )
 
     def t_cores():
         return (
-            t_core(0, j3, 1, lower),
-            t_core(1, j1, 0, upper),
-            t_core(2, j3, 1, upper),
-            t_core(3, j1, 0, lower),
+            t_core(0, j3, 1, below_cut),
+            t_core(1, j1, 0, above_cut),
+            t_core(2, j3, 1, above_cut),
+            t_core(3, j1, 0, below_cut),
         )
 
     def t_add(slot, start, count, rows_of, extra):
@@ -1012,17 +1021,17 @@
     def t_half(t):
         part = pl.ds((y1 if t == 0 else y0) * zn, zn)
         return remote(
-            gt.at[j2, part, lower], rt1.at[part], rs_s.at[20 + t], rs_r.at[20 + t], me, j2
+            gt.at[j2, part, below_cut], rt1.at[part], gx_s.at[20 + t], gx_r.at[20 + t], me, j2
         )
 
     def t_dp(slot, i, rows_of, land, sem, k, peer):
         remote(
-            gt.at[slot, i, rows_of], land.at[k], rs_s.at[sem], rs_r.at[sem], peer, j
+            gt.at[slot, i, rows_of], land.at[k], gx_s.at[sem], gx_r.at[sem], peer, j
         ).start()
 
     def t_landed(slot, rows_of, land, sem):
         part = land.at[pl.ds(1, n - 1)]
-        both(remote(part, part, rs_s.at[sem], rs_r.at[sem], beside, j))
+        both(remote(part, part, gx_s.at[sem], gx_r.at[sem], beside, j))
         return lax.fori_loop(
             1, n, lambda k, v: v + land[k].astype(F32), gt[slot, here, rows_of].astype(F32)
         )
@@ -1034,20 +1043,20 @@
     def t_two():
         cores = t_cores()
         both(cores[0])
-        t_add(j2, 0, n, lower, rt0.at[1])
+        t_add(j2, 0, n, below_cut, rt0.at[1])
         t_half(0).start()
         t_half(1).start()
         both(cores[1])
         both(cores[2])
         for t, slot in enumerate((j, j2)):
-            t_add(slot, 0, n, upper, rt0.at[t])
+            t_add(slot, 0, n, above_cut, rt0.at[t])
             peers(
                 lambda k, peer, source: t_dp(
-                    slot, spot(peer), upper, rt5.at[t], 22 + t, k, peer
+                    slot, spot(peer), above_cut, rt5.at[t], 22 + t, k, peer
                 )
             )
         both(cores[3])
-        t_add(j, 0, n, lower, rt0.at[0])
+        t_add(j, 0, n, below_cut, rt0.at[0])
 
     def tl_three(t):
         both(t_half(t))
@@ -1055,7 +1064,7 @@
 
         def body(i, carry):
             at = start + i
-            gt[j, at, lower] = (gt[j, at, lower].astype(F32) + rt1[at].astype(F32)).astype(BF)
+            gt[j, at, below_cut] = (gt[j, at, below_cut].astype(F32) + rt1[at].astype(F32)).astype(BF)
             return carry
 
         lax.fori_loop(0, zn, body, 0)
@@ -1063,25 +1072,25 @@
         def send(i, carry):
             k = 2 * i + (1 if t == 0 else 2)
             peer = lax.rem(me + k, n)
-            t_dp(j, spot(peer), lower, rt3, 24, k, peer)
+            t_dp(j, spot(peer), below_cut, rt3, 24, k, peer)
             return carry
 
         lax.fori_loop(0, zn if t == 0 else zn - 1, send, 0)
 
     def th_x():
-        return remote(gt.at[j2, here, upper], rt6, rs_s.at[25], rs_r.at[25], me, j2)
+        return remote(gt.at[j2, here, above_cut], rt6, gx_s.at[25], gx_r.at[25], me, j2)
 
     def th_four():
-        own_t[upper, :] = t_landed(j, upper, rt5.at[0], 22)
-        gt[j2, here, upper] = t_landed(j2, upper, rt5.at[1], 23).astype(BF)
+        own_t[above_cut, :] = t_landed(j, above_cut, rt5.at[0], 22)
+        gt[j2, here, above_cut] = t_landed(j2, above_cut, rt5.at[1], 23).astype(BF)
         th_x().start()
 
     def tl_five():
-        own_t[lower, :] = t_landed(j, lower, rt3, 24)
+        own_t[below_cut, :] = t_landed(j, below_cut, rt3, 24)
 
     def th_five():
         both(th_x())
-        own_t[upper, :] = own_t[upper, :] + rt6[...].astype(F32)
+        own_t[above_cut, :] = own_t[above_cut, :] + rt6[...].astype(F32)
 
 
     per = 640 // (4 * rb)
@@ -1176,12 +1185,11 @@
 
         lax.fori_loop(lo, hi, tile, 0)
 
-    hg[9:10, :] = colsum(dhid[...].astype(F32))
-    bn_t = dy_t
-    bn_t[...] = bn[...].T
+    bn_t = jnp.concatenate([bn[...].T, jnp.ones((16, tokens), BF)], axis=0)
     for b in range(2):
-        value = nn(bn_t[...], dhid[:, 640 * b : 640 * b + 640]).T.astype(BF)
-        value = value.reshape(2, 4, 80, D)
+        found = nn(bn_t, dhid[:, 640 * b : 640 * b + 640])
+        hg[9:10, 640 * b : 640 * b + 640] = found[D : D + 1]
+        value = found[0:D].T.astype(BF).reshape(2, 4, 80, D)
         for i in range(n):
             sb[2 * b : 2 * b + 2, place_of(i), :, 0 : 4 * rb] = jnp.concatenate(
                 [value[:, v, :, rb * i : rb * i + rb] for v in range(4)], axis=2
@@ -1259,17 +1267,10 @@
         for copy in dk_core(h):
             copy.start()
 
-        @pl.when(h == 2)
+        @pl.when(h == 3)
         def _():
             a_four()
-
-        @pl.when(h == 3)
-        def _():
             bl_three()
-
-        @pl.when(h == 4)
-        def _():
-            bh_three()
 
         @pl.when(h >= 1)
         def _():
@@ -1291,6 +1292,7 @@
 
     lax.fori_loop(0, 2, back_query, 0)
     dk_two(HEADS - 1)
+    bh_three()
     lax.fori_loop(2, HEADS, back_query, 0)
     bl_four()
 
@@ -1317,7 +1319,7 @@
         gm[:, place_of(i), :, 0 : 3 * rb] = jnp.concatenate(folded(value, i), axis=2)
         gm[:, place_of(i), :, mo : mo + 3 * rb] = jnp.concatenate(folded(other, i), axis=2)
     m_one()
-    tap_sums(0, FF // 256)
+    tap_sums(0, 2)
     m_two()
     for h in range(HEADS):
         dk_three(h)
@@ -1379,13 +1381,13 @@
     vg[0:1, :] = sums[0]
     vg[3:4, :] = sums[1]
     m_three()
-    tap_sums(FF // 256, FF // 128)
+    tap_sums(2, FF // 128)
     for i in range(n):
         sv[place_of(i), :, 0 : 4 * rb] = hg[:, 4 * rb * i : 4 * rb * (i + 1)].astype(BF)
         sv[place_of(i), :, 4 * rb : 5 * rb] = vg[:, rb * i : rb * i + rb].astype(BF)
 
     def v_out(k, peer, source):
-        remote(sv.at[spot(peer)], rv1.at[k], rs_s.at[26], rs_r.at[26], peer, j).start()
+        remote(sv.at[spot(peer)], rv1.at[k], gx_s.at[26], gx_r.at[26], peer, j).start()
 
     peers(v_out)
     tl_three(0)
@@ -1393,14 +1395,14 @@
     bh_four()
     m_four()
     part = rv1.at[pl.ds(1, n - 1)]
-    both(remote(part, part, rs_s.at[26], rs_r.at[26], beside, j))
+    both(remote(part, part, gx_s.at[26], gx_r.at[26], beside, j))
     rv2[j] = lax.fori_loop(
         1, n, lambda k, total: total + rv1[k].astype(F32), sv[here].astype(F32)
     ).astype(BF)
 
     def v_seq(t, slot, other):
         ref = rv2.at[slot]
-        return remote(ref, ref, rs_s.at[30 + t], rs_r.at[30 + t], me, other)
+        return remote(ref, ref, gx_s.at[30 + t], gx_r.at[30 + t], me, other)
 
     for t, other in enumerate((j1, j2, j3)):
         v_seq(t, j, other).start()
@@ -1631,14 +1633,12 @@
         vm((side, 2 * side), BF),
         vm((2 * side, side), BF),
         dma((15,)),
-        *[dma((9,)) for _ in range(2)],
         dma((n,)),
         dma((2, h)),
-        *[dma((16,)) for _ in range(2)],
+        *[dma((36,)) for _ in range(2)],
         *[dma((1,)) for _ in range(4)],
         *[dma((HEADS, 3)) for _ in range(2)],
         *[dma((4,)) for _ in range(2)],
-        *[dma((34,)) for _ in range(2)],
         *[dma((1,)) for _ in range(2)],
     ]
     anywhere = pl.BlockSpec(memory_space=pl.ANY)

time: 116 us -> 113 us (0.974)
  Pallas kernels: 115 us -> 112 us
    pallas_call x1, Pallas kernels: 111 us -> 108 us  [on_device(): pl.pallas_call(functools.partial(block_kernel, n, side, band, qa), out_sh...]
where the time goes in v5:
time: 113 us
  Pallas kernels  112 us (99%)
  between operations  1.48 us (1%)
    pallas_call x1, Pallas kernels, on_device(): pl.pallas_call(functools.partial(block_kernel, n, side, band, qa), out_sh...  108 us
    pallas_call x1, Pallas kernels, on_device(): pl.pallas_call(functools.partial(update_kernel, rb, tl, al, 128 if ml > 1...  3.37 us

profile of v5, /device:TPU:0, one launch (start us, length us, event | category | flops | bytes accessed | tf_op | source)
XLA Modules:
  0.0 113.0 jit_solution(11974280572595170391)
XLA Ops:
  1.3 108.2 %shard_map.517 = (bf16[8,320,128]{2,1,0:T(8,128)(2,1)}, bf16[1024,320]{1,0:T(8,128)(2,1)}, f32[128,768]{1,0:T(8,128)}, f32[1,128]{1,0:T(1,128)}) custom-call(s32[1]{0:T(128)S(6)} %copy.62.bucket_ref, bf16[1024,320]{1,0:T(8,128)(2,1)} %bitcast.14, bf16[8,320,128]{2,1,0:T(8,128)(2,1)} %bitcast.15, f32[40,80]{1,0:T(8,128)} %refs_4_.1, f32[160,80]{1,0:T(8,128)} %refs_5_.1, ...), custom_call_target="tpu_custom_call" | custom-call | tf_op jit(solution)/shard_map/pallas_call | solution.py:1645
  109.5 3.4 %shard_map.518 = (bf16[8,320,128]{2,1,0:T(8,128)(2,1)}, bf16[1024,320]{1,0:T(8,128)(2,1)}, f32[1,128]{1,0:T(1,128)}, f32[40,80]{1,0:T(8,128)}, f32[160,80]{1,0:T...) custom-call(f32[128,768]{1,0:T(8,128)} %get-tuple-element.64.refs_0_, ...), custom_call_target="tpu_custom_call" | custom-call | tf_op jit(solution)/shard_map/pallas_call | solution.py:1678

commit v6 on v5

--- a/solution.py
+++ b/solution.py
@@ -217,6 +217,7 @@
     tokens = band * side
     chunks = tokens // QC
     deep = band if qa == tokens else 4
+    pairs = 2 if qa == tokens else 1
     rb = wq_ref.shape[0]
     piece = tokens // n
     keys = kv.shape[2]
@@ -492,7 +493,7 @@
             a3[t, at, :] = wide[:, 128 * t : 128 * t + 128]
         return carry
 
-    lax.fori_loop(0, chunks, norm_one, 0)
+    lax.fori_loop(0, chunks, norm_one, 0, unroll=pairs)
     half = side // 2
     for dd in range(4):
         for i in range(band // 2):
@@ -639,7 +640,7 @@
             qt[h, :, across(c)] = tile.T
         return carry
 
-    lax.fori_loop(0, chunks, queries, 0)
+    lax.fori_loop(0, chunks, queries, 0, unroll=pairs)
     lax.fori_loop(2, HEADS, kv_send, 0)
 
     def send_cot(k, peer, source):
@@ -678,6 +679,10 @@
                 def _():
                     kv_forward(h + 1)
 
+                @pl.when(h == 3)
+                def _():
+                    peers(send_cot)
+
                 @pl.when(h == HEADS - 2)
                 def _():
                     fl_ya_wait()
@@ -691,7 +696,6 @@
                     fh_b_wait()
                     fh_ca()
                     fh_cb()
-                    peers(send_cot)
 
             largest = jnp.max(scores, axis=0, keepdims=True)
             powers = jnp.exp(scores - largest).astype(BF)
@@ -742,7 +746,7 @@
         bn[at, :] = low
         return carry
 
-    lax.fori_loop(0, chunks, middle, 0)
+    lax.fori_loop(0, chunks, middle, 0, unroll=pairs)
 
     edge = tokens - side
 
@@ -796,7 +800,7 @@
         hidp[rows(start + side, inner), :] = hidden_of(bn[rows(start, inner), :])
         return carry
 
-    lax.fori_loop(0, 2, inner_hidden, 0)
+    lax.fori_loop(0, 2, inner_hidden, 0, unroll=pairs)
 
     def tile_at(t):
         return pl.ds(pl.multiple_of(t * 128, 128), 128)
@@ -843,7 +847,7 @@
             out_t[c * (QC // piece) + p] = (part.T if turned else part).astype(BF)
         return carry
 
-    lax.fori_loop(0, chunks, out_chunk, 0)
+    lax.fori_loop(0, chunks, out_chunk, 0, unroll=pairs)
 
     def send_out(k, peer, source):
         remote(out_t.at[peer], out_ref.at[me], ou_s.at[0], ou_r.at[0], peer, j).start()
@@ -988,7 +992,7 @@
         (0, 1, 2, 3, 0, 0, 0, 0, 0, 4), gf.at[:, :, :, 0:al], 80, False, (ra0, ra1, ra2, ra3, ra4, ra5, ra6), own_a
     )
     b_one, b_two, bl_three, bl_four, bl_five, bh_three, bh_four, bh_five = scatter(
-        (5, 6, 27, 28, 7, 8, 9, 10, 11, 29), sb, 32, False, (rb0, rb1, rb2, rb3, rb4, rb5, rb6), own_b
+        (5, 6, 27, 28, 7, 8, 9, 36, 37, 29), sb, 32, False, (rb0, rb1, rb2, rb3, rb4, rb5, rb6), own_b
     )
     m_one, m_two, m_three, m_four, m_five, _, _, _ = scatter(
         (12, 13, 14, 15, 0, 0, 0, 0, 0, 33), gm, 32, False, (rm0, rm1, rm2, rm3, rm4, rm5, rm6), own_m
@@ -1052,7 +1056,7 @@
             t_add(slot, 0, n, above_cut, rt0.at[t])
             peers(
                 lambda k, peer, source: t_dp(
-                    slot, spot(peer), above_cut, rt5.at[t], 22 + t, k, peer
+                    slot, spot(peer), above_cut, rt5.at[t], 38 - 15 * t, k, peer
                 )
             )
         both(cores[3])
@@ -1081,7 +1085,7 @@
         return remote(gt.at[j2, here, above_cut], rt6, gx_s.at[25], gx_r.at[25], me, j2)
 
     def th_four():
-        own_t[above_cut, :] = t_landed(j, above_cut, rt5.at[0], 22)
+        own_t[above_cut, :] = t_landed(j, above_cut, rt5.at[0], 38)
         gt[j2, here, above_cut] = t_landed(j2, above_cut, rt5.at[1], 23).astype(BF)
         th_x().start()
 
@@ -1121,7 +1125,7 @@
         ).astype(BF)
         return carry
 
-    lax.fori_loop(0, 2, inner_slope, 0)
+    lax.fori_loop(0, 2, inner_slope, 0, unroll=pairs)
 
     a_two()
 
@@ -1221,7 +1225,7 @@
             )
         return (carry[0] + in_gain, carry[1] + in_shift, carry[2] + colsum(low.astype(F32)))
 
-    sums = lax.fori_loop(0, chunks, back_middle, (zero_row, zero_row, zero_row))
+    sums = lax.fori_loop(0, chunks, back_middle, (zero_row, zero_row, zero_row), unroll=pairs)
     vg[2:3, :] = sums[0]
     vg[9:10, :] = sums[1]
     vg[8:9, :] = sums[2]
@@ -1303,7 +1307,7 @@
         dq[rows(c * QC, QC), :] = low
         return total + colsum(low.astype(F32))
 
-    vg[4:5, :] = lax.fori_loop(0, chunks, flip, zero_row)
+    vg[4:5, :] = lax.fori_loop(0, chunks, flip, zero_row, unroll=pairs)
     value = nn(dq_t[...], abf[...]).astype(BF)
     other = nn(dbr_t[...], att_n[...]).astype(BF)
 
@@ -1375,7 +1379,7 @@
         bn[at, :] = (mid[at, :] + value).astype(BF)
         return (carry[0] + in_gain, carry[1] + in_shift)
 
-    sums = lax.fori_loop(0, chunks, back_first, (zero_row, zero_row))
+    sums = lax.fori_loop(0, chunks, back_first, (zero_row, zero_row), unroll=pairs)
     token_out = pltpu.make_async_copy(bn, tgrad_ref, loc.at[12])
     token_out.start()
     vg[0:1, :] = sums[0]
@@ -1635,7 +1639,7 @@
         dma((15,)),
         dma((n,)),
         dma((2, h)),
-        *[dma((36,)) for _ in range(2)],
+        *[dma((39,)) for _ in range(2)],
         *[dma((1,)) for _ in range(4)],
         *[dma((HEADS, 3)) for _ in range(2)],
         *[dma((4,)) for _ in range(2)],

time: 113 us -> 111 us (0.982)
  Pallas kernels: 112 us -> 109 us
    pallas_call x1, Pallas kernels: 108 us -> 106 us  [on_device(): pl.pallas_call(functools.partial(block_kernel, n, side, band, qa), out_sh...]
where the time goes in v6:
time: 111 us; the launch traced here: 110 us
  Pallas kernels  109 us (98%)
  between operations  1.5 us (1%)
    pallas_call x1, Pallas kernels, on_device(): pl.pallas_call(functools.partial(block_kernel, n, side, band, qa), out_sh...  106 us
    pallas_call x1, Pallas kernels, on_device(): pl.pallas_call(functools.partial(update_kernel, rb, tl, al, 128 if ml > 1...  3.37 us

profile of v6, /device:TPU:0, one launch (start us, length us, event | category | flops | bytes accessed | tf_op | source)
XLA Modules:
  0.0 110.4 jit_solution(18316184269401601098)
XLA Ops:
  1.3 105.5 %shard_map.517 = (bf16[8,320,128]{2,1,0:T(8,128)(2,1)}, bf16[1024,320]{1,0:T(8,128)(2,1)}, f32[128,768]{1,0:T(8,128)}, f32[1,128]{1,0:T(1,128)}) custom-call(s32[1]{0:T(128)S(6)} %copy.62.bucket_ref, bf16[1024,320]{1,0:T(8,128)(2,1)} %bitcast.14, bf16[8,320,128]{2,1,0:T(8,128)(2,1)} %bitcast.15, f32[40,80]{1,0:T(8,128)} %refs_4_.1, f32[160,80]{1,0:T(8,128)} %refs_5_.1, ...), custom_call_target="tpu_custom_call" | custom-call | tf_op jit(solution)/shard_map/pallas_call | solution.py:1649
  106.8 3.4 %shard_map.518 = (bf16[8,320,128]{2,1,0:T(8,128)(2,1)}, bf16[1024,320]{1,0:T(8,128)(2,1)}, f32[1,128]{1,0:T(1,128)}, f32[40,80]{1,0:T(8,128)}, f32[160,80]{1,0:T...) custom-call(f32[128,768]{1,0:T(8,128)} %get-tuple-element.64.refs_0_, ...), custom_call_target="tpu_custom_call" | custom-call | tf_op jit(solution)/shard_map/pallas_call | solution.py:1682

commit v7 on v6

--- a/solution.py
+++ b/solution.py
@@ -1294,10 +1294,10 @@
             ).astype(BF)
         return carry
 
-    lax.fori_loop(0, 2, back_query, 0)
+    lax.fori_loop(0, 2, back_query, 0, unroll=pairs)
     dk_two(HEADS - 1)
     bh_three()
-    lax.fori_loop(2, HEADS, back_query, 0)
+    lax.fori_loop(2, HEADS, back_query, 0, unroll=3 if pairs > 1 else 1)
     bl_four()
 
     dq = dy
@@ -1516,6 +1516,11 @@
         own_ref[80:91, 0 : 4 * rb],
     )
     for at in range(9):
+        if at == 2:
+            out_load.wait()
+            out_store.start()
+            tok_load.wait()
+            tok_store.start()
         pltpu.make_async_copy(in_v[at], in_v[at], in_sem.at[at]).wait()
         clipped = clip * grads[at]
         weight = in_v[at][0]
@@ -1533,10 +1538,6 @@
             pltpu.make_async_copy(
                 new_v[at].at[part], new_hbm[at + 9 * part], out_sem.at[at]
             ).start()
-    out_load.wait()
-    out_store.start()
-    tok_load.wait()
-    tok_store.start()
     for at in range(9):
         pltpu.make_async_copy(new_v[at], new_v[at], out_sem.at[at]).wait()
     for store in (norm_store, out_store, tok_store):

time: 111 us -> 110 us (level)
  no operation moved by 1% of the time
where the time goes in v7:
time: 110 us
  Pallas kernels  108 us (98%)
  between operations  1.5 us (1%)
    pallas_call x1, Pallas kernels, on_device(): pl.pallas_call(functools.partial(block_kernel, n, side, band, qa), out_sh...  105 us
    pallas_call x1, Pallas kernels, on_device(): pl.pallas_call(functools.partial(update_kernel, rb, tl, al, 128 if ml > 1...  3.29 us

profile of v7, /device:TPU:0, one launch (start us, length us, event | category | flops | bytes accessed | tf_op | source)
XLA Modules:
  0.0 109.8 jit_solution(12797955955606587998)
XLA Ops:
  1.3 105.0 %shard_map.517 = (bf16[8,320,128]{2,1,0:T(8,128)(2,1)}, bf16[1024,320]{1,0:T(8,128)(2,1)}, f32[128,768]{1,0:T(8,128)}, f32[1,128]{1,0:T(1,128)}) custom-call(s32[1]{0:T(128)S(6)} %copy.62.bucket_ref, bf16[1024,320]{1,0:T(8,128)(2,1)} %bitcast.14, bf16[8,320,128]{2,1,0:T(8,128)(2,1)} %bitcast.15, f32[40,80]{1,0:T(8,128)} %refs_4_.1, f32[160,80]{1,0:T(8,128)} %refs_5_.1, ...), custom_call_target="tpu_custom_call" | custom-call | tf_op jit(solution)/shard_map/pallas_call | solution.py:1650
  106.4 3.3 %shard_map.518 = (bf16[8,320,128]{2,1,0:T(8,128)(2,1)}, bf16[1024,320]{1,0:T(8,128)(2,1)}, f32[1,128]{1,0:T(1,128)}, f32[40,80]{1,0:T(8,128)}, f32[160,80]{1,0:T...) custom-call(f32[128,768]{1,0:T(8,128)} %get-tuple-element.64.refs_0_, ...), custom_call_target="tpu_custom_call" | custom-call | tf_op jit(solution)/shard_map/pallas_call | solution.py:1683

commit v8 on v7

--- a/solution.py
+++ b/solution.py
@@ -218,6 +218,7 @@
     chunks = tokens // QC
     deep = band if qa == tokens else 4
     pairs = 2 if qa == tokens else 1
+    flat = 4 * n - 1 if qa == tokens else 1
     rb = wq_ref.shape[0]
     piece = tokens // n
     keys = kv.shape[2]
@@ -292,7 +293,7 @@
         )
         return carry
 
-    lax.fori_loop(1, 4 * n, greet, 0)
+    lax.fori_loop(1, 4 * n, greet, 0, unroll=flat)
 
     for copy in loads[:5]:
         copy.wait()
@@ -1444,10 +1445,12 @@
         ).start()
         return carry
 
-    lax.fori_loop(1, 4 * n, send_norm, 0)
+    lax.fori_loop(1, 4 * n, send_norm, 0, unroll=flat)
     part = nrm.at[pl.ds(0, 4 * n - 1)]
     both(remote(part, part, nd_s.at[0], nd_r.at[0], beside, j))
-    nrm[4 * n] = lax.fori_loop(1, 4 * n, lambda k, total: total + nrm[k], nrm[0])
+    nrm[4 * n] = lax.fori_loop(
+        1, 4 * n, lambda k, total: total + nrm[k], nrm[0], unroll=flat
+    )
     norm_out = pltpu.make_async_copy(nrm.at[4 * n], norm_ref, loc.at[14])
     norm_out.start()
 

time: 110 us -> 110 us (level)
  no operation moved by 1% of the time
where the time goes in v8:
time: 110 us
  Pallas kernels  108 us (98%)
  between operations  1.5 us (1%)
    pallas_call x1, Pallas kernels, on_device(): pl.pallas_call(functools.partial(block_kernel, n, side, band, qa), out_sh...  105 us
    pallas_call x1, Pallas kernels, on_device(): pl.pallas_call(functools.partial(update_kernel, rb, tl, al, 128 if ml > 1...  3.29 us

profile of v8, /device:TPU:0, one launch (start us, length us, event | category | flops | bytes accessed | tf_op | source)
XLA Modules:
  0.0 109.6 jit_solution(14478467455533608179)
XLA Ops:
  1.3 104.8 %shard_map.517 = (bf16[8,320,128]{2,1,0:T(8,128)(2,1)}, bf16[1024,320]{1,0:T(8,128)(2,1)}, f32[128,768]{1,0:T(8,128)}, f32[1,128]{1,0:T(1,128)}) custom-call(s32[1]{0:T(128)S(6)} %copy.62.bucket_ref, bf16[1024,320]{1,0:T(8,128)(2,1)} %bitcast.14, bf16[8,320,128]{2,1,0:T(8,128)(2,1)} %bitcast.15, f32[40,80]{1,0:T(8,128)} %refs_4_.1, f32[160,80]{1,0:T(8,128)} %refs_5_.1, ...), custom_call_target="tpu_custom_call" | custom-call | tf_op jit(solution)/shard_map/pallas_call | solution.py:1653
  106.2 3.3 %shard_map.518 = (bf16[8,320,128]{2,1,0:T(8,128)(2,1)}, bf16[1024,320]{1,0:T(8,128)(2,1)}, f32[1,128]{1,0:T(1,128)}, f32[40,80]{1,0:T(8,128)}, f32[160,80]{1,0:T...) custom-call(f32[128,768]{1,0:T(8,128)} %get-tuple-element.64.refs_0_, ...), custom_call_target="tpu_custom_call" | custom-call | tf_op jit(solution)/shard_map/pallas_call | solution.py:1686
